TPU v7x, 128 devices: a whole 4x4x4 slice. The times are simulated.
128 devices in a mesh: ep: 16 (over x, z), sp: 8 (over y, core).
Axes of the slice: x: 4, y: 4, z: 4, core: 2. Of those that a mesh axis runs over, the one named last changes fastest.
Arguments:
- tokens: bfloat16 [16384, 3584], P(('ep', 'sp')), may hold values from -40 to 40
- cotangent: bfloat16 [16384, 3584], P(('ep', 'sp')), may hold values from -11 to 11
- norm_gain: float32 [3584], replicated, may hold values from 0.1 to 1.9
- router: float32 [3584, 16], replicated, may hold values from -0.09375 to 0.09375
- dense_gate: bfloat16 [3584, 2432], P(None, 'sp'), may hold values from -0.09375 to 0.09375
- dense_up: bfloat16 [3584, 2432], P(None, 'sp'), may hold values from -0.09375 to 0.09375
- dense_down: bfloat16 [2432, 3584], P('sp'), may hold values from -0.125 to 0.125
- expert_gate: bfloat16 [16, 3584, 2432], P('ep', None, 'sp'), may hold values from -0.09375 to 0.09375
- expert_up: bfloat16 [16, 3584, 2432], P('ep', None, 'sp'), may hold values from -0.09375 to 0.09375
- expert_down: bfloat16 [16, 2432, 3584], P('ep', 'sp'), may hold values from -0.125 to 0.125
- routes: int32 [16384, 2], P(('ep', 'sp')), may hold values from 0 to 15, all different within a row; in each aligned block of 128 rows (0 to 127, 128 to 255, ...) at most 20 rows name the same one
Outputs:
- input_grad: bfloat16 [16384, 3584], P(('ep', 'sp'))
- gain_grad: float32 [3584], replicated
- router_grad: float32 [3584, 16], replicated
Inputs may be any that keep to these rules, and one draw needn't show every extreme that they name: `routes`: each token names two different experts. Among the rows of one device no expert is named more than 20 times, and in some devices one expert is named exactly 20 times.
All inputs are finite; a program needn't handle non-finite values.
Results may differ from a plain program's by a relative error of at most 0.013.
Values may be sent and summed in bfloat16 or wider, within the bound.
No kernel may reach another device: no remote copies, remote signals or barrier semaphores. Data moves between devices by JAX's collectives and lax.ppermute only.
A program may use at most 256 MiB of HBM per device.

v0:
```python
import jax
import jax.numpy as jnp
from jax import lax
from jax.sharding import PartitionSpec as P

EPS = 1e-05


def silu_slope(gate):
    sig = jax.nn.sigmoid(gate)
    return sig * (1.0 + gate * (1.0 - sig))


def hidden_grads(rows_n, rows_dy, w_gate, w_up, w_down):
    gate = jnp.dot(rows_n, w_gate, preferred_element_type=jnp.float32)
    up = jnp.dot(rows_n, w_up, preferred_element_type=jnp.float32)
    back = lax.dot_general(
        rows_dy, w_down, (((1,), (1,)), ((), ())), preferred_element_type=jnp.float32
    )
    active = jax.nn.silu(gate)
    grad_up = (back * active).astype(jnp.bfloat16)
    grad_gate = (back * up * silu_slope(gate)).astype(jnp.bfloat16)
    into = lax.dot_general(
        grad_gate, w_gate, (((1,), (1,)), ((), ())), preferred_element_type=jnp.float32
    )
    into = into + lax.dot_general(
        grad_up, w_up, (((1,), (1,)), ((), ())), preferred_element_type=jnp.float32
    )
    return (into.astype(jnp.bfloat16), jnp.sum(active * up * back, -1).astype(jnp.bfloat16))


def lift(value):
    return lax.optimization_barrier(value).astype(jnp.float32)


def body(
    tokens,
    cotangent,
    norm_gain,
    router,
    dense_gate,
    dense_up,
    dense_down,
    expert_gate,
    expert_up,
    expert_down,
    routes,
):
    tok_dev = tokens.shape[0]
    width = tokens.shape[1]
    experts = router.shape[1]
    shards = lax.axis_size("sp")
    capacity = 5 * tok_dev // (2 * experts)
    highest = lax.Precision.HIGHEST
    values = tokens.astype(jnp.float32)
    inverse = lax.rsqrt(jnp.mean(values * values, -1, keepdims=True) + EPS)
    normed = (values * inverse * norm_gain).astype(jnp.bfloat16)
    group_rows, group_cot = (
        lax.all_gather(normed, "sp", axis=0, tiled=True),
        lax.all_gather(cotangent, "sp", axis=0, tiled=True),
    )
    rows_n = group_rows
    part, unused = hidden_grads(rows_n, group_cot, dense_gate, dense_up, dense_down)
    dense_into = lax.psum_scatter(
        lift(part).astype(jnp.bfloat16), "sp", scatter_dimension=0, tiled=True
    ).astype(jnp.float32)
    choice_ids = lax.broadcasted_iota(jnp.int32, (1, experts), 1)
    first = (routes[:, 0:1] == choice_ids).astype(jnp.float32)
    second = (routes[:, 1:2] == choice_ids).astype(jnp.float32)
    logits = jnp.dot(normed.astype(jnp.float32), router, precision=highest)
    weight_one = jax.nn.sigmoid(jnp.sum(logits * first, -1) - jnp.sum(logits * second, -1))
    weight_two = 1.0 - weight_one
    flat_ids = routes.reshape(-1)
    hits = (flat_ids[:, None] == choice_ids).astype(jnp.int32)
    places = jnp.cumsum(hits, 0) - hits
    slot = jnp.sum(hits * places, 1)
    target = flat_ids * capacity + slot
    layout = (
        lax.broadcasted_iota(jnp.int32, (experts * capacity, 2 * tok_dev), 0) == target[None, :]
    )
    layout = layout.astype(jnp.bfloat16).reshape(experts * capacity, tok_dev, 2)
    pick_one = layout[:, :, 0]
    pick_two = layout[:, :, 1]
    picker = pick_one + pick_two
    send_n = (
        jnp.dot(picker, normed, preferred_element_type=jnp.float32)
        .astype(jnp.bfloat16)
        .reshape(experts, capacity, width)
    )
    send_dy = (
        jnp.dot(picker, cotangent, preferred_element_type=jnp.float32)
        .astype(jnp.bfloat16)
        .reshape(experts, capacity, width)
    )
    own_gate = expert_gate[0]
    own_up = expert_up[0]
    own_down = expert_down[0]
    wide_n = jnp.repeat(send_n, shards, axis=0)
    wide_dy = jnp.repeat(send_dy, shards, axis=0)
    rows_n = lax.all_to_all(wide_n, ("ep", "sp"), split_axis=0, concat_axis=0, tiled=True)
    shape = rows_n.shape
    part, joint = hidden_grads(
        rows_n.reshape(-1, width),
        lax.all_to_all(wide_dy, ("ep", "sp"), split_axis=0, concat_axis=0, tiled=True).reshape(
            -1, width
        ),
        own_gate,
        own_up,
        own_down,
    )
    part, joint = (part.reshape(shape), joint.reshape(shape[:-1]))
    back_part = lax.all_to_all(part, ("ep", "sp"), split_axis=0, concat_axis=0, tiled=True)
    back_joint = lax.all_to_all(joint, ("ep", "sp"), split_axis=0, concat_axis=0, tiled=True)
    expert_into = jnp.sum(
        back_part.astype(jnp.float32).reshape(experts, shards, capacity, width), 1
    )
    expert_score = jnp.sum(back_joint.astype(jnp.float32).reshape(experts, shards, capacity), 1)
    flat_into = expert_into.reshape(experts * capacity, width)
    flat_score = expert_score.reshape(experts * capacity)
    take_one = pick_one.astype(jnp.float32).T
    take_two = pick_two.astype(jnp.float32).T
    mixer = weight_one[:, None] * take_one + weight_two[:, None] * take_two
    moe_into = jnp.dot(mixer, flat_into, precision=highest)
    score_one = jnp.dot(take_one, flat_score, precision=highest)
    score_two = jnp.dot(take_two, flat_score, precision=highest)
    delta = weight_one * weight_two * (score_one - score_two)
    grad_logits = first * delta[:, None] - second * delta[:, None]
    local_router = jnp.dot(normed.astype(jnp.float32).T, grad_logits, precision=highest)
    total = dense_into + moe_into + jnp.dot(grad_logits, router.T, precision=highest)
    local_gain = jnp.sum(total * values * inverse, 0)
    scaled = total * norm_gain
    mean_term = jnp.mean(scaled * values, -1, keepdims=True)
    input_grad = cotangent.astype(jnp.float32) + inverse * (
        scaled - values * inverse * inverse * mean_term
    )
    gain_grad, router_grad = lax.psum((local_gain, local_router), ("ep", "sp"))
    return (input_grad.astype(jnp.bfloat16), gain_grad, router_grad)


def solution(mesh):
    return jax.shard_map(
        body,
        mesh=mesh,
        in_specs=(
            P(("ep", "sp"), None),
            P(("ep", "sp"), None),
            P(),
            P(),
            P(None, "sp"),
            P(None, "sp"),
            P("sp", None),
            P("ep", None, "sp"),
            P("ep", None, "sp"),
            P("ep", "sp", None),
            P(("ep", "sp"), None),
        ),
        out_specs=(P(("ep", "sp"), None), P(), P()),
        check_vma=False,
    )
```

profile of v0, /device:TPU:1, one launch (start us, length us, event | category | flops | bytes accessed | tf_op | source)
XLA Modules:
  0.0 1322.1 jit_solution(962529835025557415)
XLA Ops:
  8.0 0.9 copy.27
  9.2 0.6 reduce-window.6
  10.4 0.7 multiply_add_fusion
  11.1 0.7 iota_compare_fusion
  11.8 1.5 fusion.18
  13.3 0.5 copy-done.16
  13.8 1.5 fusion.12
  15.3 2.1 convolution_convert_fusion
  17.4 4.1 reshape.134
  21.5 9.1 broadcast_in_dim.5
  30.6 11.9 all-to-all-start.1
  42.6 2.1 convolution_convert_fusion.1
  44.7 4.1 reshape.131
  48.8 301.2 %all-to-all-done.1 = bf16[128,20,3584]{2,1,0:T(8,128)(2,1)} async-done(((bf16[128,20,3584]{2,1,0:T(8,128)(2,1)}), bf16[128,20,3584]{2,1,0:T(8,128)(2,1)}, u32[]{:S(2)}, u32[]{:S(2)}) %all-to-all-start.1) | async-done | bytes 18350112 | tf_op jit(solution)/shard_map/all_to_all | solution.py:100
  350.0 9.1 broadcast_in_dim.4
  359.1 39.4 %all-to-all-start = ((bf16[128,20,3584]{2,1,0:T(8,128)(2,1)}), bf16[128,20,3584]{2,1,0:T(8,128)(2,1)}, u32[]{:S(2)}, u32[]{:S(2)}) async-start(bf16[128,20,3584]{2,1,0:T(8,128)(2,1)} %bitcast.101), calls=%async_computation.1 | async-start | bytes 44040192 | tf_op jit(solution)/shard_map/all_to_all | solution.py:104
  398.5 0.7 all-gather.5.cloned.1.call-update
  399.2 0.6 all-gather.3.cloned.1.call-start
  399.9 275.7 %all-gather.5.cloned.1.call-done = bf16[1024,3584]{1,0:T(8,128)(2,1)} async-done(((bf16[128,3584]{1,0:T(8,128)(2,1)}), bf16[1024,3584]{1,0:T(8,128)(2,1)}) %all-gather.5.cloned.1.call-update) | async-done | bytes 7340048 | tf_op jit(solution)/shard_map/all_gather | solution.py:59
  675.7 6.1 fusion.66
  681.8 25.4 %reshape.136 = bf16[2560,3584]{1,0:T(8,128)(2,1)} reshape(bf16[128,20,3584]{2,1,0:T(8,128)(2,1)} %all-to-all-done.1) | data formatting | bytes 36700160 | tf_op jit(solution)/shard_map/reshape | solution.py:103
  707.2 9.0 all-to-all-done
  716.1 25.2 %reshape.133 = bf16[2560,3584]{1,0:T(8,128)(2,1)} reshape(bf16[128,20,3584]{2,1,0:T(8,128)(2,1)} %all-to-all-done) | data formatting | bytes 36700160 | tf_op jit(solution)/shard_map/reshape | solution.py:104
  741.4 11.7 fusion.5
  753.1 8.6 fusion.8
  761.7 12.8 multiply_reduce_fusion
  774.6 0.7 convert_element_type.121
  775.3 16.8 %all-to-all-start.3 = ((bf16[128,1,20]{2,1,0:T(2,128)(2,1)}), bf16[128,1,20]{2,1,0:T(2,128)(2,1)S(1)}, u32[]{:S(2)}, u32[]{:S(2)}) async-start(bf16[128,1,20]{2,1,0:T(2,128)(2,1)} %convert_element_type.121), calls=%async_computation.4 | async-start | bytes 131072 | tf_op jit(solution)/shard_map/all_to_all | solution.py:113
  792.1 21.6 %fusion.3 = f32[2560,3584]{1,0:T(8,128)} fusion(bf16[1,3584,304]{1,2,0:T(8,128)(2,1)S(1)} %copy-done, f32[2560,304]{0,1:T(8,128)} %copy-done.5, f32[2560,304]{0,1:T(8,128)} %get-tuple-element.14, f32[2560,304]{0,1:T(8,128)} %copy-done.9), kind=kOutput, calls=%fused_computation.18 | convolution fusion | flops 5586206720 | bytes 48218112 | tf_op jit(solution)/shard_map/dot_general | solution.py:23
  813.7 25.1 %add_convert_fusion = bf16[2560,3584]{1,0:T(8,128)(2,1)} fusion(f32[2560,3584]{1,0:T(8,128)} %fusion.3, bf16[1,3584,304]{1,2,0:T(8,128)(2,1)} %param.19, f32[2560,304]{0,1:T(8,128)} %get-tuple-element.14, f32[2560,304]{0,1:T(8,128)} %copy-done.5), kind=kOutput, calls=%fused_computation.1 | convolution fusion | flops 5601443840 | bytes 63455232 | tf_op jit(solution)/shard_map/dot_general | solution.py:26
  838.7 25.0 %reshape.137 = bf16[128,20,3584]{2,1,0:T(8,128)(2,1)} reshape(bf16[2560,3584]{1,0:T(8,128)(2,1)} %add_convert_fusion) | data formatting | bytes 36700160 | tf_op jit(solution)/shard_map/reshape | solution.py:111
  863.7 10.1 all-to-all-start.2
  874.2 6.1 fusion.65
  880.3 13.2 fusion.25
  893.5 9.8 add_convert_fusion.1
  903.4 0.3 all-reduce.2.cloned.1.call-start
  903.7 0.3 copy-done.15
  904.0 0.5 copy-done.3
  904.6 0.8 select_reduce_fusion
  906.0 1.2 fusion.49
  907.1 277.7 %all-to-all-done.2 = bf16[128,20,3584]{2,1,0:T(8,128)(2,1)} async-done(((bf16[128,20,3584]{2,1,0:T(8,128)(2,1)}), bf16[128,20,3584]{2,1,0:T(8,128)(2,1)}, u32[]{:S(2)}, u32[]{:S(2)}) %all-to-all-start.2) | async-done | bytes 18350112 | tf_op jit(solution)/shard_map/all_to_all | solution.py:112
  1184.9 15.3 %convert_reduce_fusion = f32[16,20,3584]{2,1,0:T(8,128)} fusion(bf16[128,20,3584]{2,1,0:T(8,128)(2,1)} %all-to-all-done.2), kind=kLoop, calls=%fused_computation | loop fusion | flops 17203200 | bytes 22937600 | tf_op jit(solution)/shard_map/reduce_sum | solution.py:114
  1200.2 5.2 reshape.140
  1205.4 6.0 convolution_add_fusion.1
  1211.5 2.2 fusion.21
  1213.7 1.6 fusion.17
  1215.3 97.8 %psum.14 = f32[3584]{0:T(1024)} all-reduce(f32[3584]{0:T(1024)S(1)} %get-tuple-element.3), channel_id=1, replica_groups=mesh['ep'=16,'sp'=8] {'ep','sp'}, use_global_device_ids=true, to_apply=%region_12.13 | all-reduce | flops 3584 | bytes 28672 | tf_op jit(solution)/shard_map/psum | solution.py:136
  1313.1 1.6 copy.36
  (60 shorter events, 2.0 us)
Async XLA Ops:
  8.0 733.4 %copy-start = (bf16[1,3584,304]{1,2,0:T(8,128)(2,1)S(1)}, bf16[1,3584,304]{1,2,0:T(8,128)(2,1)}, u32[]{:S(2)}) copy-start(bf16[1,3584,304]{1,2,0:T(8,128)(2,1)} %param.18) | copy-start | bytes 6537220
  11.8 30.8 %copy-start.10 = (bf16[320,128,2]{1,0,2:T(8,128)(2,1)}, bf16[320,128,2]{1,0,2:T(8,128)(2,1)S(1)}, u32[]{:S(2)}) copy-start(bf16[320,128,2]{1,0,2:T(8,128)(2,1)S(1)} %get-tuple-element.10) | copy-start | bytes 491524
  13.3 0.5 copy-start.16
  15.3 2.2 copy-start.2
  30.6 11.9 copy-start.7
  30.6 319.3 %all-to-all-start.1 = ((bf16[128,20,3584]{2,1,0:T(8,128)(2,1)}), bf16[128,20,3584]{2,1,0:T(8,128)(2,1)}, u32[]{:S(2)}, u32[]{:S(2)}) async-start(bf16[128,20,3584]{2,1,0:T(8,128)(2,1)} %bitcast.102), calls=%async_computation.2 | async-start | bytes 44040192 | tf_op jit(solution)/shard_map/all_to_all | solution.py:100
  359.1 357.1 %all-to-all-start = ((bf16[128,20,3584]{2,1,0:T(8,128)(2,1)}), bf16[128,20,3584]{2,1,0:T(8,128)(2,1)}, u32[]{:S(2)}, u32[]{:S(2)}) async-start(bf16[128,20,3584]{2,1,0:T(8,128)(2,1)} %bitcast.101), calls=%async_computation.1 | async-start | bytes 44040192 | tf_op jit(solution)/shard_map/all_to_all | solution.py:104
  398.4 277.2 %all-gather.5.cloned.1.call-start = ((), (), s32[]{:S(2)}) async-start(), calls=%async_computation.6 | async-start | bytes 8257536 | tf_op jit(solution)/shard_map/all_gather | solution.py:59
  399.2 475.0 %all-gather.3.cloned.1.call-start = ((), (), s32[]{:S(2)}) async-start(), calls=%async_computation.5 | async-start | bytes 8257536 | tf_op jit(solution)/shard_map/all_gather | solution.py:60
  741.4 11.7 copy-start.4
  753.1 8.6 copy-start.5
  761.7 12.8 copy-start.9
  775.3 88.4 %all-to-all-start.3 = ((bf16[128,1,20]{2,1,0:T(2,128)(2,1)}), bf16[128,1,20]{2,1,0:T(2,128)(2,1)S(1)}, u32[]{:S(2)}, u32[]{:S(2)}) async-start(bf16[128,1,20]{2,1,0:T(2,128)(2,1)} %convert_element_type.121), calls=%async_computation.4 | async-start | bytes 131072 | tf_op jit(solution)/shard_map/all_to_all | solution.py:113
  863.7 321.2 %all-to-all-start.2 = ((bf16[128,20,3584]{2,1,0:T(8,128)(2,1)}), bf16[128,20,3584]{2,1,0:T(8,128)(2,1)}, u32[]{:S(2)}, u32[]{:S(2)}) async-start(bf16[128,20,3584]{2,1,0:T(8,128)(2,1)} %reshape.137), calls=%async_computation.3 | async-start | bytes 44040192 | tf_op jit(solution)/shard_map/all_to_all | solution.py:112
  873.9 331.5 %reduce-scatter.2.cloned.1.call-start = ((), (), s32[]{:S(2)}) async-start(), calls=%async_computation.7 | async-start | bytes 8257536 | tf_op jit(solution)/shard_map/reduce_scatter | solution.py:64
  903.3 0.7 copy-start.15
  903.3 1.2 copy-start.3
  903.3 1.2 copy-start.12
  903.3 2.3 copy-start.14
  903.4 409.7 %all-reduce.2.cloned.1.call-start = ((), (), s32[]{:S(2)}) async-start(), calls=%async_computation.8 | async-start | bytes 458752 | tf_op jit(solution)/shard_map/psum | solution.py:136
  1200.2 5.2 copy-start.11
  1205.4 6.1 copy-start.6
  1205.4 6.1 copy-start.13
  1205.4 6.1 copy-start.17
  1211.5 2.2 copy-start.8
  1213.7 101.0 %copy-start.1 = (bf16[1,3584,304]{1,2,0:T(8,128)(2,1)S(1)}, bf16[1,3584,304]{1,2,0:T(8,128)(2,1)}, u32[]{:S(2)}) copy-start(bf16[1,3584,304]{1,2,0:T(8,128)(2,1)} %param.18) | copy-start | bytes 6537220
Sparse Core Ops, SparseCore 0:
  401.5 274.0 all-gather.4
  677.4 64.1 all-gather.2
  903.5 274.9 reduce-scatter.1
Sparse Core Ops, SparseCore 1:
  909.2 395.0 all-reduce.1
where the time goes:
time: 1330 us; the launch traced here: 1320 us
  waiting for transfers between devices  865 us (65%)
  matrix products  130 us (10%)
  local copies, waits for them, and re-layouts  113 us (8%)
  blocking collectives  97.8 us (7%)
  starting transfers between devices  79.4 us (6%)
  other arithmetic  22.1 us (2%)
  between operations  15.8 us (1%)
    all_to_all x1, waiting for transfers between devices, body(): lax.all_to_all(wide_n, ('ep', 'sp'), split_axis=0, concat_axis=0, tiled=T...  301 us
    all_to_all x1, waiting for transfers between devices, body(): lax.all_to_all(part, ('ep', 'sp'), split_axis=0, concat_axis=0, tiled=True)  278 us
    all_gather x1, waiting for transfers between devices, body(): lax.all_gather(normed, 'sp', axis=0, tiled=True)  276 us
    psum x1, blocking collectives, body(): gain_grad, router_grad = lax.psum((local_gain, local_router), ('ep', 'sp'))  97.8 us
    all_to_all x1, starting transfers between devices, body(): lax.all_to_all(wide_dy, ('ep', 'sp'), split_axis=0, concat_axis=0, tiled=...  39.4 us
    dot_general x2, matrix products, hidden_grads(): lax.dot_general(grad_up, w_up, (((1,), (1,)), ((), ())), preferred_elemen...  34.9 us
    dot_general x2, matrix products, hidden_grads(): lax.dot_general(grad_gate, w_gate, (((1,), (1,)), ((), ())), preferred_el...  34.7 us
  transfers between devices with their start and end apart: 8, of which 4 were waited for; matrix products, arithmetic and copies ran while one was open for 17% of the time, Pallas kernels for 0%

commit v1 on v0

v1 whole, which is shorter than its diff:
```python
import jax
import jax.numpy as jnp
from jax import lax
from jax.sharding import Mesh, PartitionSpec as P

EPS = 1e-05
BF = jnp.bfloat16
F32 = jnp.float32
HIGHEST = lax.Precision.HIGHEST
PEERS = 4
NEAR = 16


def receive_from(value, k):
    return lax.ppermute(value, "y", [(i, (i - k) % PEERS) for i in range(PEERS)])


def send_to(value, k):
    return lax.ppermute(value, "y", [(i, (i + k) % PEERS) for i in range(PEERS)])


def swap(value):
    return lax.ppermute(value, "core", [(0, 1), (1, 0)])


def over_ep(value):
    return lax.all_to_all(value, "ep", split_axis=0, concat_axis=0, tiled=True)


def join_weights(gate, up, down):
    hidden = 2 * gate.shape[1]
    pad = -hidden % 128
    blank = jnp.zeros((gate.shape[0], pad), BF)
    wide = jnp.concatenate([gate, swap(gate), blank, up, swap(up), blank], 1)
    tall = jnp.concatenate([down, swap(down), jnp.zeros((pad, down.shape[1]), BF)], 0)
    return wide, tall


def hidden_grads(rows, wide, tall):
    width = tall.shape[1]
    half = tall.shape[0]
    both = jnp.dot(rows[:, :width], wide, preferred_element_type=F32)
    back = lax.dot_general(
        rows[:, width:], tall, (((1,), (1,)), ((), ())), preferred_element_type=F32
    )
    gate, up = both[:, :half], both[:, half:]
    sig = jax.nn.sigmoid(gate)
    active = gate * sig
    grad_up = back * active
    grad_gate = back * up * (sig * (1.0 + gate * (1.0 - sig)))
    joint = jnp.sum(grad_up * up, -1)
    grads = jnp.concatenate([grad_gate.astype(BF), grad_up.astype(BF)], 1)
    into = lax.dot_general(grads, wide, (((1,), (1,)), ((), ())), preferred_element_type=F32)
    return into, joint


def one_hot_rows(index, count):
    return index[..., None] == lax.broadcasted_iota(jnp.int32, (1, 1, count), 2)


def body(
    tokens,
    cotangent,
    norm_gain,
    router,
    dense_gate,
    dense_up,
    dense_down,
    expert_gate,
    expert_up,
    expert_down,
    routes,
):
    tok, width = tokens.shape
    experts = router.shape[1]
    cap = 5 * tok // (2 * experts)
    own_rows = -(-cap // 8) * 8
    far = cap - NEAR
    far_rows = -(-(cap + 2 * far) // 8) * 8

    values = tokens.astype(F32)
    inverse = lax.rsqrt(jnp.mean(values * values, -1, keepdims=True) + EPS)
    normed = (values * inverse * norm_gain).astype(BF)
    pair = jnp.concatenate([normed, cotangent], 1)

    all_routes = jnp.stack([routes] + [receive_from(routes, k) for k in (1, 2, 3)])
    choice_ids = lax.broadcasted_iota(jnp.int32, (1, 1, 1, experts), 3)
    chosen = all_routes[..., None] == choice_ids
    hits = chosen.reshape(PEERS, 2 * tok, experts).astype(BF)
    place = lax.broadcasted_iota(jnp.int32, (2 * tok, 2 * tok), 0)
    before = (lax.broadcasted_iota(jnp.int32, (2 * tok, 2 * tok), 1) < place).astype(BF)
    places = jnp.einsum("ab,kbe->kae", before, hits, preferred_element_type=F32)
    slots = jnp.sum(hits.astype(F32) * places, -1).astype(jnp.int32).reshape(PEERS, tok, 2)

    own_hot = one_hot_rows(all_routes[0] * own_rows + slots[0], experts * own_rows)
    own_pick = jnp.sum(own_hot.astype(BF), 1)
    own_send = lax.dot_general(
        own_pick, pair, (((0,), (0,)), ((), ())), preferred_element_type=F32
    ).astype(BF)
    own = over_ep(own_send)

    peers = [receive_from(pair, k) for k in (1, 2, 3)]
    rows_of_all = jnp.concatenate([pair] + peers, 0)

    base1 = jnp.where(slots[1] >= NEAR, slots[1] - NEAR, -4 * experts * far_rows)
    base2 = slots[2] + far
    base3 = jnp.where(slots[3] >= NEAR, slots[3] - NEAR + far + cap, -4 * experts * far_rows)
    far_index = jnp.concatenate(
        [all_routes[k] * far_rows + b for k, b in ((1, base1), (2, base2), (3, base3))], 0
    )
    far_hot = one_hot_rows(far_index, experts * far_rows)
    far_pick = jnp.sum(far_hot.astype(BF), 1)
    far_send = lax.dot_general(
        far_pick, rows_of_all[tok:], (((0,), (0,)), ((), ())), preferred_element_type=F32
    ).astype(BF)
    far_got = over_ep(far_send)

    near_send = own.reshape(experts, own_rows, 2 * width)[:, :NEAR].reshape(-1, 2 * width)
    near1 = receive_from(near_send, 1)
    near3 = receive_from(near_send, 3)

    wide_d, tall_d = join_weights(dense_gate, dense_up, dense_down)
    wide_e, tall_e = join_weights(expert_gate[0], expert_up[0], expert_down[0])

    dense_part, unused = hidden_grads(rows_of_all, wide_d, tall_d)
    own_into, own_joint = hidden_grads(own, wide_e, tall_e)
    near1_into, near1_joint = hidden_grads(near1, wide_e, tall_e)
    near3_into, near3_joint = hidden_grads(near3, wide_e, tall_e)
    far_into, far_joint = hidden_grads(far_got, wide_e, tall_e)

    own_joint = own_joint.reshape(experts, own_rows)
    near1_joint = near1_joint.reshape(experts, NEAR)
    near3_joint = near3_joint.reshape(experts, NEAR)
    far_joint = far_joint.reshape(experts, far_rows)
    joints = jnp.concatenate(
        [
            own_joint[:, :cap],
            near1_joint,
            far_joint[:, :far],
            far_joint[:, far : far + cap],
            near3_joint,
            far_joint[:, far + cap : far + cap + far],
        ],
        1,
    )
    joints = over_ep(joints).reshape(experts, PEERS, cap)
    score = joints[:, 0]
    for k in (1, 2, 3):
        score = score + send_to(joints[:, k], k)

    far_back = over_ep(far_into.astype(BF))
    near_back = send_to(near1_into.astype(BF), 1).astype(F32)
    near_back = near_back + send_to(near3_into.astype(BF), 3).astype(F32)
    near_back = near_back.reshape(experts, NEAR, width)
    own_into = own_into.reshape(experts, own_rows, width)
    own_into = jnp.concatenate([own_into[:, :NEAR] + near_back, own_into[:, NEAR:]], 1)
    own_back = over_ep(own_into.astype(BF).reshape(-1, width))

    logits = jnp.dot(rows_of_all[:, :width].astype(F32), router, precision=HIGHEST)
    logits = logits.reshape(PEERS, tok, 1, experts)
    picked = jnp.sum(jnp.where(chosen, logits, 0.0), -1)
    weight_one = jax.nn.sigmoid(picked[..., 0] - picked[..., 1])
    weights = jnp.stack([weight_one, 1.0 - weight_one], -1)

    far_mix = jnp.sum(jnp.where(far_hot, weights[1:].reshape(-1, 2)[..., None], 0.0), 1)
    part = dense_part[tok:] + jnp.dot(far_mix.astype(BF), far_back, preferred_element_type=F32)
    part = part.astype(BF).reshape(PEERS - 1, tok, width)
    home = [send_to(part[k - 1], k) for k in (1, 2, 3)]

    own_mix = jnp.sum(jnp.where(own_hot, weights[0][..., None], 0.0), 1)
    total = dense_part[:tok] + jnp.dot(own_mix.astype(BF), own_back, preferred_element_type=F32)
    for piece in home:
        total = total + piece.astype(F32)

    score = jnp.pad(score, ((0, 0), (0, own_rows - cap))).reshape(1, 1, -1)
    scores = jnp.sum(jnp.where(own_hot, score, 0.0), -1)
    delta = weights[0, :, 0] * weights[0, :, 1] * (scores[:, 0] - scores[:, 1])
    signed = chosen[0, :, 0].astype(F32) - chosen[0, :, 1].astype(F32)
    grad_logits = signed * delta[:, None]
    local_router = lax.dot_general(
        grad_logits, normed.astype(F32), (((0,), (0,)), ((), ())), precision=HIGHEST
    )
    axes = ("ep", "y", "core")
    devices = lax.axis_size(axes)
    spread = lax.all_to_all(local_router.reshape(devices, -1), axes, 0, 0, tiled=True)
    mine = jnp.sum(spread, 0, keepdims=True)
    router_grad = lax.all_to_all(
        jnp.broadcast_to(mine, (devices, mine.shape[1])), axes, 0, 0, tiled=True
    )
    router_grad = router_grad.reshape(experts, width).T

    total = total + jnp.dot(grad_logits, router.T, precision=HIGHEST)
    local_gain = jnp.sum(total * values * inverse, 0)
    gains = lax.all_to_all(
        jnp.broadcast_to(local_gain[None], (devices, width)), axes, 0, 0, tiled=True
    )
    gain_grad = jnp.sum(gains, 0)
    scaled = total * norm_gain
    mean_term = jnp.mean(scaled * values, -1, keepdims=True)
    input_grad = cotangent.astype(F32) + inverse * (
        scaled - values * inverse * inverse * mean_term
    )
    return (input_grad.astype(BF), gain_grad, router_grad)


def solution(mesh):
    ep, sp = mesh.devices.shape
    grid = Mesh(mesh.devices.reshape(ep, sp // 2, 2), ("ep", "y", "core"))
    shared = ("y", "core")
    rows = ("ep", "y", "core")
    return jax.shard_map(
        body,
        mesh=grid,
        in_specs=(
            P(rows, None),
            P(rows, None),
            P(),
            P(),
            P(None, shared),
            P(None, shared),
            P(shared, None),
            P("ep", None, shared),
            P("ep", None, shared),
            P("ep", shared, None),
            P(rows, None),
        ),
        out_specs=(P(rows, None), P(), P()),
        check_vma=False,
    )
```

time: 1330 us -> 578 us (0.43)
  waiting for transfers between devices: 865 us -> 223 us
  blocking collectives: 97.8 us -> 0 us
  local copies, waits for them, and re-layouts: 113 us -> 40.4 us
  starting transfers between devices: 79.4 us -> 138 us
  between operations: 15.8 us -> 1.57 us
    all_to_all x4 -> x8, waiting for transfers between devices: 588 us -> 159 us  [the longest x5 136 us: over_ep(): return lax.all_to_all(value, 'ep', split_axis=0, concat_axis=0, tiled=True)]
    all_gather x2 -> x0, waiting for transfers between devices: 276 us -> none  [the longest x1 276 us: body(): lax.all_gather(normed, 'sp', axis=0, tiled=True)]
    psum x1 -> x0, blocking collectives: 97.8 us -> none  [body(): gain_grad, router_grad = lax.psum((local_gain, local_router), ('ep', 'sp'))]
    reshape x7 -> x6, local copies, waits for them, and re-layouts: 89.2 us -> 1.23 us  [the longest x1 0.83 us: body(): router_grad = router_grad.reshape(experts, width).T]
    ppermute x0 -> x22, waiting for transfers between devices: none -> 64.4 us  [the longest x8 43.3 us: send_to(): lax.ppermute(value, 'y', [(i, (i + k) % PEERS) for i in range(PEERS)])]
    ppermute x0 -> x22, starting transfers between devices: none -> 63.5 us  [the longest x6 44.3 us: swap(): return lax.ppermute(value, 'core', [(0, 1), (1, 0)])]
    unnamed x38 -> x61, local copies, waits for them, and re-layouts: 4.05 us -> 24 us
    broadcast_in_dim x2 -> x4, local copies, waits for them, and re-layouts: 18.2 us -> 3.11 us  [the longest x1 2.19 us: body(): jnp.broadcast_to(local_gain[None], (devices, width))]
  transfers between devices with their start and end apart: 8 -> 30, of which waited for: 4 -> 9; matrix products, arithmetic and copies ran while one was open for 17% -> 32% of each run, Pallas kernels for 0% -> 0%
where the time goes in v1:
time: 578 us; the launch traced here: 571 us
  waiting for transfers between devices  223 us (39%)
  matrix products  141 us (24%)
  starting transfers between devices  138 us (24%)
  local copies, waits for them, and re-layouts  40.4 us (7%)
  other arithmetic  26.8 us (5%)
    all_to_all x5, waiting for transfers between devices, over_ep(): return lax.all_to_all(value, 'ep', split_axis=0, concat_axis=0, tiled=True)  136 us
    ppermute x6, starting transfers between devices, swap(): return lax.ppermute(value, 'core', [(0, 1), (1, 0)])  44.3 us
    ppermute x8, waiting for transfers between devices, send_to(): lax.ppermute(value, 'y', [(i, (i + k) % PEERS) for i in range(PEERS)])  43.3 us
    all_to_all x5, starting transfers between devices, over_ep(): return lax.all_to_all(value, 'ep', split_axis=0, concat_axis=0, tiled=True)  42.1 us
    dot_general x5, matrix products, hidden_grads(): lax.dot_general(grads, wide, (((1,), (1,)), ((), ())), preferred_element_...  39.7 us
    dot_general x5, matrix products, hidden_grads(): both = jnp.dot(rows[:, :width], wide, preferred_element_type=F32)  39.5 us
    dot_general x5, matrix products, hidden_grads(): lax.dot_general(rows[:, width:], tall, (((1,), (1,)), ((), ())), preferre...  29.8 us
    unnamed x61, local copies, waits for them, and re-layouts  24 us
  transfers between devices with their start and end apart: 30, of which 9 were waited for; matrix products, arithmetic and copies ran while one was open for 32% of the time, Pallas kernels for 0%

profile of v1, /device:TPU:1, one launch (start us, length us, event | category | flops | bytes accessed | tf_op | source)
XLA Modules:
  0.0 571.3 jit_solution(13167005479798240191)
XLA Ops:
  1.5 3.6 collective-permute-start.6
  9.7 2.7 pad_maximum_fusion.2
  22.4 4.1 convolution_convert_fusion.1
  26.4 7.6 %all-to-all-start = ((bf16[16,24,7168]{2,1,0:T(8,128)(2,1)}), bf16[16,24,7168]{2,1,0:T(8,128)(2,1)}, u32[]{:S(2)}, u32[]{:S(2)}) async-start(bf16[16,24,7168]{2,1,0:T(8,128)(2,1)} %bitcast.82), calls=%async_computation | async-start | bytes 11010048 | tf_op jit(solution)/shard_map/all_to_all | solution.py:27
  35.1 17.9 %collective-permute-done = bf16[128,7168]{1,0:T(8,128)(2,1)} collective-permute-done((bf16[128,7168]{1,0:T(8,128)(2,1)}, bf16[128,7168]{1,0:T(8,128)(2,1)}, u32[]{:S(2)}, u32[]{:S(2)}) %collective-permute-start) | collective-permute-done | bytes 1835040 | tf_op jit(solution)/shard_map/ppermute | solution.py:15
  53.0 41.3 %collective-permute-start.11 = (bf16[3584,304]{0,1:T(8,128)(2,1)}, bf16[3584,304]{0,1:T(8,128)(2,1)S(1)}, u32[]{:S(2)}, u32[]{:S(2)}) collective-permute-start(bf16[3584,304]{0,1:T(8,128)(2,1)} %bitcast.91), channel_id=1, source_target_pairs={{0,1},{1,0},{2,3},{3,2},{4,5},{5,4},{6,7},{7,6},{8,9},{9,8},{10,11... | collective-permute-start | bytes 6537224 | tf_op jit(solution)/shard_map/ppermute | solution.py:23
  94.3 3.2 collective-permute-done.2
  98.1 8.1 %pad_maximum_fusion = bf16[512,7168]{1,0:T(8,128)(2,1)S(1)} fusion(bf16[128,7168]{1,0:T(8,128)(2,1)} %collective-permute-done.2, bf16[128,7168]{1,0:T(8,128)(2,1)} %collective-permute-done.1, bf16[128,7168]{1,0:T(8,128)(2,1)} %collective-permute-done, bf16[128,3584]{1,0:T(8,128)(2,1)S(1)} %copy-done.2, bf16[128,3584]{1,0:T(8,128)(2,1)S(1)} %fusion.28), kind=kLoop, calls=%fused_computation.2 | loop fusion | flops 36700160 | bytes 14680064 | tf_op jit(solution)/shard_map/concatenate | solution.py:103
  106.2 2.9 copy-done.1
  109.1 2.9 fusion.62
  112.1 9.6 %convolution_convert_fusion = bf16[512,7168]{1,0:T(8,128)(2,1)} fusion(bf16[384,512]{1,0:T(8,128)(2,1)S(1)} %fusion.69, bf16[128,7168]{1,0:T(8,128)(2,1)} %collective-permute-done.2, bf16[128,7168]{1,0:T(8,128)(2,1)} %collective-permute-done.1, bf16[128,7168]{1,0:T(8,128)(2,1)} %collective-permute-done), kind=kOutput, calls=%fused_computation | convolution fusion | flops 2838757376 | bytes 13238272 | tf_op jit(solution)/shard_map/dot_general | solution.py:113
  122.2 3.4 constant_dynamic-update-slice_fusion.6
  129.2 7.9 %all-to-all-start.2 = ((bf16[16,32,7168]{2,1,0:T(8,128)(2,1)}), bf16[16,32,7168]{2,1,0:T(8,128)(2,1)}, u32[]{:S(2)}, u32[]{:S(2)}) async-start(bf16[16,32,7168]{2,1,0:T(8,128)(2,1)} %bitcast.86), calls=%async_computation.2 | async-start | bytes 14680064 | tf_op jit(solution)/shard_map/all_to_all | solution.py:27
  137.8 3.2 constant_dynamic-update-slice_fusion.2
  143.4 3.4 constant_dynamic-update-slice_fusion
  147.4 7.5 %fusion.19 = f32[512,1280]{1,0:T(8,128)S(1)} fusion(bf16[3584,1280]{0,1:T(8,128)(2,1)} %broadcast_dynamic-update-slice_fusion.3, bf16[512,7168]{1,0:T(8,128)(2,1)S(1)} %bitcast.84), kind=kOutput, calls=%fused_computation.29 | convolution fusion | flops 4697620480 | bytes 15466496 | tf_op jit(solution)/shard_map/dot_general | solution.py:42
  155.0 6.8 %fusion.52 = (bf16[512,640]{1,0:T(8,128)(2,1)}, bf16[512,640]{1,0:T(8,128)(2,1)}) fusion(f32[512,1280]{1,0:T(8,128)S(1)} %fusion.19, bf16[304,3584]{1,0:T(8,128)(2,1)} %collective-permute-done.3, bf16[304,3584]{1,0:T(8,128)(2,1)} %param.17, bf16[640]{0:T(1024)(128)(2,1)S(1)} %pad.38.clone, bf16[512,7168]{1,0:T(8,128)(2,1)S(1)} %bitcast.84), kind=kOutput, calls=%fused_computation.73 | convolution fusion | flops 2366832640 | bytes 11962368 | tf_op jit(solution)/shard_map/dot_general | solution.py:43
  161.8 4.2 slice.228
  167.8 8.3 %fusion.21 = f32[384,1280]{1,0:T(8,128)S(1)} fusion(bf16[3584,1280]{0,1:T(8,128)(2,1)} %broadcast_dynamic-update-slice_fusion.2, bf16[384,7168]{1,0:T(8,128)(2,1)} %bitcast.8), kind=kOutput, calls=%fused_computation.35 | convolution fusion | flops 3523215360 | bytes 13893632 | tf_op jit(solution)/shard_map/dot_general | solution.py:42
  176.2 6.1 %multiply_convert_fusion.2 = (bf16[384,640]{1,0:T(8,128)(2,1)}, f32[384]{0:T(512)S(1)}, bf16[384,640]{1,0:T(8,128)(2,1)}) fusion(f32[384,1280]{1,0:T(8,128)S(1)} %fusion.21, bf16[304,3584]{1,0:T(8,128)(2,1)} %collective-permute-done.9, bf16[304,3584]{1,0:T(8,128)(2,1)S(1)} %bitcast.105, bf16[640]{0:T(1024)(128)(2,1)S(1)} %pad.38.clone, ...), kind=kOutput, calls=%fused_computation.97 | convolution fusion | flops 1779056256 | bytes 10062592 | tf_op jit(solution)/shard_map/dot_general | solution.py:43
  182.3 84.7 %all-to-all-done.2 = bf16[16,32,7168]{2,1,0:T(8,128)(2,1)} async-done(((bf16[16,32,7168]{2,1,0:T(8,128)(2,1)}), bf16[16,32,7168]{2,1,0:T(8,128)(2,1)}, u32[]{:S(2)}, u32[]{:S(2)}) %all-to-all-start.2) | async-done | bytes 7340064 | tf_op jit(solution)/shard_map/all_to_all | solution.py:27
  267.0 9.8 %fusion.11 = f32[512,1280]{1,0:T(8,128)S(1)} fusion(bf16[3584,1280]{0,1:T(8,128)(2,1)} %broadcast_dynamic-update-slice_fusion.2, bf16[512,7168]{1,0:T(8,128)(2,1)} %bitcast.18), kind=kOutput, calls=%fused_computation.19 | convolution fusion | flops 4697620480 | bytes 15466496 | tf_op jit(solution)/shard_map/dot_general | solution.py:42
  276.8 7.2 %multiply_convert_fusion = (bf16[512,640]{1,0:T(8,128)(2,1)}, f32[512]{0:T(512)S(1)}, bf16[512,640]{1,0:T(8,128)(2,1)}) fusion(f32[512,1280]{1,0:T(8,128)S(1)} %fusion.11, bf16[304,3584]{1,0:T(8,128)(2,1)} %collective-permute-done.9, bf16[304,3584]{1,0:T(8,128)(2,1)S(1)} %bitcast.106, bf16[640]{0:T(1024)(128)(2,1)S(1)} %pad.38.clone, ...), kind=kOutput, calls=%fused_computation.83 | convolution fusion | flops 2367487488 | bytes 11963648 | tf_op jit(solution)/shard_map/dot_general | solution.py:43
  284.1 6.9 %fusion.42 = f32[256,1280]{1,0:T(8,128)S(1)} fusion(bf16[3584,1280]{0,1:T(8,128)(2,1)} %broadcast_dynamic-update-slice_fusion.2, bf16[256,7168]{1,0:T(8,128)(2,1)} %collective-permute-done.12), kind=kOutput, calls=%fused_computation.58 | convolution fusion | flops 2348810240 | bytes 12320768 | tf_op jit(solution)/shard_map/dot_general | solution.py:42
  291.0 4.8 multiply_convert_fusion.4
  295.9 7.0 %fusion.38 = f32[256,1280]{1,0:T(8,128)S(1)} fusion(bf16[3584,1280]{0,1:T(8,128)(2,1)} %broadcast_dynamic-update-slice_fusion.2, bf16[256,7168]{1,0:T(8,128)(2,1)} %collective-permute-done.14), kind=kOutput, calls=%fused_computation.54 | convolution fusion | flops 2348810240 | bytes 12320768 | tf_op jit(solution)/shard_map/dot_general | solution.py:42
  303.0 4.9 multiply_convert_fusion.3
  308.7 7.7 %all-to-all-start.4 = ((f32[16,1,80]{2,1,0:T(1,128)}), f32[16,1,80]{2,1,0:T(1,128)S(1)}, u32[]{:S(2)}, u32[]{:S(2)}) async-start(f32[16,1,80]{2,1,0:T(1,128)} %bitcast.23), calls=%async_computation.4 | async-start | bytes 16384 | tf_op jit(solution)/shard_map/all_to_all | solution.py:27
  316.4 7.5 %convolution_convert_fusion.4 = bf16[256,3584]{1,0:T(8,128)(2,1)} fusion(bf16[3584,1280]{0,1:T(8,128)(2,1)} %broadcast_dynamic-update-slice_fusion.2, bf16[256,640]{1,0:T(8,128)(2,1)} %get-tuple-element.26, bf16[256,640]{1,0:T(8,128)(2,1)S(1)} %get-tuple-element.24), kind=kOutput, calls=%fused_computation.12 | convolution fusion | flops 2351038464 | bytes 11665408 | tf_op jit(solution)/shard_map/dot_general | solution.py:53
  326.4 2.8 collective-permute-start.20
  329.2 7.6 %convolution_convert_fusion.3 = bf16[256,3584]{1,0:T(8,128)(2,1)} fusion(bf16[3584,1280]{0,1:T(8,128)(2,1)} %broadcast_dynamic-update-slice_fusion.2, bf16[256,640]{1,0:T(8,128)(2,1)} %get-tuple-element.29, bf16[256,640]{1,0:T(8,128)(2,1)} %get-tuple-element.27), kind=kOutput, calls=%fused_computation.11 | convolution fusion | flops 2351038464 | bytes 11665408 | tf_op jit(solution)/shard_map/dot_general | solution.py:53
  337.3 28.2 %collective-permute-done.19 = f32[16,20]{1,0:T(8,128)S(1)} collective-permute-done((f32[16,20]{1,0:T(8,128)S(1)}, f32[16,20]{1,0:T(8,128)S(1)}, u32[]{:S(2)}, u32[]{:S(2)}) %collective-permute-start.19) | collective-permute-done | bytes 1312 | tf_op jit(solution)/shard_map/ppermute | solution.py:19
  369.0 9.4 %all-to-all-start.6 = ((f32[128,1,448]{2,1,0:T(1,128)}), f32[128,1,448]{2,1,0:T(1,128)S(1)}, u32[]{:S(2)}, u32[]{:S(2)}) async-start(f32[128,1,448]{2,1,0:T(1,128)} %all_to_all.67), calls=%async_computation.6 | async-start | bytes 524288 | tf_op jit(solution)/shard_map/all_to_all | solution.py:185
  378.4 10.8 %convolution_convert_fusion.2 = bf16[512,3584]{1,0:T(8,128)(2,1)} fusion(bf16[3584,1280]{0,1:T(8,128)(2,1)} %broadcast_dynamic-update-slice_fusion.2, bf16[512,640]{1,0:T(8,128)(2,1)} %get-tuple-element.15, bf16[512,640]{1,0:T(8,128)(2,1)} %get-tuple-element.13), kind=kOutput, calls=%fused_computation.3 | convolution fusion | flops 4702076928 | bytes 14155776 | tf_op jit(solution)/shard_map/dot_general | solution.py:53
  389.9 7.1 %all-to-all-start.3 = ((bf16[16,32,3584]{2,1,0:T(8,128)(2,1)}), bf16[16,32,3584]{2,1,0:T(8,128)(2,1)}, u32[]{:S(2)}, u32[]{:S(2)}) async-start(bf16[16,32,3584]{2,1,0:T(8,128)(2,1)} %bitcast.89), calls=%async_computation.3 | async-start | bytes 7340032 | tf_op jit(solution)/shard_map/all_to_all | solution.py:27
  397.1 6.4 %fusion.65 = f32[384,3584]{1,0:T(8,128)S(1)} fusion(bf16[3584,1280]{0,1:T(8,128)(2,1)} %broadcast_dynamic-update-slice_fusion.2, bf16[384,640]{1,0:T(8,128)(2,1)} %get-tuple-element.20, bf16[384,640]{1,0:T(8,128)(2,1)S(1)} %copy-done.20), kind=kOutput, calls=%fused_computation.91 | convolution fusion | flops 3525181440 | bytes 15663104 | tf_op jit(solution)/shard_map/dot_general | solution.py:53
  407.9 41.2 %all-to-all-done.3 = bf16[16,32,3584]{2,1,0:T(8,128)(2,1)} async-done(((bf16[16,32,3584]{2,1,0:T(8,128)(2,1)}), bf16[16,32,3584]{2,1,0:T(8,128)(2,1)}, u32[]{:S(2)}, u32[]{:S(2)}) %all-to-all-start.3) | async-done | bytes 3670048 | tf_op jit(solution)/shard_map/all_to_all | solution.py:27
  449.1 11.7 %all-to-all-start.1 = ((bf16[16,24,3584]{2,1,0:T(8,128)(2,1)}), bf16[16,24,3584]{2,1,0:T(8,128)(2,1)}, u32[]{:S(2)}, u32[]{:S(2)}) async-start(bf16[16,24,3584]{2,1,0:T(8,128)(2,1)} %pad_maximum_fusion.1), calls=%async_computation.1 | async-start | bytes 5505024 | tf_op jit(solution)/shard_map/all_to_all | solution.py:27
  460.9 7.4 %fusion.53 = f32[512,3584]{1,0:T(8,128)S(1)} fusion(bf16[3584,1280]{0,1:T(8,128)(2,1)} %broadcast_dynamic-update-slice_fusion.3, bf16[512,640]{1,0:T(8,128)(2,1)S(1)} %copy-done.22, bf16[512,640]{1,0:T(8,128)(2,1)S(1)} %copy-done.21), kind=kOutput, calls=%fused_computation.74 | convolution fusion | flops 4700241920 | bytes 17825792 | tf_op jit(solution)/shard_map/dot_general | solution.py:53
  468.3 6.4 %fusion = bf16[384,3584]{1,0:T(8,128)(2,1)S(1)} fusion(f32[512,3584]{1,0:T(8,128)S(1)} %fusion.53, bf16[512,3584]{1,0:T(8,128)(2,1)} %bitcast.20, bf16[384,512]{1,0:T(8,128)(2,1)S(1)} %select_reduce_fusion), kind=kOutput, calls=%fused_computation.5 | convolution fusion | flops 1412038656 | bytes 12320768 | tf_op jit(solution)/shard_map/dot_general | solution.py:166
  483.2 10.3 %all-to-all-done.1 = bf16[16,24,3584]{2,1,0:T(8,128)(2,1)} async-done(((bf16[16,24,3584]{2,1,0:T(8,128)(2,1)}), bf16[16,24,3584]{2,1,0:T(8,128)(2,1)}, u32[]{:S(2)}, u32[]{:S(2)}) %all-to-all-start.1) | async-done | bytes 2752544 | tf_op jit(solution)/shard_map/all_to_all | solution.py:27
  494.4 12.2 %all-to-all-start.7 = ((f32[128,1,448]{2,1,0:T(1,128)}), f32[128,1,448]{2,1,0:T(1,128)S(1)}, u32[]{:S(2)}, u32[]{:S(2)}) async-start(f32[128,1,448]{2,1,0:T(1,128)} %broadcast_in_dim.92), calls=%async_computation.7 | async-start | bytes 524288 | tf_op jit(solution)/shard_map/all_to_all | solution.py:187
  506.6 14.3 %collective-permute-done.17 = bf16[128,3584]{1,0:T(8,128)(2,1)} collective-permute-done((bf16[128,3584]{1,0:T(8,128)(2,1)}, bf16[128,3584]{1,0:T(8,128)(2,1)}, u32[]{:S(2)}, u32[]{:S(2)}) %collective-permute-start.17) | collective-permute-done | bytes 917536 | tf_op jit(solution)/shard_map/ppermute | solution.py:19
  521.7 5.7 %fusion.37 = (f32[3584]{0:T(1024)S(1)}, f32[128]{0:T(128)S(1)}, f32[128,3584]{1,0:T(8,128)}) fusion(bf16[128,3584]{1,0:T(8,128)(2,1)S(1)} %copy-done.4, f32[128]{0:T(128)S(1)} %copy-done.14, f32[3584]{0:T(1024)S(1)} %copy-done.12, f32[128,3584]{1,0:T(8,128)S(1)} %fusion.91, bf16[128,3584]{1,0:T(8,128)(2,1)} %collective-permute-done.18, ...), kind=kOutput, calls=%fused_computation.52 | convolution fusion | flops 359199104 | bytes 12055552 | tf_op jit(solution)/shard_map/dot_general | solution.py:171
  529.6 11.1 %all-to-all-start.5 = ((f32[128,1,3584]{2,1,0:T(1,128)}), f32[128,1,3584]{2,1,0:T(1,128)}, u32[]{:S(2)}, u32[]{:S(2)}) async-start(f32[128,1,3584]{2,1,0:T(1,128)} %broadcast_in_dim.91), calls=%async_computation.5 | async-start | bytes 3670016 | tf_op jit(solution)/shard_map/all_to_all | solution.py:194
  542.1 3.0 fusion.33
  545.2 22.7 %all-to-all-done.5 = f32[128,1,3584]{2,1,0:T(1,128)} async-done(((f32[128,1,3584]{2,1,0:T(1,128)}), f32[128,1,3584]{2,1,0:T(1,128)}, u32[]{:S(2)}, u32[]{:S(2)}) %all-to-all-start.5) | async-done | bytes 1835040 | tf_op jit(solution)/shard_map/all_to_all | solution.py:194
  567.9 3.1 reduce_sum.164
  (164 shorter events, 52.9 us)
Async XLA Ops:
  0.6 108.5 %copy-start = (f32[3584,16]{0,1:T(8,128)S(1)}, f32[3584,16]{0,1:T(8,128)}, u32[]{:S(2)}) copy-start(f32[3584,16]{0,1:T(8,128)} %param.14) | copy-start | bytes 688132
  1.5 14.3 %copy-start.6 = (bf16[1,3584,304]{1,2,0:T(8,128)(2,1)S(1)}, bf16[1,3584,304]{1,2,0:T(8,128)(2,1)}, u32[]{:S(2)}) copy-start(bf16[1,3584,304]{1,2,0:T(8,128)(2,1)} %param.18) | copy-start | bytes 6537220
  1.5 17.5 %collective-permute-start.6 = (s32[128,2]{1,0:T(8,128)S(1)}, s32[128,2]{1,0:T(8,128)S(1)}, u32[]{:S(2)}, u32[]{:S(2)}) collective-permute-start(s32[128,2]{1,0:T(8,128)S(1)} %copy.87), channel_id=1, source_target_pairs={{0,6},{2,0},{4,2},{6,4},{1,7},{3,1},{5,3},{7,5},{8,14},{10,8},{12,... | collective-permute-start | bytes 3080 | tf_op jit(solution)/shard_map/ppermute | solution.py:15
  5.1 14.1 %collective-permute-start.7 = (s32[128,2]{1,0:T(8,128)S(1)}, s32[128,2]{1,0:T(8,128)S(1)}, u32[]{:S(2)}, u32[]{:S(2)}) collective-permute-start(s32[128,2]{1,0:T(8,128)S(1)} %copy.87), channel_id=1, source_target_pairs={{0,4},{2,6},{4,0},{6,2},{1,5},{3,7},{5,1},{7,3},{8,12},{10,14},{12... | collective-permute-start | bytes 3080 | tf_op jit(solution)/shard_map/ppermute | solution.py:15
  5.5 16.0 %collective-permute-start.8 = (s32[128,2]{1,0:T(8,128)S(1)}, s32[128,2]{1,0:T(8,128)S(1)}, u32[]{:S(2)}, u32[]{:S(2)}) collective-permute-start(s32[128,2]{1,0:T(8,128)S(1)} %copy.87), channel_id=1, source_target_pairs={{0,2},{2,4},{4,6},{6,0},{1,3},{3,5},{5,7},{7,1},{8,10},{10,12},{12... | collective-permute-start | bytes 3080 | tf_op jit(solution)/shard_map/ppermute | solution.py:15
  9.7 7.6 %copy-start.8 = (bf16[3584,304]{0,1:T(8,128)(2,1)S(1)}, bf16[3584,304]{0,1:T(8,128)(2,1)}, u32[]{:S(2)}) copy-start(bf16[3584,304]{0,1:T(8,128)(2,1)} %param.15) | copy-start | bytes 6537220
  12.4 9.8 %copy-start.15 = (s32[128,2]{0,1:T(2,128)S(1)}, s32[128,2]{0,1:T(2,128)}, u32[]{:S(2)}) copy-start(s32[128,2]{0,1:T(2,128)} %param.21) | copy-start | bytes 3076
  12.4 10.0 %copy-start.2 = (bf16[128,3584]{1,0:T(8,128)(2,1)S(1)}, bf16[128,3584]{1,0:T(8,128)(2,1)}, u32[]{:S(2)}) copy-start(bf16[128,3584]{1,0:T(8,128)(2,1)} %param.12) | copy-start | bytes 2752516
  12.4 40.6 %collective-permute-start = (bf16[128,7168]{1,0:T(8,128)(2,1)}, bf16[128,7168]{1,0:T(8,128)(2,1)}, u32[]{:S(2)}, u32[]{:S(2)}) collective-permute-start(bf16[128,7168]{1,0:T(8,128)(2,1)} %pad_maximum_fusion.2), channel_id=1, source_target_pairs={{0,6},{2,0},{4,2},{6,4},{1,7},{3,1},{5,3},{7,5},{8,14},{10,8},{12,... | collective-permute-start | bytes 5505032 | tf_op jit(solution)/shard_map/ppermute | solution.py:15
  14.4 79.9 %collective-permute-start.1 = (bf16[128,7168]{1,0:T(8,128)(2,1)}, bf16[128,7168]{1,0:T(8,128)(2,1)}, u32[]{:S(2)}, u32[]{:S(2)}) collective-permute-start(bf16[128,7168]{1,0:T(8,128)(2,1)} %pad_maximum_fusion.2), channel_id=1, source_target_pairs={{0,4},{2,6},{4,0},{6,2},{1,5},{3,7},{5,1},{7,3},{8,12},{10,14},{12... | collective-permute-start | bytes 5505032 | tf_op jit(solution)/shard_map/ppermute | solution.py:15
  19.0 78.4 %collective-permute-start.2 = (bf16[128,7168]{1,0:T(8,128)(2,1)}, bf16[128,7168]{1,0:T(8,128)(2,1)}, u32[]{:S(2)}, u32[]{:S(2)}) collective-permute-start(bf16[128,7168]{1,0:T(8,128)(2,1)} %pad_maximum_fusion.2), channel_id=1, source_target_pairs={{0,2},{2,4},{4,6},{6,0},{1,3},{3,5},{5,7},{7,1},{8,10},{10,12},{12... | collective-permute-start | bytes 5505032 | tf_op jit(solution)/shard_map/ppermute | solution.py:15
  19.2 118.7 %collective-permute-start.4 = (bf16[3584,304]{0,1:T(8,128)(2,1)}, bf16[3584,304]{0,1:T(8,128)(2,1)}, u32[]{:S(2)}, u32[]{:S(2)}) collective-permute-start(bf16[3584,304]{0,1:T(8,128)(2,1)} %param.15), channel_id=1, source_target_pairs={{0,1},{1,0},{2,3},{3,2},{4,5},{5,4},{6,7},{7,6},{8,9},{9,8},{10,11... | collective-permute-start | bytes 6537224 | tf_op jit(solution)/shard_map/ppermute | solution.py:23
  21.5 100.5 %collective-permute-start.10 = (bf16[3584,304]{0,1:T(8,128)(2,1)}, bf16[3584,304]{0,1:T(8,128)(2,1)}, u32[]{:S(2)}, u32[]{:S(2)}) collective-permute-start(bf16[3584,304]{0,1:T(8,128)(2,1)} %bitcast.90), channel_id=1, source_target_pairs={{0,1},{1,0},{2,3},{3,2},{4,5},{5,4},{6,7},{7,6},{8,9},{9,8},{10,11... | collective-permute-start | bytes 6537224 | tf_op jit(solution)/shard_map/ppermute | solution.py:23
  26.4 102.8 %all-to-all-start = ((bf16[16,24,7168]{2,1,0:T(8,128)(2,1)}), bf16[16,24,7168]{2,1,0:T(8,128)(2,1)}, u32[]{:S(2)}, u32[]{:S(2)}) async-start(bf16[16,24,7168]{2,1,0:T(8,128)(2,1)} %bitcast.82), calls=%async_computation | async-start | bytes 11010048 | tf_op jit(solution)/shard_map/all_to_all | solution.py:27
  53.0 74.8 %collective-permute-start.11 = (bf16[3584,304]{0,1:T(8,128)(2,1)}, bf16[3584,304]{0,1:T(8,128)(2,1)S(1)}, u32[]{:S(2)}, u32[]{:S(2)}) collective-permute-start(bf16[3584,304]{0,1:T(8,128)(2,1)} %bitcast.91), channel_id=1, source_target_pairs={{0,1},{1,0},{2,3},{3,2},{4,5},{5,4},{6,7},{7,6},{8,9},{9,8},{10,11... | collective-permute-start | bytes 6537224 | tf_op jit(solution)/shard_map/ppermute | solution.py:23
  94.3 81.9 %collective-permute-start.9 = (bf16[304,3584]{1,0:T(8,128)(2,1)}, bf16[304,3584]{1,0:T(8,128)(2,1)}, u32[]{:S(2)}, u32[]{:S(2)}) collective-permute-start(bf16[304,3584]{1,0:T(8,128)(2,1)} %bitcast.104), channel_id=1, source_target_pairs={{0,1},{1,0},{2,3},{3,2},{4,5},{5,4},{6,7},{7,6},{8,9},{9,8},{10,11... | collective-permute-start | bytes 6537224 | tf_op jit(solution)/shard_map/ppermute | solution.py:23
  97.5 45.9 %collective-permute-start.5 = (bf16[3584,304]{0,1:T(8,128)(2,1)}, bf16[3584,304]{0,1:T(8,128)(2,1)}, u32[]{:S(2)}, u32[]{:S(2)}) collective-permute-start(bf16[3584,304]{0,1:T(8,128)(2,1)} %param.16), channel_id=1, source_target_pairs={{0,1},{1,0},{2,3},{3,2},{4,5},{5,4},{6,7},{7,6},{8,9},{9,8},{10,11... | collective-permute-start | bytes 6537224 | tf_op jit(solution)/shard_map/ppermute | solution.py:23
  122.0 32.9 %collective-permute-start.3 = (bf16[304,3584]{1,0:T(8,128)(2,1)}, bf16[304,3584]{1,0:T(8,128)(2,1)}, u32[]{:S(2)}, u32[]{:S(2)}) collective-permute-start(bf16[304,3584]{1,0:T(8,128)(2,1)} %param.17), channel_id=1, source_target_pairs={{0,1},{1,0},{2,3},{3,2},{4,5},{5,4},{6,7},{7,6},{8,9},{9,8},{10,11... | collective-permute-start | bytes 6537224 | tf_op jit(solution)/shard_map/ppermute | solution.py:23
  129.2 137.7 %all-to-all-start.2 = ((bf16[16,32,7168]{2,1,0:T(8,128)(2,1)}), bf16[16,32,7168]{2,1,0:T(8,128)(2,1)}, u32[]{:S(2)}, u32[]{:S(2)}) async-start(bf16[16,32,7168]{2,1,0:T(8,128)(2,1)} %bitcast.86), calls=%async_computation.2 | async-start | bytes 14680064 | tf_op jit(solution)/shard_map/all_to_all | solution.py:27
  137.8 9.6 %slice-start = ((s8[7340032]{0:T(1024)(128)(4,1)}), s8[4194304]{0:T(1024)(128)(4,1)S(1)}, s32[]{:S(2)}) async-start(s8[7340032]{0:T(1024)(128)(4,1)} %bitcast.83), calls=%async_computation.8 | async-start | bytes 8388608
  166.0 118.2 %collective-permute-start.12 = (bf16[256,7168]{1,0:T(8,128)(2,1)}, bf16[256,7168]{1,0:T(8,128)(2,1)}, u32[]{:S(2)}, u32[]{:S(2)}) collective-permute-start(bf16[256,7168]{1,0:T(8,128)(2,1)} %bitcast.13), channel_id=1, source_target_pairs={{0,6},{2,0},{4,2},{6,4},{1,7},{3,1},{5,3},{7,5},{8,14},{10,8},{12,... | collective-permute-start | bytes 11010056 | tf_op jit(solution)/shard_map/ppermute | solution.py:15
  166.3 129.7 %collective-permute-start.14 = (bf16[256,7168]{1,0:T(8,128)(2,1)}, bf16[256,7168]{1,0:T(8,128)(2,1)}, u32[]{:S(2)}, u32[]{:S(2)}) collective-permute-start(bf16[256,7168]{1,0:T(8,128)(2,1)} %bitcast.13), channel_id=1, source_target_pairs={{0,2},{2,4},{4,6},{6,0},{1,3},{3,5},{5,7},{7,1},{8,10},{10,12},{12... | collective-permute-start | bytes 11010056 | tf_op jit(solution)/shard_map/ppermute | solution.py:15
  167.8 8.3 %copy-start.16 = (bf16[1,304,3584]{2,1,0:T(8,128)(2,1)S(1)}, bf16[1,304,3584]{2,1,0:T(8,128)(2,1)}, u32[]{:S(2)}) copy-start(bf16[1,304,3584]{2,1,0:T(8,128)(2,1)} %param.20) | copy-start | bytes 6537220
  267.0 9.8 %copy-start.17 = (bf16[1,304,3584]{2,1,0:T(8,128)(2,1)S(1)}, bf16[1,304,3584]{2,1,0:T(8,128)(2,1)}, u32[]{:S(2)}) copy-start(bf16[1,304,3584]{2,1,0:T(8,128)(2,1)} %param.20) | copy-start | bytes 6537220
  284.1 6.9 %copy-start.18 = (bf16[1,304,3584]{2,1,0:T(8,128)(2,1)S(1)}, bf16[1,304,3584]{2,1,0:T(8,128)(2,1)}, u32[]{:S(2)}) copy-start(bf16[1,304,3584]{2,1,0:T(8,128)(2,1)} %param.20) | copy-start | bytes 6537220
  295.9 7.0 %copy-start.19 = (bf16[1,304,3584]{2,1,0:T(8,128)(2,1)S(1)}, bf16[1,304,3584]{2,1,0:T(8,128)(2,1)}, u32[]{:S(2)}) copy-start(bf16[1,304,3584]{2,1,0:T(8,128)(2,1)} %param.20) | copy-start | bytes 6537220
  308.7 15.3 %all-to-all-start.4 = ((f32[16,1,80]{2,1,0:T(1,128)}), f32[16,1,80]{2,1,0:T(1,128)S(1)}, u32[]{:S(2)}, u32[]{:S(2)}) async-start(f32[16,1,80]{2,1,0:T(1,128)} %bitcast.23), calls=%async_computation.4 | async-start | bytes 16384 | tf_op jit(solution)/shard_map/all_to_all | solution.py:27
  323.9 79.6 %collective-permute-start.13 = (bf16[256,3584]{1,0:T(8,128)(2,1)}, bf16[256,3584]{1,0:T(8,128)(2,1)S(1)}, u32[]{:S(2)}, u32[]{:S(2)}) collective-permute-start(bf16[256,3584]{1,0:T(8,128)(2,1)} %convolution_convert_fusion.4), channel_id=1, source_target_pairs={{0,2},{2,4},{4,6},{6,0},{1,3},{3,5},{5,7},{7,1},{8,10},{10,12},{12... | collective-permute-start | bytes 5505032 | tf_op jit(solution)/shard_map/ppermute | solution.py:19
  325.3 40.2 %collective-permute-start.19 = (f32[16,20]{1,0:T(8,128)S(1)}, f32[16,20]{1,0:T(8,128)S(1)}, u32[]{:S(2)}, u32[]{:S(2)}) collective-permute-start(f32[16,20]{1,0:T(8,128)S(1)} %bitcast.103), channel_id=1, source_target_pairs={{0,2},{2,4},{4,6},{6,0},{1,3},{3,5},{5,7},{7,1},{8,10},{10,12},{12... | collective-permute-start | bytes 3848 | tf_op jit(solution)/shard_map/ppermute | solution.py:19
  326.4 39.0 %collective-permute-start.20 = (f32[16,20]{1,0:T(8,128)S(1)}, f32[16,20]{1,0:T(8,128)S(1)}, u32[]{:S(2)}, u32[]{:S(2)}) collective-permute-start(f32[16,20]{1,0:T(8,128)S(1)} %bitcast.102), channel_id=1, source_target_pairs={{0,4},{2,6},{4,0},{6,2},{1,5},{3,7},{5,1},{7,3},{8,12},{10,14},{12... | collective-permute-start | bytes 3848 | tf_op jit(solution)/shard_map/ppermute | solution.py:19
  329.2 36.3 %collective-permute-start.21 = (f32[16,20]{1,0:T(8,128)S(1)}, f32[16,20]{1,0:T(8,128)S(1)}, u32[]{:S(2)}, u32[]{:S(2)}) collective-permute-start(f32[16,20]{1,0:T(8,128)S(1)} %bitcast.101), channel_id=1, source_target_pairs={{0,6},{2,0},{4,2},{6,4},{1,7},{3,1},{5,3},{7,5},{8,14},{10,8},{12,... | collective-permute-start | bytes 3848 | tf_op jit(solution)/shard_map/ppermute | solution.py:19
  336.8 66.8 %collective-permute-start.15 = (bf16[256,3584]{1,0:T(8,128)(2,1)}, bf16[256,3584]{1,0:T(8,128)(2,1)}, u32[]{:S(2)}, u32[]{:S(2)}) collective-permute-start(bf16[256,3584]{1,0:T(8,128)(2,1)} %convolution_convert_fusion.3), channel_id=1, source_target_pairs={{0,6},{2,0},{4,2},{6,4},{1,7},{3,1},{5,3},{7,5},{8,14},{10,8},{12,... | collective-permute-start | bytes 5505032 | tf_op jit(solution)/shard_map/ppermute | solution.py:19
  369.0 20.3 %all-to-all-start.6 = ((f32[128,1,448]{2,1,0:T(1,128)}), f32[128,1,448]{2,1,0:T(1,128)S(1)}, u32[]{:S(2)}, u32[]{:S(2)}) async-start(f32[128,1,448]{2,1,0:T(1,128)} %all_to_all.67), calls=%async_computation.6 | async-start | bytes 524288 | tf_op jit(solution)/shard_map/all_to_all | solution.py:185
  389.2 7.9 %copy-start.20 = (bf16[384,640]{1,0:T(8,128)(2,1)S(1)}, bf16[384,640]{1,0:T(8,128)(2,1)}, u32[]{:S(2)}) copy-start(bf16[384,640]{1,0:T(8,128)(2,1)} %get-tuple-element.18) | copy-start | bytes 1474564
  389.9 59.2 %all-to-all-start.3 = ((bf16[16,32,3584]{2,1,0:T(8,128)(2,1)}), bf16[16,32,3584]{2,1,0:T(8,128)(2,1)}, u32[]{:S(2)}, u32[]{:S(2)}) async-start(bf16[16,32,3584]{2,1,0:T(8,128)(2,1)} %bitcast.89), calls=%async_computation.3 | async-start | bytes 7340032 | tf_op jit(solution)/shard_map/all_to_all | solution.py:27
  407.9 53.0 %copy-start.21 = (bf16[512,640]{1,0:T(8,128)(2,1)S(1)}, bf16[512,640]{1,0:T(8,128)(2,1)}, u32[]{:S(2)}) copy-start(bf16[512,640]{1,0:T(8,128)(2,1)} %get-tuple-element.16) | copy-start | bytes 1966084
  407.9 53.0 %copy-start.22 = (bf16[512,640]{1,0:T(8,128)(2,1)S(1)}, bf16[512,640]{1,0:T(8,128)(2,1)}, u32[]{:S(2)}) copy-start(bf16[512,640]{1,0:T(8,128)(2,1)} %get-tuple-element.17) | copy-start | bytes 1966084
  449.1 44.4 %all-to-all-start.1 = ((bf16[16,24,3584]{2,1,0:T(8,128)(2,1)}), bf16[16,24,3584]{2,1,0:T(8,128)(2,1)}, u32[]{:S(2)}, u32[]{:S(2)}) async-start(bf16[16,24,3584]{2,1,0:T(8,128)(2,1)} %pad_maximum_fusion.1), calls=%async_computation.1 | async-start | bytes 5505024 | tf_op jit(solution)/shard_map/all_to_all | solution.py:27
  474.7 8.2 %copy-start.11 = (f32[128,1,448]{2,1,0:T(1,128)S(1)}, f32[128,1,448]{2,1,0:T(1,128)}, u32[]{:S(2)}) copy-start(f32[128,1,448]{2,1,0:T(1,128)} %copy-done.10) | copy-start | bytes 688132
  474.7 47.0 %copy-start.4 = (bf16[128,3584]{1,0:T(8,128)(2,1)S(1)}, bf16[128,3584]{1,0:T(8,128)(2,1)}, u32[]{:S(2)}) copy-start(bf16[128,3584]{1,0:T(8,128)(2,1)} %param.11) | copy-start | bytes 2752516
  474.7 47.0 %copy-start.12 = (f32[3584]{0:T(1024)S(1)}, f32[3584]{0:T(1024)}, u32[]{:S(2)}) copy-start(f32[3584]{0:T(1024)} %param.13) | copy-start | bytes 43012
  474.7 47.0 %copy-start.14 = (f32[128]{0:T(128)S(1)}, f32[128]{0:T(128)}, u32[]{:S(2)}) copy-start(f32[128]{0:T(128)} %copy-done.13) | copy-start | bytes 1540
  476.4 30.2 %collective-permute-start.16 = (bf16[128,3584]{1,0:T(8,128)(2,1)}, bf16[128,3584]{1,0:T(8,128)(2,1)}, u32[]{:S(2)}, u32[]{:S(2)}) collective-permute-start(bf16[128,3584]{1,0:T(8,128)(2,1)} %get-tuple-element.21), channel_id=1, source_target_pairs={{0,2},{2,4},{4,6},{6,0},{1,3},{3,5},{5,7},{7,1},{8,10},{10,12},{12... | collective-permute-start | bytes 2752520 | tf_op jit(solution)/shard_map/ppermute | solution.py:19
  477.7 43.2 %collective-permute-start.17 = (bf16[128,3584]{1,0:T(8,128)(2,1)}, bf16[128,3584]{1,0:T(8,128)(2,1)}, u32[]{:S(2)}, u32[]{:S(2)}) collective-permute-start(bf16[128,3584]{1,0:T(8,128)(2,1)} %get-tuple-element.23), channel_id=1, source_target_pairs={{0,4},{2,6},{4,0},{6,2},{1,5},{3,7},{5,1},{7,3},{8,12},{10,14},{12... | collective-permute-start | bytes 2752520 | tf_op jit(solution)/shard_map/ppermute | solution.py:19
  480.2 41.5 %collective-permute-start.18 = (bf16[128,3584]{1,0:T(8,128)(2,1)}, bf16[128,3584]{1,0:T(8,128)(2,1)}, u32[]{:S(2)}, u32[]{:S(2)}) collective-permute-start(bf16[128,3584]{1,0:T(8,128)(2,1)} %get-tuple-element.22), channel_id=1, source_target_pairs={{0,6},{2,0},{4,2},{6,4},{1,7},{3,1},{5,3},{7,5},{8,14},{10,8},{12,... | collective-permute-start | bytes 2752520 | tf_op jit(solution)/shard_map/ppermute | solution.py:19
  494.4 33.1 %all-to-all-start.7 = ((f32[128,1,448]{2,1,0:T(1,128)}), f32[128,1,448]{2,1,0:T(1,128)S(1)}, u32[]{:S(2)}, u32[]{:S(2)}) async-start(f32[128,1,448]{2,1,0:T(1,128)} %broadcast_in_dim.92), calls=%async_computation.7 | async-start | bytes 524288 | tf_op jit(solution)/shard_map/all_to_all | solution.py:187
  527.4 14.7 %copy-start.3 = (bf16[128,3584]{1,0:T(8,128)(2,1)S(1)}, bf16[128,3584]{1,0:T(8,128)(2,1)}, u32[]{:S(2)}) copy-start(bf16[128,3584]{1,0:T(8,128)(2,1)} %param.12) | copy-start | bytes 2752516
  529.6 38.3 %all-to-all-start.5 = ((f32[128,1,3584]{2,1,0:T(1,128)}), f32[128,1,3584]{2,1,0:T(1,128)}, u32[]{:S(2)}, u32[]{:S(2)}) async-start(f32[128,1,3584]{2,1,0:T(1,128)} %broadcast_in_dim.91), calls=%async_computation.5 | async-start | bytes 3670016 | tf_op jit(solution)/shard_map/all_to_all | solution.py:194
  (7 other events, 25.4 us)

commit v2 on v1

v2 whole, which is shorter than its diff:
```python
import jax
import jax.numpy as jnp
from jax import lax
from jax.sharding import Mesh, PartitionSpec as P

EPS = 1e-05
BF = jnp.bfloat16
F32 = jnp.float32
HIGHEST = lax.Precision.HIGHEST
PEERS = 4


def receive_from(value, k):
    return lax.ppermute(value, "y", [(i, (i - k) % PEERS) for i in range(PEERS)])


def send_to(value, k):
    return lax.ppermute(value, "y", [(i, (i + k) % PEERS) for i in range(PEERS)])


def swap(value):
    return lax.ppermute(value, "core", [(0, 1), (1, 0)])


def over_ep(value):
    return lax.all_to_all(value, "ep", split_axis=0, concat_axis=0, tiled=True)


def join_weights(gate, up, down):
    hidden = 2 * gate.shape[1]
    pad = -hidden % 128
    blank = jnp.zeros((gate.shape[0], pad), BF)
    wide = jnp.concatenate([gate, swap(gate), blank, up, swap(up), blank], 1)
    tall = jnp.concatenate([down, swap(down), jnp.zeros((pad, down.shape[1]), BF)], 0)
    return wide, tall


def hidden_grads(rows, wide, tall):
    width = tall.shape[1]
    half = tall.shape[0]
    both = jnp.dot(rows[:, :width], wide, preferred_element_type=F32)
    back = lax.dot_general(
        rows[:, width:], tall, (((1,), (1,)), ((), ())), preferred_element_type=F32
    )
    gate, up = both[:, :half], both[:, half:]
    sig = jax.nn.sigmoid(gate)
    active = gate * sig
    grad_up = back * active
    grad_gate = back * up * (sig * (1.0 + gate * (1.0 - sig)))
    joint = jnp.sum(grad_up * up, -1)
    grads = jnp.concatenate([grad_gate.astype(BF), grad_up.astype(BF)], 1)
    into = lax.dot_general(grads, wide, (((1,), (1,)), ((), ())), preferred_element_type=F32)
    return into, joint


def after(value, *others):
    return lax.optimization_barrier((value,) + others)[0]


def over_all(value):
    value = value + swap(value)
    parts = [receive_from(value, j) for j in (1, 2, 3)]
    value = (value + parts[0]) + (parts[1] + parts[2])
    count = lax.axis_size("ep")
    side = 4
    for stride, block in ((1, side), (side, count)):
        parts = []
        for j in range(1, block // stride):
            pairs = [
                (i, i // block * block + (i % block + j * stride) % block) for i in range(count)
            ]
            parts.append(lax.ppermute(value, "ep", pairs))
        for part in parts:
            value = value + part
    return value


def slot_rows(routes, experts, rows):
    tok = routes.shape[0]
    flat = routes.reshape(2 * tok, 1)
    hits = (flat == lax.broadcasted_iota(jnp.int32, (1, experts), 1)).astype(BF)
    place = lax.broadcasted_iota(jnp.int32, (2 * tok, 2 * tok), 0)
    before = (lax.broadcasted_iota(jnp.int32, (2 * tok, 2 * tok), 1) < place).astype(BF)
    places = jnp.dot(before, hits, preferred_element_type=F32)
    slots = jnp.sum(hits.astype(F32) * places, -1).astype(jnp.int32).reshape(tok, 2)
    index = routes * rows + slots
    return index[..., None] == lax.broadcasted_iota(jnp.int32, (1, 1, experts * rows), 2)


def pick(hot, rows):
    table = jnp.sum(hot.astype(BF), 1)
    return lax.dot_general(
        table, rows, (((0,), (0,)), ((), ())), preferred_element_type=F32
    ).astype(BF)


def router_weights(normed, router, chosen):
    logits = jnp.dot(normed.astype(F32), router, precision=HIGHEST)
    picked = jnp.sum(jnp.where(chosen, logits[:, None, :], 0.0), -1)
    one = jax.nn.sigmoid(picked[:, 0:1] - picked[:, 1:2])
    return jnp.concatenate([one, 1.0 - one], 1)


def mix(hot, weights, rows):
    table = jnp.sum(jnp.where(hot, weights[..., None], 0.0), 1).astype(BF)
    return jnp.dot(table, rows, preferred_element_type=F32)


def body(
    tokens,
    cotangent,
    norm_gain,
    router,
    dense_gate,
    dense_up,
    dense_down,
    expert_gate,
    expert_up,
    expert_down,
    routes,
):
    tok, width = tokens.shape
    experts = router.shape[1]
    cap = 5 * tok // (2 * experts)
    cap = -(-cap // 8) * 8

    values = tokens.astype(F32)
    inverse = lax.rsqrt(jnp.mean(values * values, -1, keepdims=True) + EPS)
    normed = (values * inverse * norm_gain).astype(BF)
    pair = jnp.concatenate([normed, cotangent], 1)

    peer2 = receive_from(pair, 2)
    routes2 = receive_from(routes, 2)
    hot = slot_rows(routes, experts, cap)
    own = over_ep(pick(hot, pair))
    later = after(pair, peer2)
    peer1 = receive_from(later, 1)
    peer3 = receive_from(later, 3)

    hot2 = slot_rows(routes2, experts, cap)
    far_send = pick(hot2, peer2)
    far = over_ep(far_send)
    near1 = receive_from(own, 1)
    near3 = receive_from(own, 3)

    wide_e, tall_e = join_weights(expert_gate[0], expert_up[0], expert_down[0])
    wide_d, tall_d = join_weights(dense_gate, dense_up, dense_down)

    own_into, own_joint = hidden_grads(after(own, far_send), wide_e, tall_e)
    dense_rows = jnp.concatenate([pair, peer1, peer2, peer3], 0)
    dense_part, unused = hidden_grads(after(dense_rows, own_into), wide_d, tall_d)
    home1 = send_to(dense_part[tok : 2 * tok].astype(BF), 1)
    home3 = send_to(dense_part[3 * tok :].astype(BF), 3)

    far_into, far_joint = hidden_grads(after(far, dense_part), wide_e, tall_e)
    far_into = far_into.astype(BF)
    far_back = over_ep(far_into)
    near1_into, near1_joint = hidden_grads(after(near1, far_into), wide_e, tall_e)
    near1_back = send_to(near1_into.astype(BF), 1)
    near3_into, near3_joint = hidden_grads(after(near3, near1_into), wide_e, tall_e)
    near3_back = send_to(near3_into.astype(BF), 3)

    joints = jnp.stack([own_joint, near1_joint, far_joint, near3_joint])
    joints = joints.reshape(4, experts, cap).transpose(1, 0, 2).reshape(experts, 4 * cap)
    joints = over_ep(after(joints, far_back))
    own_into = own_into + near1_back.astype(F32) + near3_back.astype(F32)
    own_back = over_ep(after(own_into.astype(BF), joints))

    ids = lax.broadcasted_iota(jnp.int32, (1, 1, experts), 2)
    chosen = routes[..., None] == ids
    weights = router_weights(normed, router, chosen)
    weights2 = router_weights(peer2[:, :width], router, routes2[..., None] == ids)

    part = dense_part[2 * tok : 3 * tok] + mix(hot2, weights2, far_back)
    home2 = send_to(part.astype(BF), 2)

    joints = joints.reshape(experts, 4, cap)
    score = joints[:, 0]
    for k in (1, 2, 3):
        score = score + send_to(joints[:, k], k)
    scores = jnp.sum(jnp.where(hot, score.reshape(1, 1, -1), 0.0), -1)
    delta = weights[:, 0] * weights[:, 1] * (scores[:, 0] - scores[:, 1])
    signed = chosen[:, 0].astype(F32) - chosen[:, 1].astype(F32)
    grad_logits = signed * delta[:, None]
    local_router = lax.dot_general(
        grad_logits, normed.astype(F32), (((0,), (0,)), ((), ())), precision=HIGHEST
    )
    router_grad = over_all(local_router).T
    early = dense_part[:tok] + jnp.dot(grad_logits, router.T, precision=HIGHEST)

    total = early + mix(hot, weights, own_back)
    for piece in (home1, home3, home2):
        total = total + piece.astype(F32)
    local_gain = jnp.sum(total * values * inverse, 0)
    axes = ("ep", "y", "core")
    devices = lax.axis_size(axes)
    gains = lax.all_to_all(
        jnp.broadcast_to(local_gain[None], (devices, width)), axes, 0, 0, tiled=True
    )
    gain_grad = jnp.sum(gains, 0)
    scaled = total * norm_gain
    mean_term = jnp.mean(scaled * values, -1, keepdims=True)
    input_grad = cotangent.astype(F32) + inverse * (
        scaled - values * inverse * inverse * mean_term
    )
    return (input_grad.astype(BF), gain_grad, router_grad)


def solution(mesh):
    ep, sp = mesh.devices.shape
    grid = Mesh(mesh.devices.reshape(ep, sp // 2, 2), ("ep", "y", "core"))
    shared = ("y", "core")
    rows = ("ep", "y", "core")
    return jax.shard_map(
        body,
        mesh=grid,
        in_specs=(
            P(rows, None),
            P(rows, None),
            P(),
            P(),
            P(None, shared),
            P(None, shared),
            P(shared, None),
            P("ep", None, shared),
            P("ep", None, shared),
            P("ep", shared, None),
            P(rows, None),
        ),
        out_specs=(P(rows, None), P(), P()),
        check_vma=False,
    )
```

time: 578 us -> 497 us (0.86)
  starting transfers between devices: 138 us -> 95.9 us
  waiting for transfers between devices: 223 us -> 192 us
  other arithmetic: 26.8 us -> 43.4 us
  matrix products: 141 us -> 125 us
  local copies, waits for them, and re-layouts: 40.4 us -> 32.6 us
    all_to_all x5, waiting for transfers between devices: 136 us -> 40.3 us  [over_ep(): return lax.all_to_all(value, 'ep', split_axis=0, concat_axis=0, tiled=True)]
    ppermute x8 -> x9, waiting for transfers between devices: 21.1 us -> 82.8 us  [receive_from(): lax.ppermute(value, 'y', [(i, (i - k) % PEERS) for i in range(PEERS)])]
    ppermute x6 -> x7, starting transfers between devices: 44.3 us -> 7.84 us  [swap(): return lax.ppermute(value, 'core', [(0, 1), (1, 0)])]
    all_to_all x2 -> x0, starting transfers between devices: 21.7 us -> none  [the longest x1 12.2 us: body(): lax.all_to_all(jnp.broadcast_to(mine, (devices, mine.shape[1])), axes, 0,...]
    all_to_all x1, starting transfers between devices: 11.1 us -> 22 us  [body(): lax.all_to_all(jnp.broadcast_to(local_gain[None], (devices, width)), axes...]
    ppermute x0 -> x6, waiting for transfers between devices: none -> 9.66 us  [over_all(): parts.append(lax.ppermute(value, 'ep', pairs))]
    concatenate x3, other arithmetic: 9.85 us -> 18.9 us  [the longest x1 18.9 us: body(): dense_rows = jnp.concatenate([pair, peer1, peer2, peer3], 0)]
    dot_general x7 -> x9, matrix products: 30.6 us -> 23.2 us  [the longest x2 9.51 us: pick(): lax.dot_general(table, rows, (((0,), (0,)), ((), ())), preferred_element_...]
  transfers between devices with their start and end apart: 30 -> 36, of which waited for: 9 -> 12; matrix products, arithmetic and copies ran while one was open for 32% -> 40% of each run, Pallas kernels for 0% -> 0%
where the time goes in v2:
time: 497 us; the launch traced here: 490 us
  waiting for transfers between devices  192 us (39%)
  matrix products  125 us (25%)
  starting transfers between devices  95.9 us (19%)
  other arithmetic  43.4 us (9%)
  local copies, waits for them, and re-layouts  32.6 us (7%)
    ppermute x9, waiting for transfers between devices, receive_from(): lax.ppermute(value, 'y', [(i, (i - k) % PEERS) for i in range(PEERS)])  82.8 us
    all_to_all x5, waiting for transfers between devices, over_ep(): return lax.all_to_all(value, 'ep', split_axis=0, concat_axis=0, tiled=True)  40.3 us
    dot_general x5, matrix products, hidden_grads(): both = jnp.dot(rows[:, :width], wide, preferred_element_type=F32)  38 us
    all_to_all x5, starting transfers between devices, over_ep(): return lax.all_to_all(value, 'ep', split_axis=0, concat_axis=0, tiled=True)  37.3 us
    ppermute x8, waiting for transfers between devices, send_to(): lax.ppermute(value, 'y', [(i, (i + k) % PEERS) for i in range(PEERS)])  36.6 us
    dot_general x5, matrix products, hidden_grads(): lax.dot_general(grads, wide, (((1,), (1,)), ((), ())), preferred_element_...  36.2 us
    dot_general x5, matrix products, hidden_grads(): lax.dot_general(rows[:, width:], tall, (((1,), (1,)), ((), ())), preferre...  26.8 us
    unnamed x53, local copies, waits for them, and re-layouts  23.8 us
  transfers between devices with their start and end apart: 36, of which 12 were waited for; matrix products, arithmetic and copies ran while one was open for 40% of the time, Pallas kernels for 0%

profile of v2, /device:TPU:1, one launch (start us, length us, event | category | flops | bytes accessed | tf_op | source)
XLA Modules:
  0.0 490.0 jit_solution(3004022100742520397)
XLA Ops:
  11.2 4.0 convolution_convert_fusion.1
  15.2 7.7 %all-to-all-start = ((bf16[16,24,7168]{2,1,0:T(8,128)(2,1)}), bf16[16,24,7168]{2,1,0:T(8,128)(2,1)}, u32[]{:S(2)}, u32[]{:S(2)}) async-start(bf16[16,24,7168]{2,1,0:T(8,128)(2,1)} %bitcast.59), calls=%async_computation | async-start | bytes 11010048 | tf_op jit(solution)/shard_map/all_to_all | solution.py:26
  22.9 3.3 constant_dynamic-update-slice_fusion.3
  27.7 22.0 %collective-permute-done.3 = s32[128,2]{0,1:T(2,128)S(1)} collective-permute-done((s32[128,2]{0,1:T(2,128)S(1)}, s32[128,2]{0,1:T(2,128)S(1)}, u32[]{:S(2)}, u32[]{:S(2)}) %collective-permute-start.3) | collective-permute-done | bytes 1056 | tf_op jit(solution)/shard_map/ppermute | solution.py:14
  51.9 5.5 %convolution_convert_fusion = bf16[384,7168]{1,0:T(8,128)(2,1)} fusion(bf16[128,384]{1,0:T(8,128)(2,1)S(1)} %fusion.65, bf16[128,7168]{1,0:T(8,128)(2,1)} %collective-permute-done), kind=kOutput, calls=%fused_computation | convolution fusion | flops 707395584 | bytes 7438336 | tf_op jit(solution)/shard_map/dot_general | solution.py:92
  57.9 3.4 constant_dynamic-update-slice_fusion.6
  64.8 3.1 constant_dynamic-update-slice_fusion.4
  70.2 3.1 constant_dynamic-update-slice_fusion.2
  74.1 3.1 constant_dynamic-update-slice_fusion.1
  77.2 3.2 constant_dynamic-update-slice_fusion
  81.1 25.6 %collective-permute-done.2 = bf16[128,7168]{1,0:T(8,128)(2,1)S(1)} collective-permute-done((bf16[128,7168]{1,0:T(8,128)(2,1)}, bf16[128,7168]{1,0:T(8,128)(2,1)S(1)}, u32[]{:S(2)}, u32[]{:S(2)}) %collective-permute-start.2) | collective-permute-done | bytes 1835040 | tf_op jit(solution)/shard_map/ppermute | solution.py:14
  106.7 3.6 collective-permute-done.1
  110.3 18.9 %pad_maximum_fusion = bf16[512,7168]{1,0:T(8,128)(2,1)} fusion(bf16[128,7168]{1,0:T(8,128)(2,1)S(1)} %collective-permute-done.2, bf16[128,7168]{1,0:T(8,128)(2,1)} %collective-permute-done, bf16[128,7168]{1,0:T(8,128)(2,1)S(1)} %collective-permute-done.1, bf16[128,3584]{1,0:T(8,128)(2,1)S(1)} %copy-done.1, bf16[128,3584]{1,0:T(8,128)(2,1)S(1)} %fusion.27), kind=kLoop, calls=%fused_computation.2 | loop fusion | flops 36700160 | bytes 14680064 | tf_op jit(solution)/shard_map/concatenate | solution.py:150
  129.3 7.8 %all-to-all-start.1 = ((bf16[16,24,7168]{2,1,0:T(8,128)(2,1)}), bf16[16,24,7168]{2,1,0:T(8,128)(2,1)}, u32[]{:S(2)}, u32[]{:S(2)}) async-start(bf16[16,24,7168]{2,1,0:T(8,128)(2,1)} %bitcast.58), calls=%async_computation.1 | async-start | bytes 11010048 | tf_op jit(solution)/shard_map/all_to_all | solution.py:26
  139.9 8.3 %fusion.20 = f32[384,1280]{1,0:T(8,128)S(1)} fusion(bf16[3584,1280]{0,1:T(8,128)(2,1)} %broadcast_dynamic-update-slice_fusion.3, bf16[384,7168]{1,0:T(8,128)(2,1)} %bitcast.1), kind=kOutput, calls=%fused_computation.32 | convolution fusion | flops 3523215360 | bytes 13893632 | tf_op jit(solution)/shard_map/dot_general | solution.py:41
  148.3 5.3 %multiply_reduce_fusion.3 = (f32[384]{0:T(512)S(1)}, bf16[384,640]{1,0:T(8,128)(2,1)S(1)}, bf16[384,640]{1,0:T(8,128)(2,1)S(1)}) fusion(f32[384,1280]{1,0:T(8,128)S(1)} %fusion.20, bf16[304,3584]{1,0:T(8,128)(2,1)} %collective-permute-done.4, bf16[304,3584]{1,0:T(8,128)(2,1)S(1)} %bitcast.73, bf16[640]{0:T(1024)(128)(2,1)S(1)} %pad.23.clone, ...), kind=kOutput, calls=%fused_computation.93 | convolution fusion | flops 1779056256 | bytes 10062592 | tf_op jit(solution)/shard_map/dot_general | solution.py:42
  153.6 9.6 %fusion.46 = f32[384,3584]{1,0:T(8,128)} fusion(bf16[3584,1280]{0,1:T(8,128)(2,1)} %broadcast_dynamic-update-slice_fusion.3, bf16[384,640]{1,0:T(8,128)(2,1)S(1)} %get-tuple-element.32, bf16[384,640]{1,0:T(8,128)(2,1)S(1)} %get-tuple-element.31), kind=kOutput, calls=%fused_computation.67 | convolution fusion | flops 3525181440 | bytes 15663104 | tf_op jit(solution)/shard_map/dot_general | solution.py:52
  163.1 7.5 %fusion.5 = f32[512,1280]{1,0:T(8,128)S(1)} fusion(bf16[3584,1280]{0,1:T(8,128)(2,1)} %broadcast_dynamic-update-slice_fusion.2, bf16[512,7168]{1,0:T(8,128)(2,1)S(1)} %bitcast.62), kind=kOutput, calls=%fused_computation.13 | convolution fusion | flops 4697620480 | bytes 15466496 | tf_op jit(solution)/shard_map/dot_general | solution.py:41
  170.7 5.7 %fusion.39 = (bf16[512,640]{1,0:T(8,128)(2,1)S(1)}, bf16[512,640]{1,0:T(8,128)(2,1)S(1)}) fusion(f32[512,1280]{1,0:T(8,128)S(1)} %fusion.5, bf16[304,3584]{1,0:T(8,128)(2,1)} %collective-permute-done.7, bf16[304,3584]{1,0:T(8,128)(2,1)} %param.17, bf16[640]{0:T(1024)(128)(2,1)S(1)} %pad.23.clone, bf16[512,7168]{1,0:T(8,128)(2,1)S(1)} %bitcast.62), kind=kOutput, calls=%fused_computation.56 | convolution fusion | flops 2366832640 | bytes 11962368 | tf_op jit(solution)/shard_map/dot_general | solution.py:42
  176.4 11.3 %fusion.95 = (bf16[512,3584]{1,0:T(8,128)(2,1)}, f32[512,3584]{1,0:T(8,128)}) fusion(bf16[3584,1280]{0,1:T(8,128)(2,1)} %broadcast_dynamic-update-slice_fusion.2, bf16[512,640]{1,0:T(8,128)(2,1)S(1)} %get-tuple-element.27, bf16[512,640]{1,0:T(8,128)(2,1)S(1)} %get-tuple-element.26), kind=kOutput, calls=%fused_computation.171 | convolution fusion | flops 4702076928 | bytes 21495808 | tf_op jit(solution)/shard_map/dot_general | solution.py:52
  187.7 34.0 %all-to-all-done.1 = bf16[16,24,7168]{2,1,0:T(8,128)(2,1)} async-done(((bf16[16,24,7168]{2,1,0:T(8,128)(2,1)}), bf16[16,24,7168]{2,1,0:T(8,128)(2,1)}, u32[]{:S(2)}, u32[]{:S(2)}) %all-to-all-start.1) | async-done | bytes 5505056 | tf_op jit(solution)/shard_map/all_to_all | solution.py:26
  221.7 8.3 %fusion.16 = f32[384,1280]{1,0:T(8,128)S(1)} fusion(bf16[3584,1280]{0,1:T(8,128)(2,1)} %broadcast_dynamic-update-slice_fusion.3, bf16[384,7168]{1,0:T(8,128)(2,1)} %bitcast.7), kind=kOutput, calls=%fused_computation.28 | convolution fusion | flops 3523215360 | bytes 13893632 | tf_op jit(solution)/shard_map/dot_general | solution.py:41
  230.1 5.3 %multiply_reduce_fusion.1 = (f32[384]{0:T(512)S(1)}, bf16[384,640]{1,0:T(8,128)(2,1)S(1)}, bf16[384,640]{1,0:T(8,128)(2,1)S(1)}) fusion(f32[384,1280]{1,0:T(8,128)S(1)} %fusion.16, bf16[304,3584]{1,0:T(8,128)(2,1)} %collective-permute-done.4, bf16[304,3584]{1,0:T(8,128)(2,1)S(1)} %bitcast.74, bf16[640]{0:T(1024)(128)(2,1)S(1)} %pad.23.clone, ...), kind=kOutput, calls=%fused_computation.86 | convolution fusion | flops 1779056256 | bytes 10062592 | tf_op jit(solution)/shard_map/dot_general | solution.py:42
  235.4 5.1 %convolution_convert_fusion.3 = bf16[384,3584]{1,0:T(8,128)(2,1)} fusion(bf16[3584,1280]{0,1:T(8,128)(2,1)S(1)} %bitcast.65, bf16[384,640]{1,0:T(8,128)(2,1)S(1)} %get-tuple-element.38, bf16[384,640]{1,0:T(8,128)(2,1)S(1)} %get-tuple-element.37), kind=kOutput, calls=%fused_computation.4 | convolution fusion | flops 3526557696 | bytes 12910592 | tf_op jit(solution)/shard_map/dot_general | solution.py:52
  240.6 9.2 %all-to-all-start.2 = ((bf16[16,24,3584]{2,1,0:T(8,128)(2,1)}), bf16[16,24,3584]{2,1,0:T(8,128)(2,1)}, u32[]{:S(2)}, u32[]{:S(2)}) async-start(bf16[16,24,3584]{2,1,0:T(8,128)(2,1)} %bitcast.63), calls=%async_computation.2 | async-start | bytes 5505024 | tf_op jit(solution)/shard_map/all_to_all | solution.py:26
  249.8 7.5 %collective-permute-done.10 = bf16[384,7168]{1,0:T(8,128)(2,1)} collective-permute-done((bf16[384,7168]{1,0:T(8,128)(2,1)}, bf16[384,7168]{1,0:T(8,128)(2,1)}, u32[]{:S(2)}, u32[]{:S(2)}) %collective-permute-start.10) | collective-permute-done | bytes 5505056 | tf_op jit(solution)/shard_map/ppermute | solution.py:14
  257.3 8.3 %fusion.12 = f32[384,1280]{1,0:T(8,128)S(1)} fusion(bf16[3584,1280]{0,1:T(8,128)(2,1)} %broadcast_dynamic-update-slice_fusion.3, bf16[384,7168]{1,0:T(8,128)(2,1)} %collective-permute-done.10), kind=kOutput, calls=%fused_computation.24 | convolution fusion | flops 3523215360 | bytes 13893632 | tf_op jit(solution)/shard_map/dot_general | solution.py:41
  265.6 5.2 %multiply_reduce_fusion.2 = (f32[384]{0:T(512)S(1)}, bf16[384,640]{1,0:T(8,128)(2,1)S(1)}, bf16[384,640]{1,0:T(8,128)(2,1)S(1)}) fusion(f32[384,1280]{1,0:T(8,128)S(1)} %fusion.12, bf16[304,3584]{1,0:T(8,128)(2,1)} %collective-permute-done.4, bf16[304,3584]{1,0:T(8,128)(2,1)S(1)} %bitcast.75, bf16[640]{0:T(1024)(128)(2,1)S(1)} %pad.23.clone, ...), kind=kOutput, calls=%fused_computation.87 | convolution fusion | flops 1779056256 | bytes 10062592 | tf_op jit(solution)/shard_map/dot_general | solution.py:42
  270.9 5.1 %fusion.53 = bf16[384,3584]{1,0:T(8,128)(2,1)} fusion(bf16[3584,1280]{0,1:T(8,128)(2,1)S(1)} %bitcast.67, bf16[384,640]{1,0:T(8,128)(2,1)S(1)} %get-tuple-element.35, bf16[384,640]{1,0:T(8,128)(2,1)S(1)} %get-tuple-element.34), kind=kOutput, calls=%fused_computation.74 | convolution fusion | flops 3525181440 | bytes 12910592 | tf_op jit(solution)/shard_map/dot_general | solution.py:52
  277.2 5.5 %fusion.8 = f32[384,1280]{1,0:T(8,128)S(1)} fusion(bf16[3584,1280]{0,1:T(8,128)(2,1)S(1)} %bitcast.67, bf16[384,7168]{1,0:T(8,128)(2,1)} %collective-permute-done.11), kind=kOutput, calls=%fused_computation.20 | convolution fusion | flops 3523215360 | bytes 13893632 | tf_op jit(solution)/shard_map/dot_general | solution.py:41
  282.8 5.2 %multiply_reduce_fusion = (f32[384]{0:T(512)S(1)}, bf16[384,640]{1,0:T(8,128)(2,1)S(1)}, bf16[384,640]{1,0:T(8,128)(2,1)S(1)}) fusion(f32[384,1280]{1,0:T(8,128)S(1)} %fusion.8, bf16[304,3584]{1,0:T(8,128)(2,1)} %collective-permute-done.4, bf16[304,3584]{1,0:T(8,128)(2,1)S(1)} %bitcast.76, bf16[640]{0:T(1024)(128)(2,1)S(1)} %pad.23.clone, ...), kind=kOutput, calls=%fused_computation.82 | convolution fusion | flops 1779056256 | bytes 10062592 | tf_op jit(solution)/shard_map/dot_general | solution.py:42
  287.9 5.1 %convolution_convert_fusion.2 = bf16[384,3584]{1,0:T(8,128)(2,1)} fusion(bf16[3584,1280]{0,1:T(8,128)(2,1)S(1)} %bitcast.67, bf16[384,640]{1,0:T(8,128)(2,1)S(1)} %get-tuple-element.41, bf16[384,640]{1,0:T(8,128)(2,1)S(1)} %get-tuple-element.40), kind=kOutput, calls=%fused_computation.3 | convolution fusion | flops 3526557696 | bytes 12910592 | tf_op jit(solution)/shard_map/dot_general | solution.py:52
  299.0 6.3 %all-to-all-start.3 = ((f32[16,1,96]{2,1,0:T(1,128)}), f32[16,1,96]{2,1,0:T(1,128)S(1)}, u32[]{:S(2)}, u32[]{:S(2)}) async-start(f32[16,1,96]{2,1,0:T(1,128)} %bitcast.12), calls=%async_computation.3 | async-start | bytes 16384 | tf_op jit(solution)/shard_map/all_to_all | solution.py:26
  305.3 6.3 %all-to-all-done.3 = f32[16,1,96]{2,1,0:T(1,128)S(1)} async-done(((f32[16,1,96]{2,1,0:T(1,128)}), f32[16,1,96]{2,1,0:T(1,128)S(1)}, u32[]{:S(2)}, u32[]{:S(2)}) %all-to-all-start.3) | async-done | bytes 6176 | tf_op jit(solution)/shard_map/all_to_all | solution.py:26
  315.3 36.6 %collective-permute-done.14 = f32[16,24]{1,0:T(8,128)S(1)} collective-permute-done((f32[16,24]{1,0:T(8,128)S(1)}, f32[16,24]{1,0:T(8,128)S(1)}, u32[]{:S(2)}, u32[]{:S(2)}) %collective-permute-start.14) | collective-permute-done | bytes 1568 | tf_op jit(solution)/shard_map/ppermute | solution.py:18
  352.7 3.8 collective-permute-start.20
  356.5 6.8 %add_convert_fusion = bf16[384,3584]{1,0:T(8,128)(2,1)} fusion(bf16[384,3584]{1,0:T(8,128)(2,1)} %collective-permute-done.16, f32[384,3584]{1,0:T(8,128)} %fusion.46, bf16[384,3584]{1,0:T(8,128)(2,1)} %collective-permute-done.15), kind=kLoop, calls=%fused_computation.5 | loop fusion | flops 6881280 | bytes 13762560 | tf_op jit(solution)/shard_map/convert_element_type | solution.py:167
  363.3 6.3 %all-to-all-start.4 = ((bf16[16,24,3584]{2,1,0:T(8,128)(2,1)}), bf16[16,24,3584]{2,1,0:T(8,128)(2,1)}, u32[]{:S(2)}, u32[]{:S(2)}) async-start(bf16[16,24,3584]{2,1,0:T(8,128)(2,1)} %bitcast.60), calls=%async_computation.4 | async-start | bytes 5505024 | tf_op jit(solution)/shard_map/all_to_all | solution.py:26
  372.1 3.2 collective-permute-start.18
  379.7 3.9 fusion.37
  383.6 18.0 %collective-permute-done.22 = f32[16,3584]{1,0:T(8,128)S(1)} collective-permute-done((f32[16,3584]{1,0:T(8,128)S(1)}, f32[16,3584]{1,0:T(8,128)S(1)}, u32[]{:S(2)}, u32[]{:S(2)}) %collective-permute-start.22) | collective-permute-done | bytes 229408 | tf_op jit(solution)/shard_map/ppermute | solution.py:14
  401.6 6.1 %collective-permute-done.23 = f32[16,3584]{1,0:T(8,128)S(1)} collective-permute-done((f32[16,3584]{1,0:T(8,128)S(1)}, f32[16,3584]{1,0:T(8,128)S(1)}, u32[]{:S(2)}, u32[]{:S(2)}) %collective-permute-start.23) | collective-permute-done | bytes 229408 | tf_op jit(solution)/shard_map/ppermute | solution.py:14
  416.9 7.0 %collective-permute-done.24 = f32[16,3584]{1,0:T(8,128)S(1)} collective-permute-done((f32[16,3584]{1,0:T(8,128)S(1)}, f32[16,3584]{1,0:T(8,128)S(1)}, u32[]{:S(2)}, u32[]{:S(2)}) %collective-permute-start.24) | collective-permute-done | bytes 229408 | tf_op jit(solution)/shard_map/ppermute | solution.py:72
  426.8 3.6 convolution_add_fusion
  431.3 3.7 fusion.36
  437.2 22.0 %all-to-all-start.5 = ((f32[128,1,3584]{2,1,0:T(1,128)}), f32[128,1,3584]{2,1,0:T(1,128)}, u32[]{:S(2)}, u32[]{:S(2)}) async-start(f32[128,1,3584]{2,1,0:T(1,128)} %broadcast_in_dim.75), calls=%async_computation.5 | async-start | bytes 3670016 | tf_op jit(solution)/shard_map/all_to_all | solution.py:197
  464.1 22.3 %all-to-all-done.5 = f32[128,1,3584]{2,1,0:T(1,128)} async-done(((f32[128,1,3584]{2,1,0:T(1,128)}), f32[128,1,3584]{2,1,0:T(1,128)}, u32[]{:S(2)}, u32[]{:S(2)}) %all-to-all-start.5) | async-done | bytes 1835040 | tf_op jit(solution)/shard_map/all_to_all | solution.py:197
  486.4 3.1 reduce_sum.175
  (160 shorter events, 63.3 us)
Async XLA Ops:
  0.6 294.3 %copy-start = (f32[3584,16]{0,1:T(8,128)S(1)}, f32[3584,16]{0,1:T(8,128)}, u32[]{:S(2)}) copy-start(f32[3584,16]{0,1:T(8,128)} %param.14) | copy-start | bytes 688132
  0.7 56.7 %collective-permute-start.8 = (bf16[3584,304]{0,1:T(8,128)(2,1)}, bf16[3584,304]{0,1:T(8,128)(2,1)}, u32[]{:S(2)}, u32[]{:S(2)}) collective-permute-start(bf16[3584,304]{0,1:T(8,128)(2,1)} %param.15), channel_id=1, source_target_pairs={{0,1},{1,0},{2,3},{3,2},{4,5},{5,4},{6,7},{7,6},{8,9},{9,8},{10,11... | collective-permute-start | bytes 6537224 | tf_op jit(solution)/shard_map/ppermute | solution.py:22
  2.2 61.3 %collective-permute-start.9 = (bf16[3584,304]{0,1:T(8,128)(2,1)}, bf16[3584,304]{0,1:T(8,128)(2,1)}, u32[]{:S(2)}, u32[]{:S(2)}) collective-permute-start(bf16[3584,304]{0,1:T(8,128)(2,1)} %param.16), channel_id=1, source_target_pairs={{0,1},{1,0},{2,3},{3,2},{4,5},{5,4},{6,7},{7,6},{8,9},{9,8},{10,11... | collective-permute-start | bytes 6537224 | tf_op jit(solution)/shard_map/ppermute | solution.py:22
  3.7 6.6 %copy-start.6 = (s32[128,2]{0,1:T(2,128)S(1)}, s32[128,2]{0,1:T(2,128)}, u32[]{:S(2)}) copy-start(s32[128,2]{0,1:T(2,128)} %param.21) | copy-start | bytes 3076
  6.6 45.1 %collective-permute-start = (bf16[128,7168]{1,0:T(8,128)(2,1)}, bf16[128,7168]{1,0:T(8,128)(2,1)}, u32[]{:S(2)}, u32[]{:S(2)}) collective-permute-start(bf16[128,7168]{1,0:T(8,128)(2,1)} %pad_maximum_fusion.1), channel_id=1, source_target_pairs={{0,4},{2,6},{4,0},{6,2},{1,5},{3,7},{5,1},{7,3},{8,12},{10,14},{12... | collective-permute-start | bytes 5505032 | tf_op jit(solution)/shard_map/ppermute | solution.py:14
  9.6 59.0 %collective-permute-start.5 = (bf16[3584,304]{0,1:T(8,128)(2,1)}, bf16[3584,304]{0,1:T(8,128)(2,1)}, u32[]{:S(2)}, u32[]{:S(2)}) collective-permute-start(bf16[3584,304]{0,1:T(8,128)(2,1)} %bitcast.3), channel_id=1, source_target_pairs={{0,1},{1,0},{2,3},{3,2},{4,5},{5,4},{6,7},{7,6},{8,9},{9,8},{10,11... | collective-permute-start | bytes 6537224 | tf_op jit(solution)/shard_map/ppermute | solution.py:22
  10.3 39.4 %collective-permute-start.3 = (s32[128,2]{0,1:T(2,128)S(1)}, s32[128,2]{0,1:T(2,128)S(1)}, u32[]{:S(2)}, u32[]{:S(2)}) collective-permute-start(s32[128,2]{0,1:T(2,128)S(1)} %copy-done.6), channel_id=1, source_target_pairs={{0,4},{2,6},{4,0},{6,2},{1,5},{3,7},{5,1},{7,3},{8,12},{10,14},{12... | collective-permute-start | bytes 3080 | tf_op jit(solution)/shard_map/ppermute | solution.py:14
  15.2 114.1 %all-to-all-start = ((bf16[16,24,7168]{2,1,0:T(8,128)(2,1)}), bf16[16,24,7168]{2,1,0:T(8,128)(2,1)}, u32[]{:S(2)}, u32[]{:S(2)}) async-start(bf16[16,24,7168]{2,1,0:T(8,128)(2,1)} %bitcast.59), calls=%async_computation | async-start | bytes 11010048 | tf_op jit(solution)/shard_map/all_to_all | solution.py:26
  49.7 27.5 %collective-permute-start.6 = (bf16[3584,304]{0,1:T(8,128)(2,1)}, bf16[3584,304]{0,1:T(8,128)(2,1)}, u32[]{:S(2)}, u32[]{:S(2)}) collective-permute-start(bf16[3584,304]{0,1:T(8,128)(2,1)} %bitcast.4), channel_id=1, source_target_pairs={{0,1},{1,0},{2,3},{3,2},{4,5},{5,4},{6,7},{7,6},{8,9},{9,8},{10,11... | collective-permute-start | bytes 6537224 | tf_op jit(solution)/shard_map/ppermute | solution.py:22
  51.8 96.5 %collective-permute-start.4 = (bf16[304,3584]{1,0:T(8,128)(2,1)}, bf16[304,3584]{1,0:T(8,128)(2,1)}, u32[]{:S(2)}, u32[]{:S(2)}) collective-permute-start(bf16[304,3584]{1,0:T(8,128)(2,1)} %bitcast.72), channel_id=1, source_target_pairs={{0,1},{1,0},{2,3},{3,2},{4,5},{5,4},{6,7},{7,6},{8,9},{9,8},{10,11... | collective-permute-start | bytes 6537224 | tf_op jit(solution)/shard_map/ppermute | solution.py:22
  57.4 113.3 %collective-permute-start.7 = (bf16[304,3584]{1,0:T(8,128)(2,1)}, bf16[304,3584]{1,0:T(8,128)(2,1)}, u32[]{:S(2)}, u32[]{:S(2)}) collective-permute-start(bf16[304,3584]{1,0:T(8,128)(2,1)} %param.17), channel_id=1, source_target_pairs={{0,1},{1,0},{2,3},{3,2},{4,5},{5,4},{6,7},{7,6},{8,9},{9,8},{10,11... | collective-permute-start | bytes 6537224 | tf_op jit(solution)/shard_map/ppermute | solution.py:22
  63.4 43.3 %collective-permute-start.2 = (bf16[128,7168]{1,0:T(8,128)(2,1)}, bf16[128,7168]{1,0:T(8,128)(2,1)S(1)}, u32[]{:S(2)}, u32[]{:S(2)}) collective-permute-start(bf16[128,7168]{1,0:T(8,128)(2,1)} %pad_maximum_fusion.1), channel_id=1, source_target_pairs={{0,2},{2,4},{4,6},{6,0},{1,3},{3,5},{5,7},{7,1},{8,10},{10,12},{12... | collective-permute-start | bytes 5505032 | tf_op jit(solution)/shard_map/ppermute | solution.py:14
  68.6 41.7 %collective-permute-start.1 = (bf16[128,7168]{1,0:T(8,128)(2,1)}, bf16[128,7168]{1,0:T(8,128)(2,1)S(1)}, u32[]{:S(2)}, u32[]{:S(2)}) collective-permute-start(bf16[128,7168]{1,0:T(8,128)(2,1)} %pad_maximum_fusion.1), channel_id=1, source_target_pairs={{0,6},{2,0},{4,2},{6,4},{1,7},{3,1},{5,3},{7,5},{8,14},{10,8},{12,... | collective-permute-start | bytes 5505032 | tf_op jit(solution)/shard_map/ppermute | solution.py:14
  129.3 92.5 %all-to-all-start.1 = ((bf16[16,24,7168]{2,1,0:T(8,128)(2,1)}), bf16[16,24,7168]{2,1,0:T(8,128)(2,1)}, u32[]{:S(2)}, u32[]{:S(2)}) async-start(bf16[16,24,7168]{2,1,0:T(8,128)(2,1)} %bitcast.58), calls=%async_computation.1 | async-start | bytes 11010048 | tf_op jit(solution)/shard_map/all_to_all | solution.py:26
  137.0 11.2 %copy-start.10 = (bf16[1,304,3584]{2,1,0:T(8,128)(2,1)S(1)}, bf16[1,304,3584]{2,1,0:T(8,128)(2,1)}, u32[]{:S(2)}) copy-start(bf16[1,304,3584]{2,1,0:T(8,128)(2,1)} %param.20) | copy-start | bytes 6537220
  137.0 140.2 %collective-permute-start.11 = (bf16[384,7168]{1,0:T(8,128)(2,1)}, bf16[384,7168]{1,0:T(8,128)(2,1)}, u32[]{:S(2)}, u32[]{:S(2)}) collective-permute-start(bf16[384,7168]{1,0:T(8,128)(2,1)} %bitcast.1), channel_id=1, source_target_pairs={{0,2},{2,4},{4,6},{6,0},{1,3},{3,5},{5,7},{7,1},{8,10},{10,12},{12... | collective-permute-start | bytes 16515080 | tf_op jit(solution)/shard_map/ppermute | solution.py:14
  138.4 118.9 %collective-permute-start.10 = (bf16[384,7168]{1,0:T(8,128)(2,1)}, bf16[384,7168]{1,0:T(8,128)(2,1)}, u32[]{:S(2)}, u32[]{:S(2)}) collective-permute-start(bf16[384,7168]{1,0:T(8,128)(2,1)} %bitcast.1), channel_id=1, source_target_pairs={{0,6},{2,0},{4,2},{6,4},{1,7},{3,1},{5,3},{7,5},{8,14},{10,8},{12,... | collective-permute-start | bytes 16515080 | tf_op jit(solution)/shard_map/ppermute | solution.py:14
  139.9 23.2 %slice-start = ((s8[7340032]{0:T(1024)(128)(4,1)}), s8[4194304]{0:T(1024)(128)(4,1)S(1)}, s32[]{:S(2)}) async-start(s8[7340032]{0:T(1024)(128)(4,1)} %bitcast.61), calls=%async_computation.6 | async-start | bytes 8388608
  148.2 14.9 %slice-start.1 = ((s8[7340032]{0:T(1024)(128)(4,1)}), s8[3145728]{0:T(1024)(128)(4,1)S(1)}, s32[]{:S(2)}) async-start(s8[7340032]{0:T(1024)(128)(4,1)} %bitcast.61), calls=%async_computation.7 | async-start | bytes 6291456
  221.7 8.3 %copy-start.11 = (bf16[1,304,3584]{2,1,0:T(8,128)(2,1)S(1)}, bf16[1,304,3584]{2,1,0:T(8,128)(2,1)}, u32[]{:S(2)}) copy-start(bf16[1,304,3584]{2,1,0:T(8,128)(2,1)} %param.20) | copy-start | bytes 6537220
  221.7 13.7 %slice-start.2 = ((s8[9175040]{0:T(1024)(128)(4,1)}), s8[786432]{0:T(1024)(128)(4,1)S(1)}, s32[]{:S(2)}) async-start(s8[9175040]{0:T(1024)(128)(4,1)} %bitcast.64), calls=%async_computation.8 | async-start | bytes 1572864
  221.7 13.7 %slice-start.3 = ((s8[9175040]{0:T(1024)(128)(4,1)}), s8[4194304]{0:T(1024)(128)(4,1)S(1)}, s32[]{:S(2)}) async-start(s8[9175040]{0:T(1024)(128)(4,1)} %bitcast.64), calls=%async_computation.9 | async-start | bytes 8388608
  240.6 58.4 %all-to-all-start.2 = ((bf16[16,24,3584]{2,1,0:T(8,128)(2,1)}), bf16[16,24,3584]{2,1,0:T(8,128)(2,1)}, u32[]{:S(2)}, u32[]{:S(2)}) async-start(bf16[16,24,3584]{2,1,0:T(8,128)(2,1)} %bitcast.63), calls=%async_computation.2 | async-start | bytes 5505024 | tf_op jit(solution)/shard_map/all_to_all | solution.py:26
  249.8 15.9 %copy-start.12 = (bf16[1,304,3584]{2,1,0:T(8,128)(2,1)S(1)}, bf16[1,304,3584]{2,1,0:T(8,128)(2,1)}, u32[]{:S(2)}) copy-start(bf16[1,304,3584]{2,1,0:T(8,128)(2,1)} %param.20) | copy-start | bytes 6537220
  257.3 13.6 %slice-start.5 = ((s8[9175040]{0:T(1024)(128)(4,1)}), s8[4194304]{0:T(1024)(128)(4,1)S(1)}, s32[]{:S(2)}) async-start(s8[9175040]{0:T(1024)(128)(4,1)} %bitcast.66), calls=%async_computation.11 | async-start | bytes 8388608
  257.3 13.6 %slice-start.6 = ((s8[9175040]{0:T(1024)(128)(4,1)}), s8[4194304]{0:T(1024)(128)(4,1)S(1)}, s32[]{:S(2)}) async-start(s8[9175040]{0:T(1024)(128)(4,1)} %bitcast.66), calls=%async_computation.12 | async-start | bytes 8388608
  276.0 80.5 %collective-permute-start.15 = (bf16[384,3584]{1,0:T(8,128)(2,1)}, bf16[384,3584]{1,0:T(8,128)(2,1)}, u32[]{:S(2)}, u32[]{:S(2)}) collective-permute-start(bf16[384,3584]{1,0:T(8,128)(2,1)} %fusion.53), channel_id=1, source_target_pairs={{0,2},{2,4},{4,6},{6,0},{1,3},{3,5},{5,7},{7,1},{8,10},{10,12},{12... | collective-permute-start | bytes 8257544 | tf_op jit(solution)/shard_map/ppermute | solution.py:18
  293.0 63.5 %collective-permute-start.16 = (bf16[384,3584]{1,0:T(8,128)(2,1)}, bf16[384,3584]{1,0:T(8,128)(2,1)}, u32[]{:S(2)}, u32[]{:S(2)}) collective-permute-start(bf16[384,3584]{1,0:T(8,128)(2,1)} %convolution_convert_fusion.2), channel_id=1, source_target_pairs={{0,6},{2,0},{4,2},{6,4},{1,7},{3,1},{5,3},{7,5},{8,14},{10,8},{12,... | collective-permute-start | bytes 8257544 | tf_op jit(solution)/shard_map/ppermute | solution.py:18
  299.0 12.7 %all-to-all-start.3 = ((f32[16,1,96]{2,1,0:T(1,128)}), f32[16,1,96]{2,1,0:T(1,128)S(1)}, u32[]{:S(2)}, u32[]{:S(2)}) async-start(f32[16,1,96]{2,1,0:T(1,128)} %bitcast.12), calls=%async_computation.3 | async-start | bytes 16384 | tf_op jit(solution)/shard_map/all_to_all | solution.py:26
  312.9 39.0 %collective-permute-start.14 = (f32[16,24]{1,0:T(8,128)S(1)}, f32[16,24]{1,0:T(8,128)S(1)}, u32[]{:S(2)}, u32[]{:S(2)}) collective-permute-start(f32[16,24]{1,0:T(8,128)S(1)} %bitcast.71), channel_id=1, source_target_pairs={{0,6},{2,0},{4,2},{6,4},{1,7},{3,1},{5,3},{7,5},{8,14},{10,8},{12,... | collective-permute-start | bytes 4616 | tf_op jit(solution)/shard_map/ppermute | solution.py:18
  314.5 37.5 %collective-permute-start.13 = (f32[16,24]{1,0:T(8,128)S(1)}, f32[16,24]{1,0:T(8,128)S(1)}, u32[]{:S(2)}, u32[]{:S(2)}) collective-permute-start(f32[16,24]{1,0:T(8,128)S(1)} %bitcast.70), channel_id=1, source_target_pairs={{0,4},{2,6},{4,0},{6,2},{1,5},{3,7},{5,1},{7,3},{8,12},{10,14},{12... | collective-permute-start | bytes 4616 | tf_op jit(solution)/shard_map/ppermute | solution.py:18
  314.5 37.5 %collective-permute-start.12 = (f32[16,24]{1,0:T(8,128)S(1)}, f32[16,24]{1,0:T(8,128)S(1)}, u32[]{:S(2)}, u32[]{:S(2)}) collective-permute-start(f32[16,24]{1,0:T(8,128)S(1)} %bitcast.69), channel_id=1, source_target_pairs={{0,2},{2,4},{4,6},{6,0},{1,3},{3,5},{5,7},{7,1},{8,10},{10,12},{12... | collective-permute-start | bytes 4616 | tf_op jit(solution)/shard_map/ppermute | solution.py:18
  352.7 22.6 %collective-permute-start.20 = (f32[16,3584]{1,0:T(8,128)S(1)}, f32[16,3584]{1,0:T(8,128)S(1)}, u32[]{:S(2)}, u32[]{:S(2)}) collective-permute-start(f32[16,3584]{1,0:T(8,128)S(1)} %fusion.73), channel_id=1, source_target_pairs={{0,1},{1,0},{2,3},{3,2},{4,5},{5,4},{6,7},{7,6},{8,9},{9,8},{10,11... | collective-permute-start | bytes 688136 | tf_op jit(solution)/shard_map/ppermute | solution.py:22
  363.3 63.5 %all-to-all-start.4 = ((bf16[16,24,3584]{2,1,0:T(8,128)(2,1)}), bf16[16,24,3584]{2,1,0:T(8,128)(2,1)}, u32[]{:S(2)}, u32[]{:S(2)}) async-start(bf16[16,24,3584]{2,1,0:T(8,128)(2,1)} %bitcast.60), calls=%async_computation.4 | async-start | bytes 5505024 | tf_op jit(solution)/shard_map/all_to_all | solution.py:26
  372.1 58.3 %collective-permute-start.18 = (bf16[128,3584]{1,0:T(8,128)(2,1)}, bf16[128,3584]{1,0:T(8,128)(2,1)}, u32[]{:S(2)}, u32[]{:S(2)}) collective-permute-start(bf16[128,3584]{1,0:T(8,128)(2,1)} %get-tuple-element.29), channel_id=1, source_target_pairs={{0,6},{2,0},{4,2},{6,4},{1,7},{3,1},{5,3},{7,5},{8,14},{10,8},{12,... | collective-permute-start | bytes 2752520 | tf_op jit(solution)/shard_map/ppermute | solution.py:18
  375.3 56.0 %collective-permute-start.17 = (bf16[128,3584]{1,0:T(8,128)(2,1)S(1)}, bf16[128,3584]{1,0:T(8,128)(2,1)}, u32[]{:S(2)}, u32[]{:S(2)}) collective-permute-start(bf16[128,3584]{1,0:T(8,128)(2,1)S(1)} %get-tuple-element.28), channel_id=1, source_target_pairs={{0,2},{2,4},{4,6},{6,0},{1,3},{3,5},{5,7},{7,1},{8,10},{10,12},{12... | collective-permute-start | bytes 2752520 | tf_op jit(solution)/shard_map/ppermute | solution.py:18
  375.3 26.2 %collective-permute-start.22 = (f32[16,3584]{1,0:T(8,128)S(1)}, f32[16,3584]{1,0:T(8,128)S(1)}, u32[]{:S(2)}, u32[]{:S(2)}) collective-permute-start(f32[16,3584]{1,0:T(8,128)S(1)} %add.147), channel_id=1, source_target_pairs={{0,4},{2,6},{4,0},{6,2},{1,5},{3,7},{5,1},{7,3},{8,12},{10,14},{12... | collective-permute-start | bytes 688136 | tf_op jit(solution)/shard_map/ppermute | solution.py:14
  376.8 30.9 %collective-permute-start.23 = (f32[16,3584]{1,0:T(8,128)S(1)}, f32[16,3584]{1,0:T(8,128)S(1)}, u32[]{:S(2)}, u32[]{:S(2)}) collective-permute-start(f32[16,3584]{1,0:T(8,128)S(1)} %add.147), channel_id=1, source_target_pairs={{0,2},{2,4},{4,6},{6,0},{1,3},{3,5},{5,7},{7,1},{8,10},{10,12},{12... | collective-permute-start | bytes 688136 | tf_op jit(solution)/shard_map/ppermute | solution.py:14
  378.7 29.0 %collective-permute-start.21 = (f32[16,3584]{1,0:T(8,128)S(1)}, f32[16,3584]{1,0:T(8,128)S(1)}, u32[]{:S(2)}, u32[]{:S(2)}) collective-permute-start(f32[16,3584]{1,0:T(8,128)S(1)} %add.147), channel_id=1, source_target_pairs={{0,6},{2,0},{4,2},{6,4},{1,7},{3,1},{5,3},{7,5},{8,14},{10,8},{12,... | collective-permute-start | bytes 688136 | tf_op jit(solution)/shard_map/ppermute | solution.py:14
  407.7 6.5 %collective-permute-start.26 = (f32[16,3584]{1,0:T(8,128)S(1)}, f32[16,3584]{1,0:T(8,128)S(1)}, u32[]{:S(2)}, u32[]{:S(2)}) collective-permute-start(f32[16,3584]{1,0:T(8,128)S(1)} %add_add_fusion.1), channel_id=1, source_target_pairs={{0,24},{8,0},{16,8},{24,16},{32,56},{40,32},{48,40},{56,48},{64,88... | collective-permute-start | bytes 688136 | tf_op jit(solution)/shard_map/ppermute | solution.py:72
  410.1 6.7 %collective-permute-start.25 = (f32[16,3584]{1,0:T(8,128)S(1)}, f32[16,3584]{1,0:T(8,128)S(1)}, u32[]{:S(2)}, u32[]{:S(2)}) collective-permute-start(f32[16,3584]{1,0:T(8,128)S(1)} %add_add_fusion.1), channel_id=1, source_target_pairs={{0,16},{8,24},{16,0},{24,8},{32,48},{40,56},{48,32},{56,40},{64,80... | collective-permute-start | bytes 688136 | tf_op jit(solution)/shard_map/ppermute | solution.py:72
  410.6 13.3 %collective-permute-start.24 = (f32[16,3584]{1,0:T(8,128)S(1)}, f32[16,3584]{1,0:T(8,128)S(1)}, u32[]{:S(2)}, u32[]{:S(2)}) collective-permute-start(f32[16,3584]{1,0:T(8,128)S(1)} %add_add_fusion.1), channel_id=1, source_target_pairs={{0,8},{8,16},{16,24},{24,0},{32,40},{40,48},{48,56},{56,32},{64,72... | collective-permute-start | bytes 688136 | tf_op jit(solution)/shard_map/ppermute | solution.py:72
  414.3 17.0 %collective-permute-start.19 = (bf16[128,3584]{1,0:T(8,128)(2,1)}, bf16[128,3584]{1,0:T(8,128)(2,1)}, u32[]{:S(2)}, u32[]{:S(2)}) collective-permute-start(bf16[128,3584]{1,0:T(8,128)(2,1)} %fusion.37), channel_id=1, source_target_pairs={{0,4},{2,6},{4,0},{6,2},{1,5},{3,7},{5,1},{7,3},{8,12},{10,14},{12... | collective-permute-start | bytes 2752520 | tf_op jit(solution)/shard_map/ppermute | solution.py:18
  424.0 35.2 %collective-permute-start.29 = (f32[16,3584]{1,0:T(8,128)S(1)}, f32[16,3584]{1,0:T(8,128)S(1)}, u32[]{:S(2)}, u32[]{:S(2)}) collective-permute-start(f32[16,3584]{1,0:T(8,128)S(1)} %add_add_fusion), channel_id=1, source_target_pairs={{0,96},{8,104},{16,112},{24,120},{32,0},{40,8},{48,16},{56,24},{64... | collective-permute-start | bytes 688136 | tf_op jit(solution)/shard_map/ppermute | solution.py:72
  426.1 33.0 %collective-permute-start.28 = (f32[16,3584]{1,0:T(8,128)S(1)}, f32[16,3584]{1,0:T(8,128)}, u32[]{:S(2)}, u32[]{:S(2)}) collective-permute-start(f32[16,3584]{1,0:T(8,128)S(1)} %add_add_fusion), channel_id=1, source_target_pairs={{0,64},{8,72},{16,80},{24,88},{32,96},{40,104},{48,112},{56,120},{... | collective-permute-start | bytes 688136 | tf_op jit(solution)/shard_map/ppermute | solution.py:72
  430.4 28.8 %collective-permute-start.27 = (f32[16,3584]{1,0:T(8,128)S(1)}, f32[16,3584]{1,0:T(8,128)}, u32[]{:S(2)}, u32[]{:S(2)}) collective-permute-start(f32[16,3584]{1,0:T(8,128)S(1)} %add_add_fusion), channel_id=1, source_target_pairs={{0,32},{8,40},{16,48},{24,56},{32,64},{40,72},{48,80},{56,88},{64,... | collective-permute-start | bytes 688136 | tf_op jit(solution)/shard_map/ppermute | solution.py:72
  437.2 23.8 %copy-start.9 = (f32[128]{0:T(128)S(1)}, f32[128]{0:T(128)}, u32[]{:S(2)}) copy-start(f32[128]{0:T(128)} %copy-done.7) | copy-start | bytes 1540
  437.2 49.2 %all-to-all-start.5 = ((f32[128,1,3584]{2,1,0:T(1,128)}), f32[128,1,3584]{2,1,0:T(1,128)}, u32[]{:S(2)}, u32[]{:S(2)}) async-start(f32[128,1,3584]{2,1,0:T(1,128)} %broadcast_in_dim.75), calls=%async_computation.5 | async-start | bytes 3670016 | tf_op jit(solution)/shard_map/all_to_all | solution.py:197
  (9 other events, 39.4 us)

commit v3 on v2

v3 whole, which is shorter than its diff:
```python
import jax
import jax.numpy as jnp
from jax import lax
from jax.experimental import pallas as pl
from jax.experimental.pallas import tpu as pltpu
from jax.sharding import Mesh, PartitionSpec as P

EPS = 1e-05
BF = jnp.bfloat16
F32 = jnp.float32
HIGHEST = lax.Precision.HIGHEST
PEERS = 4
NEAR = 16
VMEM_LIMIT = 44 * 1024 * 1024


def receive_from(value, k):
    return lax.ppermute(value, "y", [(i, (i - k) % PEERS) for i in range(PEERS)])


def send_to(value, k):
    return lax.ppermute(value, "y", [(i, (i + k) % PEERS) for i in range(PEERS)])


def swap(value):
    return lax.ppermute(value, "core", [(0, 1), (1, 0)])


def over(value, axes="ep"):
    return lax.all_to_all(value, axes, split_axis=0, concat_axis=0, tiled=True)


def after(value, *others):
    return lax.optimization_barrier((value,) + others)[0]


def join_weights(gate, up, down):
    hidden = 2 * gate.shape[1]
    pad = -hidden % 128
    blank = jnp.zeros((gate.shape[0], pad), BF)
    wide = jnp.concatenate([gate, swap(gate), blank, up, swap(up), blank], 1)
    tall = jnp.concatenate([down, swap(down), jnp.zeros((pad, down.shape[1]), BF)], 0)
    return wide, tall


def hidden_kernel(count, rows_per_step, *refs):
    sources = refs[:count]
    wide, tall, into, joint, both, back, grads = refs[count : count + 7]
    step = pl.program_id(0)
    width = tall.shape[1]
    half = tall.shape[0]
    if count == 1:
        rows = sources[0]
    else:
        rows = refs[count + 7]
        size = sources[0].shape[0]
        each = rows_per_step // size
        for p in range(count):

            @pl.when(step == p // each)
            def _(p=p):
                rows[(p % each) * size : (p % each + 1) * size, :] = sources[p][...]

    tile = 256 if (2 * half) % 256 == 0 else 128

    def first(j, carry):
        cols = pl.ds(pl.multiple_of(j * tile, tile), tile)
        both[:, cols] = jnp.dot(rows[:, :width], wide[:, cols], preferred_element_type=F32)
        return carry

    lax.fori_loop(0, 2 * half // tile, first, 0)
    back[...] = lax.dot_general(
        rows[:, width:], tall[...], (((1,), (1,)), ((), ())), preferred_element_type=F32
    )
    gate, up, dy = both[:, :half], both[:, half:], back[...]
    sig = jax.nn.sigmoid(gate)
    active = gate * sig
    grad_up = dy * active
    grads[:, half:] = grad_up.astype(BF)
    grads[:, :half] = (dy * up * (sig + active * (1.0 - sig))).astype(BF)
    score = jnp.sum(grad_up * up, -1, keepdims=True)
    joint[...] = jnp.broadcast_to(score, joint.shape)
    block = 512 if width % 512 == 0 else 128

    def last(j, carry):
        cols = pl.ds(pl.multiple_of(j * block, block), block)
        into[:, cols] = lax.dot_general(
            grads[...], wide[cols, :], (((1,), (1,)), ((), ())), preferred_element_type=F32
        ).astype(BF)
        return carry

    lax.fori_loop(0, width // block, last, 0)


def hidden_grads(sources, wide, tall, step_rows):
    count = len(sources)
    size = sources[0].shape[0]
    total = count * size
    half, width = tall.shape
    steps = total // step_rows
    if count == 1:
        row_specs = [pl.BlockSpec((step_rows, 2 * width), lambda i: (i, 0))]
        extra = []
    else:
        row_specs = [
            pl.BlockSpec((size, 2 * width), lambda i: (0, 0), pipeline_mode=pl.Buffered(1))
        ] * count
        extra = [pltpu.VMEM((step_rows, 2 * width), BF)]

    def whole(shape):
        return pl.BlockSpec(shape, lambda i: (0, 0), pipeline_mode=pl.Buffered(1))

    into, joint = pl.pallas_call(
        lambda *refs: hidden_kernel(count, step_rows, *refs),
        grid=(steps,),
        in_specs=row_specs + [whole(wide.shape), whole(tall.shape)],
        out_specs=[
            pl.BlockSpec((step_rows, width), lambda i: (i, 0)),
            pl.BlockSpec((step_rows, 128), lambda i: (i, 0)),
        ],
        out_shape=[
            jax.ShapeDtypeStruct((total, width), BF),
            jax.ShapeDtypeStruct((total, 128), F32),
        ],
        scratch_shapes=[
            pltpu.VMEM((step_rows, 2 * half), F32),
            pltpu.VMEM((step_rows, half), F32),
            pltpu.VMEM((step_rows, 2 * half), BF),
        ]
        + extra,
        compiler_params=pltpu.CompilerParams(vmem_limit_bytes=VMEM_LIMIT),
        cost_estimate=pl.CostEstimate(
            flops=10 * total * width * half,
            bytes_accessed=6 * half * width + 6 * total * width,
            transcendentals=total * half,
        ),
    )(*sources, wide, tall)
    return into, joint[:, 0]


def pick_kernel(*refs):
    count = len(refs) // 2
    total = jnp.dot(refs[0][...], refs[count][...], preferred_element_type=F32)
    for i in range(1, count):
        total = total + jnp.dot(refs[i][...], refs[count + i][...], preferred_element_type=F32)
    refs[-1][...] = total.astype(BF)


def pick_rows(tables, sources):
    rows, tok = tables[0].shape
    width = sources[0].shape[1]
    block = 1024 if width % 1024 == 0 else 128
    count = len(sources)
    return pl.pallas_call(
        pick_kernel,
        grid=(width // block,),
        in_specs=[pl.BlockSpec((rows, tok), lambda i: (0, 0))] * count
        + [pl.BlockSpec((tok, block), lambda i: (0, i))] * count,
        out_specs=pl.BlockSpec((rows, block), lambda i: (0, i)),
        out_shape=jax.ShapeDtypeStruct((rows, width), BF),
        compiler_params=pltpu.CompilerParams(vmem_limit_bytes=VMEM_LIMIT),
        cost_estimate=pl.CostEstimate(
            flops=2 * count * rows * tok * width,
            bytes_accessed=2 * width * (rows + count * tok),
            transcendentals=0,
        ),
    )(*tables, *sources)


def slots_of(routes, experts):
    tok = routes.shape[0]
    flat = routes.reshape(2 * tok, 1)
    hits = (flat == lax.broadcasted_iota(jnp.int32, (1, experts), 1)).astype(BF)
    place = lax.broadcasted_iota(jnp.int32, (2 * tok, 2 * tok), 0)
    before = (lax.broadcasted_iota(jnp.int32, (2 * tok, 2 * tok), 1) < place).astype(BF)
    places = jnp.dot(before, hits, preferred_element_type=F32)
    return jnp.sum(hits.astype(F32) * places, -1).astype(jnp.int32).reshape(tok, 2)


def spread(index, rows):
    return index[..., None] == lax.broadcasted_iota(jnp.int32, (1, 1, rows), 2)


def picker(index, rows):
    hits = lax.broadcasted_iota(jnp.int32, (rows, 1), 0)
    return (hits == index[:, 0][None]).astype(BF) + (hits == index[:, 1][None]).astype(BF)


def router_weights(normed, router, chosen):
    logits = jnp.dot(normed.astype(F32), router, precision=HIGHEST)
    picked = jnp.sum(jnp.where(chosen, logits[:, None, :], 0.0), -1)
    one = jax.nn.sigmoid(picked[:, 0:1] - picked[:, 1:2])
    return jnp.concatenate([one, 1.0 - one], 1)


def mixer(hot, weights):
    return jnp.sum(jnp.where(hot, weights[..., None], 0.0), 1).astype(BF)


def body(
    tokens,
    cotangent,
    norm_gain,
    router,
    dense_gate,
    dense_up,
    dense_down,
    expert_gate,
    expert_up,
    expert_down,
    routes,
):
    tok, width = tokens.shape
    experts = router.shape[1]
    cap = 5 * tok // (2 * experts)
    own_rows = -(-cap // 8) * 8
    rest = cap - NEAR
    far_rows = -(-(cap + 2 * rest) // 8) * 8
    starts = {1: 0, 2: rest, 3: rest + cap}
    own_all = experts * own_rows
    far_all = experts * far_rows
    near_all = experts * NEAR
    none = -4 * far_all

    values = tokens.astype(F32)
    inverse = lax.rsqrt(jnp.mean(values * values, -1, keepdims=True) + EPS)
    normed = (values * inverse * norm_gain).astype(BF)
    pair = jnp.concatenate([normed, cotangent], 1)

    peer_routes = {k: receive_from(routes, k) for k in (1, 2, 3)}
    peer = {k: receive_from(pair, k) for k in (1, 2, 3)}
    own_index = routes * own_rows + slots_of(routes, experts)
    own = over(pick_rows([picker(own_index, own_all)], [pair]))

    far_index = {}
    for k in (1, 2, 3):
        slots = slots_of(peer_routes[k], experts)
        row = peer_routes[k] * far_rows + starts[k]
        if k == 2:
            far_index[k] = row + slots
        else:
            far_index[k] = jnp.where(slots >= NEAR, row + slots - NEAR, none)
    far_send = pick_rows(
        [picker(far_index[k], far_all) for k in (1, 2, 3)], [peer[k] for k in (1, 2, 3)]
    )
    far = over(far_send)
    near_send = own.reshape(experts, own_rows, 2 * width)[:, :NEAR].reshape(near_all, 2 * width)
    near1 = receive_from(near_send, 1)
    near3 = receive_from(near_send, 3)

    wide_e, tall_e = join_weights(expert_gate[0], expert_up[0], expert_down[0])
    wide_d, tall_d = join_weights(dense_gate, dense_up, dense_down)

    own_into, own_joint = hidden_grads(
        [after(own, far_send, near_send)], wide_e, tall_e, own_all // 2
    )
    dense_part, unused = hidden_grads(
        [after(pair, own_into)] + [peer[k] for k in (1, 2, 3)], wide_d, tall_d, 2 * tok
    )
    near_into, near_joint = hidden_grads(
        [after(near1, dense_part), near3], wide_e, tall_e, near_all
    )
    near1_back = send_to(near_into[:near_all], 1)
    near3_back = send_to(near_into[near_all:], 3)
    far_into, far_joint = hidden_grads([after(far, near_into)], wide_e, tall_e, far_all // 2)
    far_back = over(far_into)

    own_joint = own_joint.reshape(experts, own_rows)[:, :cap]
    near_joint = near_joint.reshape(2, experts, NEAR)
    far_joint = far_joint.reshape(experts, far_rows)
    joints = jnp.stack(
        [
            own_joint,
            jnp.concatenate([near_joint[0], far_joint[:, :rest]], 1),
            far_joint[:, starts[2] : starts[2] + cap],
            jnp.concatenate([near_joint[1], far_joint[:, starts[3] : starts[3] + rest]], 1),
        ],
        1,
    )
    plane = lax.broadcasted_iota(jnp.int32, (1, PEERS, PEERS, 1), 1)
    offset = lax.broadcasted_iota(jnp.int32, (1, PEERS, PEERS, 1), 2)
    meant = plane == (lax.axis_index("y") + offset) % PEERS
    joints = jnp.sum(jnp.where(meant, joints[:, None], 0.0), 2).reshape(experts * PEERS, cap)
    joints = over(after(joints, far_back), ("ep", "y"))
    score = jnp.sum(joints.reshape(experts, PEERS, cap), 1)

    near_back = near1_back.astype(F32) + near3_back.astype(F32)
    near_back = near_back.reshape(experts, NEAR, width)
    own_sum = own_into.astype(F32).reshape(experts, own_rows, width)
    own_sum = own_sum + jnp.pad(near_back, ((0, 0), (0, own_rows - NEAR), (0, 0)))
    own_sum = own_sum.astype(BF).reshape(own_all, width)
    own_back = over(after(own_sum, joints))

    ids = lax.broadcasted_iota(jnp.int32, (1, 1, experts), 2)
    chosen = routes[..., None] == ids
    weights = router_weights(normed, router, chosen)
    far_mix = []
    for k in (1, 2, 3):
        peer_weights = router_weights(peer[k][:, :width], router, peer_routes[k][..., None] == ids)
        far_mix.append(mixer(spread(far_index[k], far_all), peer_weights))
    mixed = jnp.dot(jnp.concatenate(far_mix, 0), far_back, preferred_element_type=F32)
    mixed = (mixed + dense_part[tok:].astype(F32)).astype(BF)
    home = [send_to(mixed[(k - 1) * tok : k * tok], k) for k in (2, 1, 3)]

    own_hot = spread(own_index, own_all)
    score = jnp.pad(score, ((0, 0), (0, own_rows - cap))).reshape(1, 1, -1)
    scores = jnp.sum(jnp.where(own_hot, score, 0.0), -1)
    delta = weights[:, 0] * weights[:, 1] * (scores[:, 0] - scores[:, 1])
    signed = chosen[:, 0].astype(F32) - chosen[:, 1].astype(F32)
    grad_logits = signed * delta[:, None]
    local_router = lax.dot_general(
        grad_logits, normed.astype(F32), (((0,), (0,)), ((), ())), precision=HIGHEST
    )
    early = dense_part[:tok].astype(F32)
    early = early + jnp.dot(grad_logits, router.T, precision=HIGHEST)

    own_mix = mixer(own_hot, weights)
    total = early + jnp.dot(own_mix, own_back, preferred_element_type=F32)
    for piece in home:
        total = total + piece.astype(F32)
    local_gain = jnp.sum(total * values * inverse, 0, keepdims=True)
    axes = ("ep", "y", "core")
    devices = lax.axis_size(axes)
    local = jnp.concatenate([local_router, local_gain], 0).reshape(devices, -1)
    mine = jnp.sum(over(local, axes), 0, keepdims=True)
    sums = over(jnp.broadcast_to(mine, local.shape), axes).reshape(experts + 1, width)
    scaled = total * norm_gain
    mean_term = jnp.mean(scaled * values, -1, keepdims=True)
    input_grad = cotangent.astype(F32) + inverse * (
        scaled - values * inverse * inverse * mean_term
    )
    return (input_grad.astype(BF), sums[experts], sums[:experts].T)


def solution(mesh):
    ep, sp = mesh.devices.shape
    grid = Mesh(mesh.devices.reshape(ep, sp // 2, 2), ("ep", "y", "core"))
    shared = ("y", "core")
    rows = ("ep", "y", "core")
    return jax.shard_map(
        body,
        mesh=grid,
        in_specs=(
            P(rows, None),
            P(rows, None),
            P(),
            P(),
            P(None, shared),
            P(None, shared),
            P(shared, None),
            P("ep", None, shared),
            P("ep", None, shared),
            P("ep", shared, None),
            P(rows, None),
        ),
        out_specs=(P(rows, None), P(), P()),
        check_vma=False,
    )
```

time: 497 us -> 516 us (1.038)
  Pallas kernels: 0 us -> 110 us
  matrix products: 125 us -> 20.7 us
  local copies, waits for them, and re-layouts: 32.6 us -> 98.5 us
  waiting for transfers between devices: 192 us -> 173 us
  other arithmetic: 43.4 us -> 24.8 us
  starting transfers between devices: 95.9 us -> 81.6 us
    pallas_call x0 -> x6, Pallas kernels: none -> 110 us  [the longest x4 96.5 us: hidden_grads(): pl.pallas_call(lambda *refs: hidden_kernel(count, step_rows, *refs), grid...]
    dot_general x22 -> x7, matrix products: 121 us -> 13.5 us  [the longest x1 5.31 us: body(): total = early + jnp.dot(own_mix, own_back, preferred_element_type=F32)]
    all_to_all x6 -> x7, waiting for transfers between devices: 62.7 us -> 23.2 us  [over(): return lax.all_to_all(value, axes, split_axis=0, concat_axis=0, tiled=True)]
    ppermute x8 -> x5, waiting for transfers between devices: 36.6 us -> 74.6 us  [send_to(): lax.ppermute(value, 'y', [(i, (i + k) % PEERS) for i in range(PEERS)])]
    concatenate x2, local copies, waits for them, and re-layouts: 1.43 us -> 34.5 us  [join_weights(): wide = jnp.concatenate([gate, swap(gate), blank, up, swap(up), blank], 1)]
    ppermute x0 -> x4, local copies, waits for them, and re-layouts: none -> 17.9 us  [swap(): return lax.ppermute(value, 'core', [(0, 1), (1, 0)])]
    concatenate x1 -> x2, other arithmetic: 18.9 us -> 6.28 us  [the longest x1 6.25 us: join_weights(): jnp.concatenate([down, swap(down), jnp.zeros((pad, down.shape[1]), BF)], 0)]
    ppermute x6 -> x0, waiting for transfers between devices: 9.66 us -> none  [over_all(): parts.append(lax.ppermute(value, 'ep', pairs))]
  transfers between devices with their start and end apart: 36 -> 26, of which waited for: 12 -> 9; matrix products, arithmetic and copies ran while one was open for 40% -> 23% of each run, Pallas kernels for 0% -> 17%
where the time goes in v3:
time: 516 us; the launch traced here: 510 us
  waiting for transfers between devices  173 us (34%)
  Pallas kernels  110 us (21%)
  local copies, waits for them, and re-layouts  98.5 us (19%)
  starting transfers between devices  81.6 us (16%)
  other arithmetic  24.8 us (5%)
  matrix products  20.7 us (4%)
    pallas_call x4, Pallas kernels, hidden_grads(): pl.pallas_call(lambda *refs: hidden_kernel(count, step_rows, *refs), grid...  96.5 us
    ppermute x8, waiting for transfers between devices, receive_from(): lax.ppermute(value, 'y', [(i, (i - k) % PEERS) for i in range(PEERS)])  75.2 us
    ppermute x5, waiting for transfers between devices, send_to(): lax.ppermute(value, 'y', [(i, (i + k) % PEERS) for i in range(PEERS)])  74.6 us
    all_to_all x7, starting transfers between devices, over(): return lax.all_to_all(value, axes, split_axis=0, concat_axis=0, tiled=True)  60.3 us
    concatenate x2, local copies, waits for them, and re-layouts, join_weights(): wide = jnp.concatenate([gate, swap(gate), blank, up, swap(up), blank], 1)  34.5 us
    unnamed x43, local copies, waits for them, and re-layouts  28.4 us
    all_to_all x7, waiting for transfers between devices, over(): return lax.all_to_all(value, axes, split_axis=0, concat_axis=0, tiled=True)  23.2 us
    ppermute x4, local copies, waits for them, and re-layouts, swap(): return lax.ppermute(value, 'core', [(0, 1), (1, 0)])  17.9 us
  transfers between devices with their start and end apart: 26, of which 9 were waited for; matrix products, arithmetic and copies ran while one was open for 23% of the time, Pallas kernels for 17%

profile of v3, /device:TPU:1, one launch (start us, length us, event | category | flops | bytes accessed | tf_op | source)
XLA Modules:
  0.0 510.0 jit_solution(3909843722102332929)
XLA Ops:
  5.8 2.9 shard_map.130
  8.7 2.4 copy-done.1
  11.1 8.6 %all-to-all-start = ((bf16[16,24,7168]{2,1,0:T(8,128)(2,1)}), bf16[16,24,7168]{2,1,0:T(8,128)(2,1)}, u32[]{:S(2)}, u32[]{:S(2)}) async-start(bf16[16,24,7168]{2,1,0:T(8,128)(2,1)} %bitcast.49), calls=%async_computation | async-start | bytes 11010048 | tf_op jit(solution)/shard_map/all_to_all | solution.py:30
  21.1 2.6 collective-permute-start.1
  23.7 2.2 collective-permute-start.4
  28.1 2.4 collective-permute-start.8
  31.4 75.1 %collective-permute-done = s32[128,2]{1,0:T(8,128)S(1)} collective-permute-done((s32[128,2]{1,0:T(8,128)S(1)}, s32[128,2]{1,0:T(8,128)S(1)}, u32[]{:S(2)}, u32[]{:S(2)}) %collective-permute-start) | collective-permute-done | bytes 1056 | tf_op jit(solution)/shard_map/ppermute | solution.py:18
  106.5 2.2 collective-permute-start.7
  110.7 10.5 %shard_map.131 = bf16[512,7168]{1,0:T(8,128)(2,1)} custom-call(bf16[512,128]{1,0:T(8,128)(2,1)S(1)} %fusion.41.refs_0_, bf16[512,128]{1,0:T(8,128)(2,1)S(1)} %get-tuple-element.60.refs_1_, bf16[512,128]{1,0:T(8,128)(2,1)S(1)} %get-tuple-element.59.refs_2_, bf16[128,7168]{1,0:T(8,128)(2,1)} %collective-permute-done.3.refs_3_.refs_1_, ...), custom_call_target="tpu_custom_call" | custom-call | flops 2818572288 | bytes 12845056 | tf_op jit(solution)/shard_map/pallas_call | solution.py:154
  121.2 6.6 %all-to-all-start.1 = ((bf16[16,32,7168]{2,1,0:T(8,128)(2,1)}), bf16[16,32,7168]{2,1,0:T(8,128)(2,1)}, u32[]{:S(2)}, u32[]{:S(2)}) async-start(bf16[16,32,7168]{2,1,0:T(8,128)(2,1)} %bitcast.52), calls=%async_computation.1 | async-start | bytes 14680064 | tf_op jit(solution)/shard_map/all_to_all | solution.py:30
  127.8 4.4 copy.144
  132.2 4.4 copy.146
  136.6 4.4 copy.138
  141.1 4.4 copy.140
  151.5 4.2 slice.177
  156.3 2.0 collective-permute-start.12
  160.4 4.7 copy.145
  165.1 4.4 copy.147
  169.6 17.2 %concatenate.42.refs_4_ = bf16[3584,1280]{1,0:T(8,128)(2,1)} concatenate(bf16[3584,304]{1,0:T(8,128)(2,1)} %copy.144, bf16[3584,304]{1,0:T(8,128)(2,1)} %copy.145, bf16[3584,32]{1,0:T(8,128)(2,1)S(1)} %broadcast.121, bf16[3584,304]{1,0:T(8,128)(2,1)} %copy.146, bf16[3584,304]{1,0:T(8,128)(2,1)} %copy.147, bf16[3584,32]{1,0:T(8,128)(2,1)S(1)} %broadcast.121), dimensions={1} | concatenate | bytes 18350080 | tf_op jit(solution)/shard_map/concatenate | solution.py:41
  186.8 4.4 copy.143
  191.2 4.4 copy.142
  195.7 17.2 %concatenate.40.refs_1_.refs_2_ = bf16[3584,1280]{1,0:T(8,128)(2,1)} concatenate(bf16[3584,304]{1,0:T(8,128)(2,1)} %bitcast.54, bf16[3584,304]{1,0:T(8,128)(2,1)} %copy.142, bf16[3584,32]{1,0:T(8,128)(2,1)S(1)} %broadcast.121, bf16[3584,304]{1,0:T(8,128)(2,1)} %bitcast.55, bf16[3584,304]{1,0:T(8,128)(2,1)} %copy.143, bf16[3584,32]{1,0:T(8,128)(2,1)S(1)} %broadcast.121), dimensions={1} | concatenate | bytes 18350080 | tf_op jit(solution)/shard_map/concatenate | solution.py:41
  212.9 6.3 %maximum_maximum_fusion.1 = (bf16[640,3584]{1,0:T(8,128)(2,1)}, bf16[640,3584]{1,0:T(8,128)(2,1)S(1)}) fusion(bf16[304,3584]{1,0:T(8,128)(2,1)} %collective-permute-done.11, bf16[304,3584]{1,0:T(8,128)(2,1)} %param.17, bf16[640]{0:T(1024)(128)(2,1)S(1)} %pad.36.clone, bf16[304,3584]{1,0:T(8,128)(2,1)} %collective-permute-done.8, bf16[304,3584]{1,0:T(8,128)(2,1)} %bitcast.59), kind=kLoop, calls=%fused_computation.4 | loop fusion | flops 25231360 | bytes 17892608 | tf_op jit(solution)/shard_map/concatenate | solution.py:42
  219.2 23.1 %shard_map.132 = (bf16[384,3584]{1,0:T(8,128)(2,1)S(1)}, f32[384,128]{1,0:T(8,128)S(1)}) custom-call(bf16[384,7168]{1,0:T(8,128)(2,1)} %bitcast.1.refs_0_, bf16[3584,1280]{1,0:T(8,128)(2,1)} %concatenate.40.refs_1_.refs_2_, bf16[640,3584]{1,0:T(8,128)(2,1)S(1)} %get-tuple-element.58.refs_2_.refs_3_), custom_call_target="tpu_custom_call" | custom-call | flops 8808038400 | bytes 22020096 | tf_op jit(solution)/shard_map/pallas_call | solution.py:113
  243.8 25.8 %shard_map.133 = (bf16[512,3584]{1,0:T(8,128)(2,1)}, f32[512,128]{1,0:T(8,128)}) custom-call(bf16[128,7168]{1,0:T(8,128)(2,1)S(1)} %pad_maximum_fusion.refs_1_.refs_0_, bf16[128,7168]{1,0:T(8,128)(2,1)} %collective-permute-done.3.refs_3_.refs_1_, bf16[128,7168]{1,0:T(8,128)(2,1)} %collective-permute-done.4.refs_4_.refs_2_, ...), custom_call_target="tpu_custom_call" | custom-call | flops 11744051200 | bytes 24772608 | tf_op jit(solution)/shard_map/pallas_call | solution.py:113
  269.7 25.2 %shard_map.134 = (bf16[512,3584]{1,0:T(8,128)(2,1)S(1)}, f32[512,128]{1,0:T(8,128)S(1)}) custom-call(bf16[256,7168]{1,0:T(8,128)(2,1)} %collective-permute-done.12.refs_0_, bf16[256,7168]{1,0:T(8,128)(2,1)} %collective-permute-done.13.refs_1_, bf16[3584,1280]{1,0:T(8,128)(2,1)} %concatenate.40.refs_1_.refs_2_, bf16[640,3584]{1,0:T(8,128)(2,1)} %copy-done.2), custom_call_target="tpu_custom_call" | custom-call | flops 11744051200 | bytes 24772608 | tf_op jit(solution)/shard_map/pallas_call | solution.py:113
  296.7 2.3 copy-done.3
  299.0 22.4 %shard_map.135 = (bf16[512,3584]{1,0:T(8,128)(2,1)S(1)}, f32[512,128]{1,0:T(8,128)S(1)}) custom-call(bf16[512,7168]{1,0:T(8,128)(2,1)} %bitcast.11.refs_0_, bf16[3584,1280]{1,0:T(8,128)(2,1)} %concatenate.40.refs_1_.refs_2_, bf16[640,3584]{1,0:T(8,128)(2,1)S(1)} %copy-done.3), custom_call_target="tpu_custom_call" | custom-call | flops 11744051200 | bytes 24772608 | tf_op jit(solution)/shard_map/pallas_call | solution.py:113
  323.2 16.4 %all-to-all-start.2 = ((bf16[16,32,3584]{2,1,0:T(8,128)(2,1)}), bf16[16,32,3584]{2,1,0:T(8,128)(2,1)}, u32[]{:S(2)}, u32[]{:S(2)}) async-start(bf16[16,32,3584]{2,1,0:T(8,128)(2,1)} %bitcast.50), calls=%async_computation.2 | async-start | bytes 7340032 | tf_op jit(solution)/shard_map/all_to_all | solution.py:30
  339.6 4.1 fusion.63
  343.7 2.7 collective-permute-start.15
  348.5 37.4 %collective-permute-done.14 = bf16[256,3584]{1,0:T(8,128)(2,1)} collective-permute-done((bf16[256,3584]{1,0:T(8,128)(2,1)}, bf16[256,3584]{1,0:T(8,128)(2,1)}, u32[]{:S(2)}, u32[]{:S(2)}) %collective-permute-start.14) | collective-permute-done | bytes 1835040 | tf_op jit(solution)/shard_map/ppermute | solution.py:22
  385.9 4.5 convert_add_fusion.1
  391.4 12.0 %all-to-all-start.3 = ((f32[64,1,20]{2,1,0:T(1,128)}), f32[64,1,20]{2,1,0:T(1,128)S(1)}, u32[]{:S(2)}, u32[]{:S(2)}) async-start(f32[64,1,20]{2,1,0:T(1,128)} %bitcast.19), calls=%async_computation.3 | async-start | bytes 65536 | tf_op jit(solution)/shard_map/all_to_all | solution.py:30
  403.4 4.2 fusion
  407.6 4.1 all-to-all-done.3
  411.7 4.5 all-to-all-start.4
  416.3 4.5 add_convert_fusion
  426.1 2.9 fusion.50
  429.0 13.7 %collective-permute-done.16 = bf16[128,3584]{1,0:T(8,128)(2,1)S(1)} collective-permute-done((bf16[128,3584]{1,0:T(8,128)(2,1)}, bf16[128,3584]{1,0:T(8,128)(2,1)S(1)}, u32[]{:S(2)}, u32[]{:S(2)}) %collective-permute-start.16) | collective-permute-done | bytes 917536 | tf_op jit(solution)/shard_map/ppermute | solution.py:22
  442.7 20.9 %collective-permute-done.18 = bf16[128,3584]{1,0:T(8,128)(2,1)} collective-permute-done((bf16[128,3584]{1,0:T(8,128)(2,1)}, bf16[128,3584]{1,0:T(8,128)(2,1)}, u32[]{:S(2)}, u32[]{:S(2)}) %collective-permute-start.18) | collective-permute-done | bytes 917536 | tf_op jit(solution)/shard_map/ppermute | solution.py:22
  463.6 2.5 collective-permute-done.17
  466.2 5.3 %fusion.12 = (f32[3584]{0:T(1024)S(1)}, f32[128]{0:T(128)}, f32[128,3584]{1,0:T(8,128)S(1)}) fusion(bf16[128,3584]{1,0:T(8,128)(2,1)S(1)} %copy-done.9, f32[128]{0:T(128)S(1)} %copy-done.18, f32[3584]{0:T(1024)S(1)} %copy-done.14, bf16[128,3584]{1,0:T(8,128)(2,1)} %collective-permute-done.18, bf16[128,3584]{1,0:T(8,128)(2,1)} %collective-permute-done.17, ...), kind=kOutput, calls=%fused_computation.21 | convolution fusion | flops 359657856 | bytes 11138048 | tf_op jit(solution)/shard_map/dot_general | solution.py:318
  472.7 7.5 %all-to-all-start.5 = ((f32[128,1,476]{2,1,0:T(1,128)}), f32[128,1,476]{2,1,0:T(1,128)S(1)}, u32[]{:S(2)}, u32[]{:S(2)}) async-start(f32[128,1,476]{2,1,0:T(1,128)} %all_to_all.65), calls=%async_computation.5 | async-start | bytes 524288 | tf_op jit(solution)/shard_map/all_to_all | solution.py:30
  480.8 10.1 %all-to-all-done.5 = f32[128,1,476]{2,1,0:T(1,128)S(1)} async-done(((f32[128,1,476]{2,1,0:T(1,128)}), f32[128,1,476]{2,1,0:T(1,128)S(1)}, u32[]{:S(2)}, u32[]{:S(2)}) %all-to-all-start.5) | async-done | bytes 243744 | tf_op jit(solution)/shard_map/all_to_all | solution.py:30
  492.0 4.8 all-to-all-start.6
  496.8 2.8 fusion.8
  499.5 8.0 %all-to-all-done.6 = f32[128,1,476]{2,1,0:T(1,128)S(1)} async-done(((f32[128,1,476]{2,1,0:T(1,128)}), f32[128,1,476]{2,1,0:T(1,128)S(1)}, u32[]{:S(2)}, u32[]{:S(2)}) %all-to-all-start.6) | async-done | bytes 243744 | tf_op jit(solution)/shard_map/all_to_all | solution.py:30
  (166 shorter events, 38.8 us)
Async XLA Ops:
  0.6 25.8 %copy-start = (f32[3584,16]{0,1:T(8,128)S(1)}, f32[3584,16]{0,1:T(8,128)}, u32[]{:S(2)}) copy-start(f32[3584,16]{0,1:T(8,128)} %param.14) | copy-start | bytes 688132
  0.6 3.9 copy-start.8
  3.7 2.1 copy-start.17
  4.3 1.3 copy-start.12
  5.6 20.8 %copy-start.10 = (bf16[128,3584]{1,0:T(8,128)(2,1)}, bf16[128,3584]{1,0:T(8,128)(2,1)S(1)}, u32[]{:S(2)}) copy-start(bf16[128,3584]{1,0:T(8,128)(2,1)S(1)} %fusion.3) | copy-start | bytes 2752516
  8.7 2.4 copy-start.1
  11.1 16.1 %copy-start.15 = (s32[128,2]{0,1:T(2,128)S(1)}, s32[128,2]{0,1:T(2,128)}, u32[]{:S(2)}) copy-start(s32[128,2]{0,1:T(2,128)} %param.21) | copy-start | bytes 3076
  11.1 110.1 %all-to-all-start = ((bf16[16,24,7168]{2,1,0:T(8,128)(2,1)}), bf16[16,24,7168]{2,1,0:T(8,128)(2,1)}, u32[]{:S(2)}, u32[]{:S(2)}) async-start(bf16[16,24,7168]{2,1,0:T(8,128)(2,1)} %bitcast.49), calls=%async_computation | async-start | bytes 11010048 | tf_op jit(solution)/shard_map/all_to_all | solution.py:30
  19.7 7.5 %collective-permute-start.2 = (s32[128,2]{1,0:T(8,128)S(1)}, s32[128,2]{1,0:T(8,128)S(1)}, u32[]{:S(2)}, u32[]{:S(2)}) collective-permute-start(s32[128,2]{1,0:T(8,128)S(1)} %copy.133), channel_id=1, source_target_pairs={{0,2},{2,4},{4,6},{6,0},{1,3},{3,5},{5,7},{7,1},{8,10},{10,12},{12... | collective-permute-start | bytes 3080 | tf_op jit(solution)/shard_map/ppermute | solution.py:18
  21.1 7.0 %collective-permute-start.1 = (s32[128,2]{1,0:T(8,128)S(1)}, s32[128,2]{1,0:T(8,128)S(1)}, u32[]{:S(2)}, u32[]{:S(2)}) collective-permute-start(s32[128,2]{1,0:T(8,128)S(1)} %copy.133), channel_id=1, source_target_pairs={{0,4},{2,6},{4,0},{6,2},{1,5},{3,7},{5,1},{7,3},{8,12},{10,14},{12... | collective-permute-start | bytes 3080 | tf_op jit(solution)/shard_map/ppermute | solution.py:18
  23.7 86.3 %collective-permute-start.5 = (bf16[128,7168]{1,0:T(8,128)(2,1)S(1)}, bf16[128,7168]{1,0:T(8,128)(2,1)}, u32[]{:S(2)}, u32[]{:S(2)}) collective-permute-start(bf16[128,7168]{1,0:T(8,128)(2,1)S(1)} %pad_maximum_fusion.refs_1_.refs_0_), channel_id=1, source_target_pairs={{0,2},{2,4},{4,6},{6,0},{1,3},{3,5},{5,7},{7,1},{8,10},{10,12},{12... | collective-permute-start | bytes 5505032 | tf_op jit(solution)/shard_map/ppermute | solution.py:18
  23.7 86.4 %collective-permute-start.4 = (bf16[128,7168]{1,0:T(8,128)(2,1)S(1)}, bf16[128,7168]{1,0:T(8,128)(2,1)}, u32[]{:S(2)}, u32[]{:S(2)}) collective-permute-start(bf16[128,7168]{1,0:T(8,128)(2,1)S(1)} %pad_maximum_fusion.refs_1_.refs_0_), channel_id=1, source_target_pairs={{0,4},{2,6},{4,0},{6,2},{1,5},{3,7},{5,1},{7,3},{8,12},{10,14},{12... | collective-permute-start | bytes 5505032 | tf_op jit(solution)/shard_map/ppermute | solution.py:18
  26.0 84.7 %collective-permute-start.3 = (bf16[128,7168]{1,0:T(8,128)(2,1)S(1)}, bf16[128,7168]{1,0:T(8,128)(2,1)}, u32[]{:S(2)}, u32[]{:S(2)}) collective-permute-start(bf16[128,7168]{1,0:T(8,128)(2,1)S(1)} %pad_maximum_fusion.refs_1_.refs_0_), channel_id=1, source_target_pairs={{0,6},{2,0},{4,2},{6,4},{1,7},{3,1},{5,3},{7,5},{8,14},{10,8},{12,... | collective-permute-start | bytes 5505032 | tf_op jit(solution)/shard_map/ppermute | solution.py:18
  27.3 79.2 %collective-permute-start = (s32[128,2]{1,0:T(8,128)S(1)}, s32[128,2]{1,0:T(8,128)S(1)}, u32[]{:S(2)}, u32[]{:S(2)}) collective-permute-start(s32[128,2]{1,0:T(8,128)S(1)} %copy.133), channel_id=1, source_target_pairs={{0,6},{2,0},{4,2},{6,4},{1,7},{3,1},{5,3},{7,5},{8,14},{10,8},{12,... | collective-permute-start | bytes 3080 | tf_op jit(solution)/shard_map/ppermute | solution.py:18
  28.1 184.8 %collective-permute-start.8 = (bf16[304,3584]{1,0:T(8,128)(2,1)}, bf16[304,3584]{1,0:T(8,128)(2,1)}, u32[]{:S(2)}, u32[]{:S(2)}) collective-permute-start(bf16[304,3584]{1,0:T(8,128)(2,1)} %bitcast.58), channel_id=1, source_target_pairs={{0,1},{1,0},{2,3},{3,2},{4,5},{5,4},{6,7},{7,6},{8,9},{9,8},{10,11... | collective-permute-start | bytes 6537224 | tf_op jit(solution)/shard_map/ppermute | solution.py:26
  106.5 39.7 %collective-permute-start.7 = (bf16[3584,304]{0,1:T(8,128)(2,1)}, bf16[3584,304]{0,1:T(8,128)(2,1)}, u32[]{:S(2)}, u32[]{:S(2)}) collective-permute-start(bf16[3584,304]{0,1:T(8,128)(2,1)} %bitcast.56), channel_id=1, source_target_pairs={{0,1},{1,0},{2,3},{3,2},{4,5},{5,4},{6,7},{7,6},{8,9},{9,8},{10,11... | collective-permute-start | bytes 6537224 | tf_op jit(solution)/shard_map/ppermute | solution.py:26
  110.0 81.2 %collective-permute-start.6 = (bf16[3584,304]{0,1:T(8,128)(2,1)}, bf16[3584,304]{0,1:T(8,128)(2,1)}, u32[]{:S(2)}, u32[]{:S(2)}) collective-permute-start(bf16[3584,304]{0,1:T(8,128)(2,1)} %bitcast.57), channel_id=1, source_target_pairs={{0,1},{1,0},{2,3},{3,2},{4,5},{5,4},{6,7},{7,6},{8,9},{9,8},{10,11... | collective-permute-start | bytes 6537224 | tf_op jit(solution)/shard_map/ppermute | solution.py:26
  110.1 45.6 %collective-permute-start.9 = (bf16[3584,304]{0,1:T(8,128)(2,1)}, bf16[3584,304]{0,1:T(8,128)(2,1)}, u32[]{:S(2)}, u32[]{:S(2)}) collective-permute-start(bf16[3584,304]{0,1:T(8,128)(2,1)} %param.15), channel_id=1, source_target_pairs={{0,1},{1,0},{2,3},{3,2},{4,5},{5,4},{6,7},{7,6},{8,9},{9,8},{10,11... | collective-permute-start | bytes 6537224 | tf_op jit(solution)/shard_map/ppermute | solution.py:26
  110.6 45.7 %collective-permute-start.10 = (bf16[3584,304]{0,1:T(8,128)(2,1)}, bf16[3584,304]{0,1:T(8,128)(2,1)}, u32[]{:S(2)}, u32[]{:S(2)}) collective-permute-start(bf16[3584,304]{0,1:T(8,128)(2,1)} %param.16), channel_id=1, source_target_pairs={{0,1},{1,0},{2,3},{3,2},{4,5},{5,4},{6,7},{7,6},{8,9},{9,8},{10,11... | collective-permute-start | bytes 6537224 | tf_op jit(solution)/shard_map/ppermute | solution.py:26
  121.2 175.5 %all-to-all-start.1 = ((bf16[16,32,7168]{2,1,0:T(8,128)(2,1)}), bf16[16,32,7168]{2,1,0:T(8,128)(2,1)}, u32[]{:S(2)}, u32[]{:S(2)}) async-start(bf16[16,32,7168]{2,1,0:T(8,128)(2,1)} %bitcast.52), calls=%async_computation.1 | async-start | bytes 14680064 | tf_op jit(solution)/shard_map/all_to_all | solution.py:30
  146.2 66.7 %collective-permute-start.11 = (bf16[304,3584]{1,0:T(8,128)(2,1)}, bf16[304,3584]{1,0:T(8,128)(2,1)}, u32[]{:S(2)}, u32[]{:S(2)}) collective-permute-start(bf16[304,3584]{1,0:T(8,128)(2,1)} %param.17), channel_id=1, source_target_pairs={{0,1},{1,0},{2,3},{3,2},{4,5},{5,4},{6,7},{7,6},{8,9},{9,8},{10,11... | collective-permute-start | bytes 6537224 | tf_op jit(solution)/shard_map/ppermute | solution.py:26
  155.7 114.0 %collective-permute-start.13 = (bf16[256,7168]{1,0:T(8,128)(2,1)}, bf16[256,7168]{1,0:T(8,128)(2,1)}, u32[]{:S(2)}, u32[]{:S(2)}) collective-permute-start(bf16[256,7168]{1,0:T(8,128)(2,1)} %bitcast.2), channel_id=1, source_target_pairs={{0,2},{2,4},{4,6},{6,0},{1,3},{3,5},{5,7},{7,1},{8,10},{10,12},{12... | collective-permute-start | bytes 11010056 | tf_op jit(solution)/shard_map/ppermute | solution.py:18
  156.3 113.4 %collective-permute-start.12 = (bf16[256,7168]{1,0:T(8,128)(2,1)}, bf16[256,7168]{1,0:T(8,128)(2,1)}, u32[]{:S(2)}, u32[]{:S(2)}) collective-permute-start(bf16[256,7168]{1,0:T(8,128)(2,1)} %bitcast.2), channel_id=1, source_target_pairs={{0,6},{2,0},{4,2},{6,4},{1,7},{3,1},{5,3},{7,5},{8,14},{10,8},{12,... | collective-permute-start | bytes 11010056 | tf_op jit(solution)/shard_map/ppermute | solution.py:18
  219.2 23.1 %copy-start.2 = (bf16[640,3584]{1,0:T(8,128)(2,1)}, bf16[640,3584]{1,0:T(8,128)(2,1)S(1)}, u32[]{:S(2)}) copy-start(bf16[640,3584]{1,0:T(8,128)(2,1)S(1)} %get-tuple-element.58.refs_2_.refs_3_) | copy-start | bytes 13762564
  242.3 1.6 copy-start.6
  294.9 1.8 copy-start.5
  296.7 2.3 copy-start.3
  321.4 1.8 copy-start.4
  323.2 68.1 %all-to-all-start.2 = ((bf16[16,32,3584]{2,1,0:T(8,128)(2,1)}), bf16[16,32,3584]{2,1,0:T(8,128)(2,1)}, u32[]{:S(2)}, u32[]{:S(2)}) async-start(bf16[16,32,3584]{2,1,0:T(8,128)(2,1)} %bitcast.50), calls=%async_computation.2 | async-start | bytes 7340032 | tf_op jit(solution)/shard_map/all_to_all | solution.py:30
  343.7 42.2 %collective-permute-start.14 = (bf16[256,3584]{1,0:T(8,128)(2,1)}, bf16[256,3584]{1,0:T(8,128)(2,1)}, u32[]{:S(2)}, u32[]{:S(2)}) collective-permute-start(bf16[256,3584]{1,0:T(8,128)(2,1)} %get-tuple-element.50), channel_id=1, source_target_pairs={{0,2},{2,4},{4,6},{6,0},{1,3},{3,5},{5,7},{7,1},{8,10},{10,12},{12... | collective-permute-start | bytes 5505032 | tf_op jit(solution)/shard_map/ppermute | solution.py:22
  343.7 42.2 %collective-permute-start.15 = (bf16[256,3584]{1,0:T(8,128)(2,1)}, bf16[256,3584]{1,0:T(8,128)(2,1)}, u32[]{:S(2)}, u32[]{:S(2)}) collective-permute-start(bf16[256,3584]{1,0:T(8,128)(2,1)} %get-tuple-element.51), channel_id=1, source_target_pairs={{0,6},{2,0},{4,2},{6,4},{1,7},{3,1},{5,3},{7,5},{8,14},{10,8},{12,... | collective-permute-start | bytes 5505032 | tf_op jit(solution)/shard_map/ppermute | solution.py:22
  348.5 54.8 %copy-start.7 = (bf16[384,3584]{1,0:T(8,128)(2,1)S(1)}, bf16[384,3584]{1,0:T(8,128)(2,1)}, u32[]{:S(2)}) copy-start(bf16[384,3584]{1,0:T(8,128)(2,1)} %copy-done.6) | copy-start | bytes 8257540
  391.4 20.3 %all-to-all-start.3 = ((f32[64,1,20]{2,1,0:T(1,128)}), f32[64,1,20]{2,1,0:T(1,128)S(1)}, u32[]{:S(2)}, u32[]{:S(2)}) async-start(f32[64,1,20]{2,1,0:T(1,128)} %bitcast.19), calls=%async_computation.3 | async-start | bytes 65536 | tf_op jit(solution)/shard_map/all_to_all | solution.py:30
  411.7 54.5 %all-to-all-start.4 = ((bf16[16,24,3584]{2,1,0:T(8,128)(2,1)}), bf16[16,24,3584]{2,1,0:T(8,128)(2,1)}, u32[]{:S(2)}, u32[]{:S(2)}) async-start(bf16[16,24,3584]{2,1,0:T(8,128)(2,1)} %fusion), calls=%async_computation.4 | async-start | bytes 5505024 | tf_op jit(solution)/shard_map/all_to_all | solution.py:30
  420.8 4.8 copy-start.11
  420.8 4.8 copy-start.16
  422.4 43.8 %copy-start.9 = (bf16[128,3584]{1,0:T(8,128)(2,1)S(1)}, bf16[128,3584]{1,0:T(8,128)(2,1)}, u32[]{:S(2)}) copy-start(bf16[128,3584]{1,0:T(8,128)(2,1)} %param.11) | copy-start | bytes 2752516
  422.4 43.8 %copy-start.14 = (f32[3584]{0:T(1024)S(1)}, f32[3584]{0:T(1024)}, u32[]{:S(2)}) copy-start(f32[3584]{0:T(1024)} %param.13) | copy-start | bytes 43012
  422.4 43.8 %copy-start.18 = (f32[128]{0:T(128)S(1)}, f32[128]{0:T(128)}, u32[]{:S(2)}) copy-start(f32[128]{0:T(128)} %copy-done.17) | copy-start | bytes 1540
  422.4 20.3 %collective-permute-start.16 = (bf16[128,3584]{1,0:T(8,128)(2,1)}, bf16[128,3584]{1,0:T(8,128)(2,1)S(1)}, u32[]{:S(2)}, u32[]{:S(2)}) collective-permute-start(bf16[128,3584]{1,0:T(8,128)(2,1)} %get-tuple-element.52), channel_id=1, source_target_pairs={{0,4},{2,6},{4,0},{6,2},{1,5},{3,7},{5,1},{7,3},{8,12},{10,14},{12... | collective-permute-start | bytes 2752520 | tf_op jit(solution)/shard_map/ppermute | solution.py:22
  423.3 40.4 %collective-permute-start.18 = (bf16[128,3584]{1,0:T(8,128)(2,1)}, bf16[128,3584]{1,0:T(8,128)(2,1)}, u32[]{:S(2)}, u32[]{:S(2)}) collective-permute-start(bf16[128,3584]{1,0:T(8,128)(2,1)} %get-tuple-element.53), channel_id=1, source_target_pairs={{0,6},{2,0},{4,2},{6,4},{1,7},{3,1},{5,3},{7,5},{8,14},{10,8},{12,... | collective-permute-start | bytes 2752520 | tf_op jit(solution)/shard_map/ppermute | solution.py:22
  425.1 41.1 %collective-permute-start.17 = (bf16[128,3584]{1,0:T(8,128)(2,1)}, bf16[128,3584]{1,0:T(8,128)(2,1)}, u32[]{:S(2)}, u32[]{:S(2)}) collective-permute-start(bf16[128,3584]{1,0:T(8,128)(2,1)} %get-tuple-element.54), channel_id=1, source_target_pairs={{0,2},{2,4},{4,6},{6,0},{1,3},{3,5},{5,7},{7,1},{8,10},{10,12},{12... | collective-permute-start | bytes 2752520 | tf_op jit(solution)/shard_map/ppermute | solution.py:22
  442.7 23.5 %copy-start.13 = (bf16[128,3584]{1,0:T(8,128)(2,1)}, bf16[128,3584]{1,0:T(8,128)(2,1)S(1)}, u32[]{:S(2)}) copy-start(bf16[128,3584]{1,0:T(8,128)(2,1)S(1)} %collective-permute-done.16) | copy-start | bytes 2752516
  472.7 18.2 %all-to-all-start.5 = ((f32[128,1,476]{2,1,0:T(1,128)}), f32[128,1,476]{2,1,0:T(1,128)S(1)}, u32[]{:S(2)}, u32[]{:S(2)}) async-start(f32[128,1,476]{2,1,0:T(1,128)} %all_to_all.65), calls=%async_computation.5 | async-start | bytes 524288 | tf_op jit(solution)/shard_map/all_to_all | solution.py:30
  492.0 15.5 %all-to-all-start.6 = ((f32[128,1,476]{2,1,0:T(1,128)}), f32[128,1,476]{2,1,0:T(1,128)S(1)}, u32[]{:S(2)}, u32[]{:S(2)}) async-start(f32[128,1,476]{2,1,0:T(1,128)} %broadcast_in_dim.152), calls=%async_computation.6 | async-start | bytes 524288 | tf_op jit(solution)/shard_map/all_to_all | solution.py:30

commit v4 on v3

--- a/solution.py
+++ b/solution.py
@@ -12,6 +12,7 @@
 PEERS = 4
 NEAR = 16
 VMEM_LIMIT = 44 * 1024 * 1024
+TRANS = (((1,), (1,)), ((), ()))
 
 
 def receive_from(value, k):
@@ -34,25 +35,39 @@
     return lax.optimization_barrier((value,) + others)[0]
 
 
-def join_weights(gate, up, down):
-    hidden = 2 * gate.shape[1]
-    pad = -hidden % 128
-    blank = jnp.zeros((gate.shape[0], pad), BF)
-    wide = jnp.concatenate([gate, swap(gate), blank, up, swap(up), blank], 1)
-    tall = jnp.concatenate([down, swap(down), jnp.zeros((pad, down.shape[1]), BF)], 0)
-    return wide, tall
+def weight_pieces(gate, up, down):
+    both = [gate.T, up.T, down]
+    return [piece for value in both for piece in (value, swap(value))]
 
 
 def hidden_kernel(count, rows_per_step, *refs):
     sources = refs[:count]
-    wide, tall, into, joint, both, back, grads = refs[count : count + 7]
+    pieces = refs[count : count + 6]
+    into, joint, table, both, back, grads, sems = refs[count + 6 : count + 13]
     step = pl.program_id(0)
-    width = tall.shape[1]
-    half = tall.shape[0]
+    part, width = pieces[0].shape
+    half = table.shape[0] // 3
+    copies = []
+    for i in range(6):
+        start = i // 2 * half + i % 2 * part
+        copies.append(
+            pltpu.make_async_copy(pieces[i], table.at[pl.ds(start, part), :], sems.at[i])
+        )
+
+    @pl.when(step == 0)
+    def _():
+        for copy in copies:
+            copy.start()
+        if half > 2 * part:
+            for i in range(3):
+                table[i * half + 2 * part : (i + 1) * half, :] = jnp.zeros(
+                    (half - 2 * part, width), BF
+                )
+
     if count == 1:
         rows = sources[0]
     else:
-        rows = refs[count + 7]
+        rows = refs[count + 13]
         size = sources[0].shape[0]
         each = rows_per_step // size
         for p in range(count):
@@ -61,16 +76,19 @@
             def _(p=p):
                 rows[(p % each) * size : (p % each + 1) * size, :] = sources[p][...]
 
-    tile = 256 if (2 * half) % 256 == 0 else 128
-
-    def first(j, carry):
-        cols = pl.ds(pl.multiple_of(j * tile, tile), tile)
-        both[:, cols] = jnp.dot(rows[:, :width], wide[:, cols], preferred_element_type=F32)
-        return carry
-
-    lax.fori_loop(0, 2 * half // tile, first, 0)
+    def wait(i, j):
+        @pl.when(step == 0)
+        def _():
+            for copy in copies[i:j]:
+                copy.wait()
+
+    wait(0, 4)
+    both[...] = lax.dot_general(
+        rows[:, :width], table[: 2 * half, :], TRANS, preferred_element_type=F32
+    )
+    wait(4, 6)
     back[...] = lax.dot_general(
-        rows[:, width:], tall[...], (((1,), (1,)), ((), ())), preferred_element_type=F32
+        rows[:, width:], table[2 * half :, :], TRANS, preferred_element_type=F32
     )
     gate, up, dy = both[:, :half], both[:, half:], back[...]
     sig = jax.nn.sigmoid(gate)
@@ -80,24 +98,17 @@
     grads[:, :half] = (dy * up * (sig + active * (1.0 - sig))).astype(BF)
     score = jnp.sum(grad_up * up, -1, keepdims=True)
     joint[...] = jnp.broadcast_to(score, joint.shape)
-    block = 512 if width % 512 == 0 else 128
-
-    def last(j, carry):
-        cols = pl.ds(pl.multiple_of(j * block, block), block)
-        into[:, cols] = lax.dot_general(
-            grads[...], wide[cols, :], (((1,), (1,)), ((), ())), preferred_element_type=F32
-        ).astype(BF)
-        return carry
-
-    lax.fori_loop(0, width // block, last, 0)
-
-
-def hidden_grads(sources, wide, tall, step_rows):
+    into[...] = jnp.dot(
+        grads[...], table[: 2 * half, :], preferred_element_type=F32
+    ).astype(BF)
+
+
+def hidden_grads(sources, pieces, step_rows):
     count = len(sources)
     size = sources[0].shape[0]
     total = count * size
-    half, width = tall.shape
-    steps = total // step_rows
+    part, width = pieces[0].shape
+    half = -(-2 * part // 128) * 128
     if count == 1:
         row_specs = [pl.BlockSpec((step_rows, 2 * width), lambda i: (i, 0))]
         extra = []
@@ -106,14 +117,10 @@
             pl.BlockSpec((size, 2 * width), lambda i: (0, 0), pipeline_mode=pl.Buffered(1))
         ] * count
         extra = [pltpu.VMEM((step_rows, 2 * width), BF)]
-
-    def whole(shape):
-        return pl.BlockSpec(shape, lambda i: (0, 0), pipeline_mode=pl.Buffered(1))
-
     into, joint = pl.pallas_call(
         lambda *refs: hidden_kernel(count, step_rows, *refs),
-        grid=(steps,),
-        in_specs=row_specs + [whole(wide.shape), whole(tall.shape)],
+        grid=(total // step_rows,),
+        in_specs=row_specs + [pl.BlockSpec(memory_space=pl.ANY)] * 6,
         out_specs=[
             pl.BlockSpec((step_rows, width), lambda i: (i, 0)),
             pl.BlockSpec((step_rows, 128), lambda i: (i, 0)),
@@ -123,9 +130,11 @@
             jax.ShapeDtypeStruct((total, 128), F32),
         ],
         scratch_shapes=[
+            pltpu.VMEM((3 * half, width), BF),
             pltpu.VMEM((step_rows, 2 * half), F32),
             pltpu.VMEM((step_rows, half), F32),
             pltpu.VMEM((step_rows, 2 * half), BF),
+            pltpu.SemaphoreType.DMA((6,)),
         ]
         + extra,
         compiler_params=pltpu.CompilerParams(vmem_limit_bytes=VMEM_LIMIT),
@@ -134,37 +143,43 @@
             bytes_accessed=6 * half * width + 6 * total * width,
             transcendentals=total * half,
         ),
-    )(*sources, wide, tall)
+    )(*sources, *pieces)
     return into, joint[:, 0]
 
 
-def pick_kernel(*refs):
-    count = len(refs) // 2
-    total = jnp.dot(refs[0][...], refs[count][...], preferred_element_type=F32)
-    for i in range(1, count):
-        total = total + jnp.dot(refs[i][...], refs[count + i][...], preferred_element_type=F32)
-    refs[-1][...] = total.astype(BF)
-
-
-def pick_rows(tables, sources):
-    rows, tok = tables[0].shape
-    width = sources[0].shape[1]
-    block = 1024 if width % 1024 == 0 else 128
+def pick_kernel(count, *refs):
+    table, sources, out = refs[0], refs[1 : 1 + count], refs[1 + count]
+    if count == 1:
+        rows = sources[0][...]
+    else:
+        tall = refs[2 + count]
+        tok = sources[0].shape[0]
+        for i in range(count):
+            tall[i * tok : (i + 1) * tok, :] = sources[i][...]
+        rows = tall[...]
+    out[...] = jnp.dot(table[...], rows, preferred_element_type=F32).astype(BF)
+
+
+def pick_rows(table, sources, block=1024):
+    rows, depth = table.shape
+    tok, width = sources[0].shape
+    block = block if width % block == 0 else 128
     count = len(sources)
     return pl.pallas_call(
-        pick_kernel,
+        lambda *refs: pick_kernel(count, *refs),
         grid=(width // block,),
-        in_specs=[pl.BlockSpec((rows, tok), lambda i: (0, 0))] * count
+        in_specs=[pl.BlockSpec((rows, depth), lambda i: (0, 0))]
         + [pl.BlockSpec((tok, block), lambda i: (0, i))] * count,
         out_specs=pl.BlockSpec((rows, block), lambda i: (0, i)),
         out_shape=jax.ShapeDtypeStruct((rows, width), BF),
+        scratch_shapes=[pltpu.VMEM((depth, block), BF)] if count > 1 else [],
         compiler_params=pltpu.CompilerParams(vmem_limit_bytes=VMEM_LIMIT),
         cost_estimate=pl.CostEstimate(
-            flops=2 * count * rows * tok * width,
-            bytes_accessed=2 * width * (rows + count * tok),
+            flops=2 * rows * depth * width,
+            bytes_accessed=2 * width * (rows + depth),
             transcendentals=0,
         ),
-    )(*tables, *sources)
+    )(table, *sources)
 
 
 def slots_of(routes, experts):
@@ -229,8 +244,9 @@
 
     peer_routes = {k: receive_from(routes, k) for k in (1, 2, 3)}
     peer = {k: receive_from(pair, k) for k in (1, 2, 3)}
-    own_index = routes * own_rows + slots_of(routes, experts)
-    own = over(pick_rows([picker(own_index, own_all)], [pair]))
+    known = after(routes, *peer_routes.values())
+    own_index = known * own_rows + slots_of(known, experts)
+    own = over(pick_rows(picker(own_index, own_all), [pair]))
 
     far_index = {}
     for k in (1, 2, 3):
@@ -240,29 +256,28 @@
             far_index[k] = row + slots
         else:
             far_index[k] = jnp.where(slots >= NEAR, row + slots - NEAR, none)
-    far_send = pick_rows(
-        [picker(far_index[k], far_all) for k in (1, 2, 3)], [peer[k] for k in (1, 2, 3)]
-    )
+    far_table = jnp.concatenate([far_index[k] for k in (1, 2, 3)], 0)
+    far_send = pick_rows(picker(far_table, far_all), [peer[k] for k in (1, 2, 3)])
     far = over(far_send)
     near_send = own.reshape(experts, own_rows, 2 * width)[:, :NEAR].reshape(near_all, 2 * width)
     near1 = receive_from(near_send, 1)
     near3 = receive_from(near_send, 3)
 
-    wide_e, tall_e = join_weights(expert_gate[0], expert_up[0], expert_down[0])
-    wide_d, tall_d = join_weights(dense_gate, dense_up, dense_down)
+    expert = weight_pieces(expert_gate[0], expert_up[0], expert_down[0])
+    dense = weight_pieces(dense_gate, dense_up, dense_down)
 
     own_into, own_joint = hidden_grads(
-        [after(own, far_send, near_send)], wide_e, tall_e, own_all // 2
+        [after(own, far_send, near_send)], expert, own_all
     )
     dense_part, unused = hidden_grads(
-        [after(pair, own_into)] + [peer[k] for k in (1, 2, 3)], wide_d, tall_d, 2 * tok
+        [after(pair, own_into)] + [peer[k] for k in (1, 2, 3)], dense, 2 * tok
     )
     near_into, near_joint = hidden_grads(
-        [after(near1, dense_part), near3], wide_e, tall_e, near_all
+        [after(near1, dense_part), near3], expert, near_all
     )
     near1_back = send_to(near_into[:near_all], 1)
     near3_back = send_to(near_into[near_all:], 3)
-    far_into, far_joint = hidden_grads([after(far, near_into)], wide_e, tall_e, far_all // 2)
+    far_into, far_joint = hidden_grads([after(far, near_into)], expert, far_all // 2)
     far_back = over(far_into)
 
     own_joint = own_joint.reshape(experts, own_rows)[:, :cap]

time: 516 us -> 457 us (0.89)
  local copies, waits for them, and re-layouts: 98.5 us -> 21.4 us
  waiting for transfers between devices: 173 us -> 221 us
  Pallas kernels: 110 us -> 96.8 us
  starting transfers between devices: 81.6 us -> 69 us
  other arithmetic: 24.8 us -> 18.3 us
    ppermute x8, waiting for transfers between devices: 75.2 us -> 110 us  [receive_from(): lax.ppermute(value, 'y', [(i, (i - k) % PEERS) for i in range(PEERS)])]
    concatenate x3 -> x0, local copies, waits for them, and re-layouts: 34.6 us -> none  [the longest x2 34.5 us: join_weights(): wide = jnp.concatenate([gate, swap(gate), blank, up, swap(up), blank], 1)]
    unnamed x43 -> x28, local copies, waits for them, and re-layouts: 28.4 us -> 6.12 us
    ppermute x4 -> x0, local copies, waits for them, and re-layouts: 17.9 us -> none  [swap(): return lax.ppermute(value, 'core', [(0, 1), (1, 0)])]
    all_to_all x7, waiting for transfers between devices: 23.2 us -> 38.5 us  [over(): return lax.all_to_all(value, axes, split_axis=0, concat_axis=0, tiled=True)]
    pallas_call x4, Pallas kernels: 96.5 us -> 84.4 us  [hidden_grads(): pl.pallas_call(lambda *refs: hidden_kernel(count, step_rows, *refs), grid...]
    all_to_all x7, starting transfers between devices: 60.3 us -> 49.4 us  [over(): return lax.all_to_all(value, axes, split_axis=0, concat_axis=0, tiled=True)]
    concatenate x1, other arithmetic: 6.25 us -> 0.01 us  [body(): far_table = jnp.concatenate([far_index[k] for k in (1, 2, 3)], 0)]
  transfers between devices with their start and end apart: 26 -> 26, of which waited for: 9 -> 13; matrix products, arithmetic and copies ran while one was open for 23% -> 10% of each run, Pallas kernels for 17% -> 16%
where the time goes in v4:
time: 457 us; the launch traced here: 449 us
  waiting for transfers between devices  221 us (48%)
  Pallas kernels  96.8 us (21%)
  starting transfers between devices  69 us (15%)
  local copies, waits for them, and re-layouts  21.4 us (5%)
  matrix products  20.7 us (5%)
  other arithmetic  18.3 us (4%)
    ppermute x8, waiting for transfers between devices, receive_from(): lax.ppermute(value, 'y', [(i, (i - k) % PEERS) for i in range(PEERS)])  110 us
    pallas_call x4, Pallas kernels, hidden_grads(): pl.pallas_call(lambda *refs: hidden_kernel(count, step_rows, *refs), grid...  84.4 us
    ppermute x5, waiting for transfers between devices, send_to(): lax.ppermute(value, 'y', [(i, (i + k) % PEERS) for i in range(PEERS)])  70.9 us
    all_to_all x7, starting transfers between devices, over(): return lax.all_to_all(value, axes, split_axis=0, concat_axis=0, tiled=True)  49.4 us
    all_to_all x7, waiting for transfers between devices, over(): return lax.all_to_all(value, axes, split_axis=0, concat_axis=0, tiled=True)  38.5 us
    pallas_call x2, Pallas kernels, pick_rows(): pl.pallas_call(lambda *refs: pick_kernel(count, *refs), grid=(width // bl...  12.4 us
    ppermute x8, starting transfers between devices, receive_from(): lax.ppermute(value, 'y', [(i, (i - k) % PEERS) for i in range(PEERS)])  9.59 us
  transfers between devices with their start and end apart: 26, of which 13 were waited for; matrix products, arithmetic and copies ran while one was open for 10% of the time, Pallas kernels for 16%

profile of v4, /device:TPU:1, one launch (start us, length us, event | category | flops | bytes accessed | tf_op | source)
XLA Modules:
  0.0 449.3 jit_solution(13826208220499895080)
XLA Ops:
  0.7 3.8 collective-permute-start.1
  4.9 2.3 collective-permute-start
  7.2 1.4 fusion.9
  8.6 1.5 fusion.3
  11.5 2.9 shard_map.130
  14.5 2.4 copy-done.1
  16.9 7.6 %all-to-all-start = ((bf16[16,24,7168]{2,1,0:T(8,128)(2,1)}), bf16[16,24,7168]{2,1,0:T(8,128)(2,1)}, u32[]{:S(2)}, u32[]{:S(2)}) async-start(bf16[16,24,7168]{2,1,0:T(8,128)(2,1)} %bitcast.57), calls=%async_computation | async-start | bytes 11010048 | tf_op jit(solution)/shard_map/all_to_all | solution.py:31
  28.4 36.0 %collective-permute-done.3.refs_1_ = bf16[128,7168]{1,0:T(8,128)(2,1)} collective-permute-done((bf16[128,7168]{1,0:T(8,128)(2,1)S(1)}, bf16[128,7168]{1,0:T(8,128)(2,1)}, u32[]{:S(2)}, u32[]{:S(2)}) %collective-permute-start.3) | collective-permute-done | bytes 1835040 | tf_op jit(solution)/shard_map/ppermute | solution.py:19
  65.1 42.6 %collective-permute-done.5.refs_3_ = bf16[128,7168]{1,0:T(8,128)(2,1)} collective-permute-done((bf16[128,7168]{1,0:T(8,128)(2,1)S(1)}, bf16[128,7168]{1,0:T(8,128)(2,1)}, u32[]{:S(2)}, u32[]{:S(2)}) %collective-permute-start.5) | collective-permute-done | bytes 1835040 | tf_op jit(solution)/shard_map/ppermute | solution.py:19
  107.7 9.5 %shard_map.131 = bf16[512,7168]{1,0:T(8,128)(2,1)} custom-call(bf16[512,384]{1,0:T(8,128)(2,1)S(1)} %fusion.25.refs_0_, bf16[128,7168]{1,0:T(8,128)(2,1)} %collective-permute-done.3.refs_1_, bf16[128,7168]{1,0:T(8,128)(2,1)} %collective-permute-done.4.refs_2_, bf16[128,7168]{1,0:T(8,128)(2,1)} %collective-permute-done.5.refs_3_), custom_call_target="tpu_custom_call" | custom-call | flops 2818572288 | bytes 12845056 | tf_op jit(solution)/shard_map/pallas_call | solution.py:168
  117.2 6.6 %all-to-all-start.1 = ((bf16[16,32,7168]{2,1,0:T(8,128)(2,1)}), bf16[16,32,7168]{2,1,0:T(8,128)(2,1)}, u32[]{:S(2)}, u32[]{:S(2)}) async-start(bf16[16,32,7168]{2,1,0:T(8,128)(2,1)} %bitcast.68), calls=%async_computation.1 | async-start | bytes 14680064 | tf_op jit(solution)/shard_map/all_to_all | solution.py:31
  126.1 2.5 slice.155
  130.1 2.0 fusion.17
  132.9 2.2 collective-permute-done.8.refs_6_.refs_7_
  136.0 2.0 fusion.19
  138.0 2.0 fusion.21
  140.1 17.8 %shard_map.132 = (bf16[384,3584]{1,0:T(8,128)(2,1)}, f32[384,128]{1,0:T(8,128)S(1)}) custom-call(bf16[384,7168]{1,0:T(8,128)(2,1)} %bitcast.3.refs_0_, bf16[304,3584]{1,0:T(8,128)(2,1)S(1)} %bitcast.61, bf16[304,3584]{1,0:T(8,128)(2,1)} %collective-permute-done.6.refs_2_.refs_3_, bf16[304,3584]{1,0:T(8,128)(2,1)S(1)} %bitcast.65, ...), custom_call_target="tpu_custom_call" | custom-call | flops 8808038400 | bytes 22020096 | tf_op jit(solution)/shard_map/pallas_call | solution.py:120
  157.9 22.7 %shard_map.133 = (bf16[512,3584]{1,0:T(8,128)(2,1)}, f32[512,128]{1,0:T(8,128)}) custom-call(bf16[128,7168]{1,0:T(8,128)(2,1)S(1)} %pad_maximum_fusion.refs_1_.refs_0_, bf16[128,7168]{1,0:T(8,128)(2,1)} %collective-permute-done.3.refs_1_, bf16[128,7168]{1,0:T(8,128)(2,1)} %collective-permute-done.4.refs_2_, ...), custom_call_target="tpu_custom_call" | custom-call | flops 11744051200 | bytes 24772608 | tf_op jit(solution)/shard_map/pallas_call | solution.py:120
  180.6 29.0 %collective-permute-done.12.refs_0_ = bf16[256,7168]{1,0:T(8,128)(2,1)} collective-permute-done((bf16[256,7168]{1,0:T(8,128)(2,1)S(1)}, bf16[256,7168]{1,0:T(8,128)(2,1)}, u32[]{:S(2)}, u32[]{:S(2)}) %collective-permute-start.12) | collective-permute-done | bytes 3670048 | tf_op jit(solution)/shard_map/ppermute | solution.py:19
  209.7 1.6 collective-permute-done.13.refs_1_
  211.2 22.5 %shard_map.134 = (bf16[512,3584]{1,0:T(8,128)(2,1)}, f32[512,128]{1,0:T(8,128)S(1)}) custom-call(bf16[256,7168]{1,0:T(8,128)(2,1)} %collective-permute-done.12.refs_0_, bf16[256,7168]{1,0:T(8,128)(2,1)} %collective-permute-done.13.refs_1_, bf16[304,3584]{1,0:T(8,128)(2,1)S(1)} %bitcast.62, bf16[304,3584]{1,0:T(8,128)(2,1)} %collective-permute-done.6.refs_2_.refs_3_, ...), custom_call_target="tpu_custom_call" | custom-call | flops 11744051200 | bytes 24772608 | tf_op jit(solution)/shard_map/pallas_call | solution.py:120
  233.7 17.0 %all-to-all-done.1 = bf16[16,32,7168]{2,1,0:T(8,128)(2,1)} async-done(((bf16[16,32,7168]{2,1,0:T(8,128)(2,1)}), bf16[16,32,7168]{2,1,0:T(8,128)(2,1)}, u32[]{:S(2)}, u32[]{:S(2)}) %all-to-all-start.1) | async-done | bytes 7340064 | tf_op jit(solution)/shard_map/all_to_all | solution.py:31
  250.8 1.6 copy-done.4
  252.4 1.6 copy-done.6
  254.0 21.4 %shard_map.135 = (bf16[512,3584]{1,0:T(8,128)(2,1)}, f32[512,128]{1,0:T(8,128)S(1)}) custom-call(bf16[512,7168]{1,0:T(8,128)(2,1)} %bitcast.17.refs_0_, bf16[304,3584]{1,0:T(8,128)(2,1)S(1)} %bitcast.63, bf16[304,3584]{1,0:T(8,128)(2,1)} %collective-permute-done.6.refs_2_.refs_3_, bf16[304,3584]{1,0:T(8,128)(2,1)S(1)} %bitcast.67, ...), custom_call_target="tpu_custom_call" | custom-call | flops 11744051200 | bytes 24772608 | tf_op jit(solution)/shard_map/pallas_call | solution.py:120
  275.4 8.6 %all-to-all-start.2 = ((bf16[16,32,3584]{2,1,0:T(8,128)(2,1)}), bf16[16,32,3584]{2,1,0:T(8,128)(2,1)}, u32[]{:S(2)}, u32[]{:S(2)}) async-start(bf16[16,32,3584]{2,1,0:T(8,128)(2,1)} %bitcast.70), calls=%async_computation.2 | async-start | bytes 7340032 | tf_op jit(solution)/shard_map/all_to_all | solution.py:31
  284.0 4.1 fusion.57
  288.1 2.7 collective-permute-start.15
  292.9 35.2 %collective-permute-done.14 = bf16[256,3584]{1,0:T(8,128)(2,1)} collective-permute-done((bf16[256,3584]{1,0:T(8,128)(2,1)}, bf16[256,3584]{1,0:T(8,128)(2,1)}, u32[]{:S(2)}, u32[]{:S(2)}) %collective-permute-start.14) | collective-permute-done | bytes 1835040 | tf_op jit(solution)/shard_map/ppermute | solution.py:23
  328.1 4.4 convert_add_fusion.1
  332.5 9.3 %all-to-all-start.3 = ((f32[64,1,20]{2,1,0:T(1,128)}), f32[64,1,20]{2,1,0:T(1,128)S(1)}, u32[]{:S(2)}, u32[]{:S(2)}) async-start(f32[64,1,20]{2,1,0:T(1,128)} %bitcast.25), calls=%async_computation.3 | async-start | bytes 65536 | tf_op jit(solution)/shard_map/all_to_all | solution.py:31
  341.8 5.0 %fusion = bf16[16,24,3584]{2,1,0:T(8,128)(2,1)} fusion(bf16[16,24,3584]{2,1,0:T(8,128)(2,1)} %bitcast.73, f32[16,16,3584]{2,1,0:T(8,128)} %bitcast.69), kind=kLoop, calls=%fused_computation.1 | loop fusion | flops 4128768 | bytes 9175040 | tf_op jit(solution)/shard_map/convert_element_type | solution.py:306
  346.8 3.3 all-to-all-done.3
  350.1 4.5 all-to-all-start.4
  354.8 4.5 add_convert_fusion
  359.3 1.6 fusion.58
  360.9 1.4 collective-permute-start.16
  362.6 2.6 collective-permute-start.18
  366.1 2.9 fusion.44
  369.0 9.7 %collective-permute-done.16 = bf16[128,3584]{1,0:T(8,128)(2,1)S(1)} collective-permute-done((bf16[128,3584]{1,0:T(8,128)(2,1)}, bf16[128,3584]{1,0:T(8,128)(2,1)S(1)}, u32[]{:S(2)}, u32[]{:S(2)}) %collective-permute-start.16) | collective-permute-done | bytes 917536 | tf_op jit(solution)/shard_map/ppermute | solution.py:23
  378.7 26.0 %collective-permute-done.17 = bf16[128,3584]{1,0:T(8,128)(2,1)} collective-permute-done((bf16[128,3584]{1,0:T(8,128)(2,1)}, bf16[128,3584]{1,0:T(8,128)(2,1)}, u32[]{:S(2)}, u32[]{:S(2)}) %collective-permute-start.17) | collective-permute-done | bytes 917536 | tf_op jit(solution)/shard_map/ppermute | solution.py:23
  404.7 5.3 %fusion.12 = (f32[3584]{0:T(1024)S(1)}, f32[128]{0:T(128)}, f32[128,3584]{1,0:T(8,128)S(1)}) fusion(bf16[128,3584]{1,0:T(8,128)(2,1)S(1)} %copy-done.7, f32[128]{0:T(128)S(1)} %add_rsqrt_fusion, f32[3584]{0:T(1024)S(1)} %copy-done.10, bf16[128,3584]{1,0:T(8,128)(2,1)} %collective-permute-done.18, bf16[128,3584]{1,0:T(8,128)(2,1)} %collective-permute-done.17, ...), kind=kOutput, calls=%fused_computation.19 | convolution fusion | flops 359657856 | bytes 11138048 | tf_op jit(solution)/shard_map/dot_general | solution.py:333
  410.0 1.1 all_to_all.65
  411.2 8.0 %all-to-all-start.5 = ((f32[128,1,476]{2,1,0:T(1,128)}), f32[128,1,476]{2,1,0:T(1,128)S(1)}, u32[]{:S(2)}, u32[]{:S(2)}) async-start(f32[128,1,476]{2,1,0:T(1,128)} %all_to_all.65), calls=%async_computation.5 | async-start | bytes 524288 | tf_op jit(solution)/shard_map/all_to_all | solution.py:31
  419.8 10.1 %all-to-all-done.5 = f32[128,1,476]{2,1,0:T(1,128)S(1)} async-done(((f32[128,1,476]{2,1,0:T(1,128)}), f32[128,1,476]{2,1,0:T(1,128)S(1)}, u32[]{:S(2)}, u32[]{:S(2)}) %all-to-all-start.5) | async-done | bytes 243744 | tf_op jit(solution)/shard_map/all_to_all | solution.py:31
  431.0 4.8 %all-to-all-start.6 = ((f32[128,1,476]{2,1,0:T(1,128)}), f32[128,1,476]{2,1,0:T(1,128)S(1)}, u32[]{:S(2)}, u32[]{:S(2)}) async-start(f32[128,1,476]{2,1,0:T(1,128)} %broadcast_in_dim.152), calls=%async_computation.6 | async-start | bytes 524288 | tf_op jit(solution)/shard_map/all_to_all | solution.py:31
  435.8 2.7 fusion.8
  438.5 8.0 %all-to-all-done.6 = f32[128,1,476]{2,1,0:T(1,128)S(1)} async-done(((f32[128,1,476]{2,1,0:T(1,128)}), f32[128,1,476]{2,1,0:T(1,128)S(1)}, u32[]{:S(2)}, u32[]{:S(2)}) %all-to-all-start.6) | async-done | bytes 243744 | tf_op jit(solution)/shard_map/all_to_all | solution.py:31
  (136 shorter events, 19.2 us)
Async XLA Ops:
  0.6 124.5 %copy-start = (f32[3584,16]{0,1:T(8,128)S(1)}, f32[3584,16]{0,1:T(8,128)}, u32[]{:S(2)}) copy-start(f32[3584,16]{0,1:T(8,128)} %param.14) | copy-start | bytes 688132
  0.6 9.4 %copy-start.8 = (bf16[128,3584]{1,0:T(8,128)(2,1)S(1)}, bf16[128,3584]{1,0:T(8,128)(2,1)}, u32[]{:S(2)}) copy-start(bf16[128,3584]{1,0:T(8,128)(2,1)} %param.12) | copy-start | bytes 2752516
  0.7 9.6 %collective-permute-start.1 = (s32[128,2]{0,1:T(2,128)}, s32[128,2]{0,1:T(2,128)S(1)}, u32[]{:S(2)}, u32[]{:S(2)}) collective-permute-start(s32[128,2]{0,1:T(2,128)} %param.21), channel_id=1, source_target_pairs={{0,4},{2,6},{4,0},{6,2},{1,5},{3,7},{5,1},{7,3},{8,12},{10,14},{12... | collective-permute-start | bytes 3080 | tf_op jit(solution)/shard_map/ppermute | solution.py:19
  4.5 5.8 %collective-permute-start.2 = (s32[128,2]{0,1:T(2,128)}, s32[128,2]{0,1:T(2,128)S(1)}, u32[]{:S(2)}, u32[]{:S(2)}) collective-permute-start(s32[128,2]{0,1:T(2,128)} %param.21), channel_id=1, source_target_pairs={{0,2},{2,4},{4,6},{6,0},{1,3},{3,5},{5,7},{7,1},{8,10},{10,12},{12... | collective-permute-start | bytes 3080 | tf_op jit(solution)/shard_map/ppermute | solution.py:19
  4.9 5.4 %collective-permute-start = (s32[128,2]{0,1:T(2,128)}, s32[128,2]{0,1:T(2,128)S(1)}, u32[]{:S(2)}, u32[]{:S(2)}) collective-permute-start(s32[128,2]{0,1:T(2,128)} %param.21), channel_id=1, source_target_pairs={{0,6},{2,0},{4,2},{6,4},{1,7},{3,1},{5,3},{7,5},{8,14},{10,8},{12,... | collective-permute-start | bytes 3080 | tf_op jit(solution)/shard_map/ppermute | solution.py:19
  8.6 396.0 %copy-start.12 = (f32[128]{0:T(128)}, f32[128]{0:T(128)S(1)}, u32[]{:S(2)}) copy-start(f32[128]{0:T(128)S(1)} %add_rsqrt_fusion) | copy-start | bytes 1540
  10.1 0.7 copy-start.11
  14.5 2.4 copy-start.1
  16.9 100.3 %all-to-all-start = ((bf16[16,24,7168]{2,1,0:T(8,128)(2,1)}), bf16[16,24,7168]{2,1,0:T(8,128)(2,1)}, u32[]{:S(2)}, u32[]{:S(2)}) async-start(bf16[16,24,7168]{2,1,0:T(8,128)(2,1)} %bitcast.57), calls=%async_computation | async-start | bytes 11010048 | tf_op jit(solution)/shard_map/all_to_all | solution.py:31
  24.5 39.9 %collective-permute-start.3 = (bf16[128,7168]{1,0:T(8,128)(2,1)S(1)}, bf16[128,7168]{1,0:T(8,128)(2,1)}, u32[]{:S(2)}, u32[]{:S(2)}) collective-permute-start(bf16[128,7168]{1,0:T(8,128)(2,1)S(1)} %pad_maximum_fusion.refs_1_.refs_0_), channel_id=1, source_target_pairs={{0,6},{2,0},{4,2},{6,4},{1,7},{3,1},{5,3},{7,5},{8,14},{10,8},{12,... | collective-permute-start | bytes 5505032 | tf_op jit(solution)/shard_map/ppermute | solution.py:19
  24.8 40.3 %collective-permute-start.4 = (bf16[128,7168]{1,0:T(8,128)(2,1)S(1)}, bf16[128,7168]{1,0:T(8,128)(2,1)}, u32[]{:S(2)}, u32[]{:S(2)}) collective-permute-start(bf16[128,7168]{1,0:T(8,128)(2,1)S(1)} %pad_maximum_fusion.refs_1_.refs_0_), channel_id=1, source_target_pairs={{0,4},{2,6},{4,0},{6,2},{1,5},{3,7},{5,1},{7,3},{8,12},{10,14},{12... | collective-permute-start | bytes 5505032 | tf_op jit(solution)/shard_map/ppermute | solution.py:19
  25.6 82.1 %collective-permute-start.5 = (bf16[128,7168]{1,0:T(8,128)(2,1)S(1)}, bf16[128,7168]{1,0:T(8,128)(2,1)}, u32[]{:S(2)}, u32[]{:S(2)}) collective-permute-start(bf16[128,7168]{1,0:T(8,128)(2,1)S(1)} %pad_maximum_fusion.refs_1_.refs_0_), channel_id=1, source_target_pairs={{0,2},{2,4},{4,6},{6,0},{1,3},{3,5},{5,7},{7,1},{8,10},{10,12},{12... | collective-permute-start | bytes 5505032 | tf_op jit(solution)/shard_map/ppermute | solution.py:19
  117.2 133.6 %all-to-all-start.1 = ((bf16[16,32,7168]{2,1,0:T(8,128)(2,1)}), bf16[16,32,7168]{2,1,0:T(8,128)(2,1)}, u32[]{:S(2)}, u32[]{:S(2)}) async-start(bf16[16,32,7168]{2,1,0:T(8,128)(2,1)} %bitcast.68), calls=%async_computation.1 | async-start | bytes 14680064 | tf_op jit(solution)/shard_map/all_to_all | solution.py:31
  123.8 8.3 %collective-permute-start.6 = (bf16[304,3584]{1,0:T(8,128)(2,1)}, bf16[304,3584]{1,0:T(8,128)(2,1)}, u32[]{:S(2)}, u32[]{:S(2)}) collective-permute-start(bf16[304,3584]{1,0:T(8,128)(2,1)} %bitcast.60), channel_id=1, source_target_pairs={{0,1},{1,0},{2,3},{3,2},{4,5},{5,4},{6,7},{7,6},{8,9},{9,8},{10,11... | collective-permute-start | bytes 6537224 | tf_op jit(solution)/shard_map/ppermute | solution.py:27
  124.6 8.2 %collective-permute-start.7 = (bf16[304,3584]{1,0:T(8,128)(2,1)}, bf16[304,3584]{1,0:T(8,128)(2,1)}, u32[]{:S(2)}, u32[]{:S(2)}) collective-permute-start(bf16[304,3584]{1,0:T(8,128)(2,1)} %bitcast.64), channel_id=1, source_target_pairs={{0,1},{1,0},{2,3},{3,2},{4,5},{5,4},{6,7},{7,6},{8,9},{9,8},{10,11... | collective-permute-start | bytes 6537224 | tf_op jit(solution)/shard_map/ppermute | solution.py:27
  124.7 10.4 %collective-permute-start.8 = (bf16[304,3584]{1,0:T(8,128)(2,1)}, bf16[304,3584]{1,0:T(8,128)(2,1)}, u32[]{:S(2)}, u32[]{:S(2)}) collective-permute-start(bf16[304,3584]{1,0:T(8,128)(2,1)} %bitcast.75), channel_id=1, source_target_pairs={{0,1},{1,0},{2,3},{3,2},{4,5},{5,4},{6,7},{7,6},{8,9},{9,8},{10,11... | collective-permute-start | bytes 6537224 | tf_op jit(solution)/shard_map/ppermute | solution.py:27
  126.1 6.8 %copy-start.2 = (bf16[3584,304]{0,1:T(8,128)(2,1)S(1)}, bf16[3584,304]{0,1:T(8,128)(2,1)}, u32[]{:S(2)}) copy-start(bf16[3584,304]{0,1:T(8,128)(2,1)} %param.15) | copy-start | bytes 6537220
  126.1 14.0 %copy-start.5 = (bf16[1,3584,304]{1,2,0:T(8,128)(2,1)S(1)}, bf16[1,3584,304]{1,2,0:T(8,128)(2,1)}, u32[]{:S(2)}) copy-start(bf16[1,3584,304]{1,2,0:T(8,128)(2,1)} %param.19) | copy-start | bytes 6537220
  128.6 11.5 %copy-start.3 = (bf16[1,3584,304]{1,2,0:T(8,128)(2,1)S(1)}, bf16[1,3584,304]{1,2,0:T(8,128)(2,1)}, u32[]{:S(2)}) copy-start(bf16[1,3584,304]{1,2,0:T(8,128)(2,1)} %param.18) | copy-start | bytes 6537220
  128.6 81.1 %collective-permute-start.12 = (bf16[256,7168]{1,0:T(8,128)(2,1)S(1)}, bf16[256,7168]{1,0:T(8,128)(2,1)}, u32[]{:S(2)}, u32[]{:S(2)}) collective-permute-start(bf16[256,7168]{1,0:T(8,128)(2,1)S(1)} %bitcast.71), channel_id=1, source_target_pairs={{0,6},{2,0},{4,2},{6,4},{1,7},{3,1},{5,3},{7,5},{8,14},{10,8},{12,... | collective-permute-start | bytes 11010056 | tf_op jit(solution)/shard_map/ppermute | solution.py:19
  129.3 81.9 %collective-permute-start.13 = (bf16[256,7168]{1,0:T(8,128)(2,1)S(1)}, bf16[256,7168]{1,0:T(8,128)(2,1)}, u32[]{:S(2)}, u32[]{:S(2)}) collective-permute-start(bf16[256,7168]{1,0:T(8,128)(2,1)S(1)} %bitcast.72), channel_id=1, source_target_pairs={{0,2},{2,4},{4,6},{6,0},{1,3},{3,5},{5,7},{7,1},{8,10},{10,12},{12... | collective-permute-start | bytes 11010056 | tf_op jit(solution)/shard_map/ppermute | solution.py:19
  132.1 25.8 %collective-permute-start.10 = (bf16[304,3584]{1,0:T(8,128)(2,1)}, bf16[304,3584]{1,0:T(8,128)(2,1)}, u32[]{:S(2)}, u32[]{:S(2)}) collective-permute-start(bf16[304,3584]{1,0:T(8,128)(2,1)} %bitcast.13.refs_6_), channel_id=1, source_target_pairs={{0,1},{1,0},{2,3},{3,2},{4,5},{5,4},{6,7},{7,6},{8,9},{9,8},{10,11... | collective-permute-start | bytes 6537224 | tf_op jit(solution)/shard_map/ppermute | solution.py:27
  132.8 25.1 %collective-permute-start.9 = (bf16[304,3584]{1,0:T(8,128)(2,1)S(1)}, bf16[304,3584]{1,0:T(8,128)(2,1)}, u32[]{:S(2)}, u32[]{:S(2)}) collective-permute-start(bf16[304,3584]{1,0:T(8,128)(2,1)S(1)} %bitcast.58), channel_id=1, source_target_pairs={{0,1},{1,0},{2,3},{3,2},{4,5},{5,4},{6,7},{7,6},{8,9},{9,8},{10,11... | collective-permute-start | bytes 6537224 | tf_op jit(solution)/shard_map/ppermute | solution.py:27
  135.1 22.8 %collective-permute-start.11 = (bf16[304,3584]{1,0:T(8,128)(2,1)}, bf16[304,3584]{1,0:T(8,128)(2,1)}, u32[]{:S(2)}, u32[]{:S(2)}) collective-permute-start(bf16[304,3584]{1,0:T(8,128)(2,1)} %refs_8_.1), channel_id=1, source_target_pairs={{0,1},{1,0},{2,3},{3,2},{4,5},{5,4},{6,7},{7,6},{8,9},{9,8},{10,11... | collective-permute-start | bytes 6537224 | tf_op jit(solution)/shard_map/ppermute | solution.py:27
  250.7 1.6 copy-start.4
  252.4 1.6 copy-start.6
  275.4 57.1 %all-to-all-start.2 = ((bf16[16,32,3584]{2,1,0:T(8,128)(2,1)}), bf16[16,32,3584]{2,1,0:T(8,128)(2,1)}, u32[]{:S(2)}, u32[]{:S(2)}) async-start(bf16[16,32,3584]{2,1,0:T(8,128)(2,1)} %bitcast.70), calls=%async_computation.2 | async-start | bytes 7340032 | tf_op jit(solution)/shard_map/all_to_all | solution.py:31
  288.1 40.0 %collective-permute-start.14 = (bf16[256,3584]{1,0:T(8,128)(2,1)}, bf16[256,3584]{1,0:T(8,128)(2,1)}, u32[]{:S(2)}, u32[]{:S(2)}) collective-permute-start(bf16[256,3584]{1,0:T(8,128)(2,1)} %get-tuple-element.46), channel_id=1, source_target_pairs={{0,2},{2,4},{4,6},{6,0},{1,3},{3,5},{5,7},{7,1},{8,10},{10,12},{12... | collective-permute-start | bytes 5505032 | tf_op jit(solution)/shard_map/ppermute | solution.py:23
  288.1 40.0 %collective-permute-start.15 = (bf16[256,3584]{1,0:T(8,128)(2,1)}, bf16[256,3584]{1,0:T(8,128)(2,1)}, u32[]{:S(2)}, u32[]{:S(2)}) collective-permute-start(bf16[256,3584]{1,0:T(8,128)(2,1)} %get-tuple-element.47), channel_id=1, source_target_pairs={{0,6},{2,0},{4,2},{6,4},{1,7},{3,1},{5,3},{7,5},{8,14},{10,8},{12,... | collective-permute-start | bytes 5505032 | tf_op jit(solution)/shard_map/ppermute | solution.py:23
  332.5 17.7 %all-to-all-start.3 = ((f32[64,1,20]{2,1,0:T(1,128)}), f32[64,1,20]{2,1,0:T(1,128)S(1)}, u32[]{:S(2)}, u32[]{:S(2)}) async-start(f32[64,1,20]{2,1,0:T(1,128)} %bitcast.25), calls=%async_computation.3 | async-start | bytes 65536 | tf_op jit(solution)/shard_map/all_to_all | solution.py:31
  350.1 54.5 %all-to-all-start.4 = ((bf16[16,24,3584]{2,1,0:T(8,128)(2,1)}), bf16[16,24,3584]{2,1,0:T(8,128)(2,1)}, u32[]{:S(2)}, u32[]{:S(2)}) async-start(bf16[16,24,3584]{2,1,0:T(8,128)(2,1)} %fusion), calls=%async_computation.4 | async-start | bytes 5505024 | tf_op jit(solution)/shard_map/all_to_all | solution.py:31
  360.9 43.8 %copy-start.7 = (bf16[128,3584]{1,0:T(8,128)(2,1)S(1)}, bf16[128,3584]{1,0:T(8,128)(2,1)}, u32[]{:S(2)}) copy-start(bf16[128,3584]{1,0:T(8,128)(2,1)} %param.11) | copy-start | bytes 2752516
  360.9 43.8 %copy-start.10 = (f32[3584]{0:T(1024)S(1)}, f32[3584]{0:T(1024)}, u32[]{:S(2)}) copy-start(f32[3584]{0:T(1024)} %param.13) | copy-start | bytes 43012
  360.9 17.8 %collective-permute-start.16 = (bf16[128,3584]{1,0:T(8,128)(2,1)}, bf16[128,3584]{1,0:T(8,128)(2,1)S(1)}, u32[]{:S(2)}, u32[]{:S(2)}) collective-permute-start(bf16[128,3584]{1,0:T(8,128)(2,1)} %get-tuple-element.48), channel_id=1, source_target_pairs={{0,4},{2,6},{4,0},{6,2},{1,5},{3,7},{5,1},{7,3},{8,12},{10,14},{12... | collective-permute-start | bytes 2752520 | tf_op jit(solution)/shard_map/ppermute | solution.py:23
  362.3 42.3 %collective-permute-start.17 = (bf16[128,3584]{1,0:T(8,128)(2,1)}, bf16[128,3584]{1,0:T(8,128)(2,1)}, u32[]{:S(2)}, u32[]{:S(2)}) collective-permute-start(bf16[128,3584]{1,0:T(8,128)(2,1)} %get-tuple-element.50), channel_id=1, source_target_pairs={{0,2},{2,4},{4,6},{6,0},{1,3},{3,5},{5,7},{7,1},{8,10},{10,12},{12... | collective-permute-start | bytes 2752520 | tf_op jit(solution)/shard_map/ppermute | solution.py:23
  362.6 42.1 %collective-permute-start.18 = (bf16[128,3584]{1,0:T(8,128)(2,1)}, bf16[128,3584]{1,0:T(8,128)(2,1)}, u32[]{:S(2)}, u32[]{:S(2)}) collective-permute-start(bf16[128,3584]{1,0:T(8,128)(2,1)} %get-tuple-element.49), channel_id=1, source_target_pairs={{0,6},{2,0},{4,2},{6,4},{1,7},{3,1},{5,3},{7,5},{8,14},{10,8},{12,... | collective-permute-start | bytes 2752520 | tf_op jit(solution)/shard_map/ppermute | solution.py:23
  378.7 26.0 %copy-start.9 = (bf16[128,3584]{1,0:T(8,128)(2,1)}, bf16[128,3584]{1,0:T(8,128)(2,1)S(1)}, u32[]{:S(2)}) copy-start(bf16[128,3584]{1,0:T(8,128)(2,1)S(1)} %collective-permute-done.16) | copy-start | bytes 2752516
  410.0 25.7 %copy-start.13 = (f32[128]{0:T(128)S(1)}, f32[128]{0:T(128)}, u32[]{:S(2)}) copy-start(f32[128]{0:T(128)} %copy-done.12) | copy-start | bytes 1540
  411.2 18.8 %all-to-all-start.5 = ((f32[128,1,476]{2,1,0:T(1,128)}), f32[128,1,476]{2,1,0:T(1,128)S(1)}, u32[]{:S(2)}, u32[]{:S(2)}) async-start(f32[128,1,476]{2,1,0:T(1,128)} %all_to_all.65), calls=%async_computation.5 | async-start | bytes 524288 | tf_op jit(solution)/shard_map/all_to_all | solution.py:31
  431.0 15.5 %all-to-all-start.6 = ((f32[128,1,476]{2,1,0:T(1,128)}), f32[128,1,476]{2,1,0:T(1,128)S(1)}, u32[]{:S(2)}, u32[]{:S(2)}) async-start(f32[128,1,476]{2,1,0:T(1,128)} %broadcast_in_dim.152), calls=%async_computation.6 | async-start | bytes 524288 | tf_op jit(solution)/shard_map/all_to_all | solution.py:31

commit v5 on v4

v5 whole, which is shorter than its diff:
```python
import jax
import jax.numpy as jnp
from jax import lax
from jax.experimental import pallas as pl
from jax.experimental.pallas import tpu as pltpu
from jax.sharding import Mesh, PartitionSpec as P

EPS = 1e-05
BF = jnp.bfloat16
F32 = jnp.float32
HIGHEST = lax.Precision.HIGHEST
PEERS = 4
VMEM_LIMIT = 50 * 1024 * 1024
TRANS = (((1,), (1,)), ((), ()))


def receive_from(value, k):
    return lax.ppermute(value, "y", [(i, (i - k) % PEERS) for i in range(PEERS)])


def send_to(value, k):
    return lax.ppermute(value, "y", [(i, (i + k) % PEERS) for i in range(PEERS)])


def swap(value):
    return lax.ppermute(value, "core", [(0, 1), (1, 0)])


def over(value, axes="ep"):
    return lax.all_to_all(value, axes, split_axis=0, concat_axis=0, tiled=True)


def after(value, *others):
    return lax.optimization_barrier((value,) + others)[0]


def weight_pieces(gate, up, down):
    both = [gate.T, up.T, down]
    return [piece for value in both for piece in (value, swap(value))]


def shuffle_table(cap, group):
    size = 2 * group * cap
    row = lax.broadcasted_iota(jnp.int32, (size, size), 0)
    col = lax.broadcasted_iota(jnp.int32, (size, size), 1)
    part, left = row // (group * cap), row % (group * cap)
    return (col == left // cap * (2 * cap) + part * cap + left % cap).astype(BF)


def hidden_kernel(count, mixed, *refs):
    sources = refs[:count]
    pieces = refs[count : count + 6]
    refs = refs[count + 6 :]
    if mixed:
        table, table_back = refs[:2]
        refs = refs[2:]
    into, joint, weights, normed, other, both, back, grads, sems = refs
    step = pl.program_id(0)
    part, width = pieces[0].shape
    half = weights.shape[0] // 3
    copies = []
    for i in range(6):
        start = i // 2 * half + i % 2 * part
        copies.append(
            pltpu.make_async_copy(pieces[i], weights.at[pl.ds(start, part), :], sems.at[i])
        )

    @pl.when(step == 0)
    def _():
        for copy in copies:
            copy.start()
        if half > 2 * part:
            for i in range(3):
                weights[i * half + 2 * part : (i + 1) * half, :] = jnp.zeros(
                    (half - 2 * part, width), BF
                )

    size = sources[0].shape[0] // 2
    each = normed.shape[0] // size
    for p in range(count):

        @pl.when(step == p // each)
        def _(p=p):
            if mixed:
                chunk = table.shape[0]
                for i in range(2 * size // chunk):
                    got = jnp.dot(
                        table[...],
                        sources[p][i * chunk : (i + 1) * chunk, :],
                        preferred_element_type=F32,
                    ).astype(BF)
                    at = slice(i * chunk // 2, (i + 1) * chunk // 2)
                    normed[at, :] = got[: chunk // 2]
                    other[at, :] = got[chunk // 2 :]
            else:
                at = slice((p % each) * size, (p % each + 1) * size)
                normed[at, :] = sources[p][:size, :]
                other[at, :] = sources[p][size:, :]

    def wait(i, j):
        @pl.when(step == 0)
        def _():
            for copy in copies[i:j]:
                copy.wait()

    wait(0, 4)
    both[...] = lax.dot_general(
        normed[...], weights[: 2 * half, :], TRANS, preferred_element_type=F32
    )
    wait(4, 6)
    back[...] = lax.dot_general(
        other[...], weights[2 * half :, :], TRANS, preferred_element_type=F32
    )
    gate, up, dy = both[:, :half], both[:, half:], back[...]
    sig = jax.nn.sigmoid(gate)
    active = gate * sig
    grad_up = dy * active
    grads[:, half:] = grad_up.astype(BF)
    grads[:, :half] = (dy * up * (sig + active * (1.0 - sig))).astype(BF)
    score = jnp.sum(grad_up * up, -1, keepdims=True)
    joint[...] = jnp.broadcast_to(score, joint.shape)
    if mixed:
        other[...] = jnp.dot(
            grads[...], weights[: 2 * half, :], preferred_element_type=F32
        ).astype(BF)
        chunk = table.shape[0]
        for i in range(2 * size // chunk):
            at = slice(i * chunk // 2, (i + 1) * chunk // 2)
            sides = jnp.concatenate([other[at, : width // 2], other[at, width // 2 :]], 0)
            into[i * chunk : (i + 1) * chunk, :] = jnp.dot(
                table_back[...], sides, preferred_element_type=F32
            ).astype(BF)
    else:
        into[...] = jnp.dot(
            grads[...], weights[: 2 * half, :], preferred_element_type=F32
        ).astype(BF)


def hidden_grads(sources, pieces, tables=()):
    count = len(sources)
    mixed = len(tables) > 0
    size = sources[0].shape[0] // 2
    part, width = pieces[0].shape
    half = -(-2 * part // 128) * 128
    step_rows = size if mixed else 2 * size
    total = count * size
    out = (2 * total, width // 2) if mixed else (total, width)
    block = (2 * step_rows, width // 2) if mixed else (step_rows, width)

    def whole(value):
        return pl.BlockSpec(value.shape, lambda i: (0, 0), pipeline_mode=pl.Buffered(1))

    into, joint = pl.pallas_call(
        lambda *refs: hidden_kernel(count, mixed, *refs),
        grid=(total // step_rows,),
        in_specs=[whole(v) for v in sources]
        + [pl.BlockSpec(memory_space=pl.ANY)] * 6
        + [whole(v) for v in tables],
        out_specs=[
            pl.BlockSpec(block, lambda i: (i, 0)),
            pl.BlockSpec((step_rows, 128), lambda i: (i, 0)),
        ],
        out_shape=[jax.ShapeDtypeStruct(out, BF), jax.ShapeDtypeStruct((total, 128), F32)],
        scratch_shapes=[
            pltpu.VMEM((3 * half, width), BF),
            pltpu.VMEM((step_rows, width), BF),
            pltpu.VMEM((step_rows, width), BF),
            pltpu.VMEM((step_rows, 2 * half), F32),
            pltpu.VMEM((step_rows, half), F32),
            pltpu.VMEM((step_rows, 2 * half), BF),
            pltpu.SemaphoreType.DMA((6,)),
        ],
        compiler_params=pltpu.CompilerParams(vmem_limit_bytes=VMEM_LIMIT),
        cost_estimate=pl.CostEstimate(
            flops=10 * total * width * half,
            bytes_accessed=6 * half * width + 6 * total * width,
            transcendentals=total * half,
        ),
    )(*sources, *pieces, *tables)
    return into, joint[:, 0]


def pick_kernel(table, rows, out):
    out[...] = jnp.dot(table[...], rows[...], preferred_element_type=F32).astype(BF)


def pick_rows(table, source):
    rows, depth = table.shape
    width = source.shape[1]
    block = 512 if width % 512 == 0 else 128
    return pl.pallas_call(
        pick_kernel,
        grid=(width // block,),
        in_specs=[
            pl.BlockSpec((rows, depth), lambda i: (0, 0)),
            pl.BlockSpec((depth, block), lambda i: (0, i)),
        ],
        out_specs=pl.BlockSpec((rows, block), lambda i: (0, i)),
        out_shape=jax.ShapeDtypeStruct((rows, width), BF),
        compiler_params=pltpu.CompilerParams(vmem_limit_bytes=VMEM_LIMIT),
        cost_estimate=pl.CostEstimate(
            flops=2 * rows * depth * width,
            bytes_accessed=2 * width * (rows + depth),
            transcendentals=0,
        ),
    )(table, source)


def slots_of(routes, experts):
    tok = routes.shape[0]
    flat = routes.reshape(2 * tok, 1)
    hits = (flat == lax.broadcasted_iota(jnp.int32, (1, experts), 1)).astype(BF)
    place = lax.broadcasted_iota(jnp.int32, (2 * tok, 2 * tok), 0)
    before = (lax.broadcasted_iota(jnp.int32, (2 * tok, 2 * tok), 1) < place).astype(BF)
    places = jnp.dot(before, hits, preferred_element_type=F32)
    return jnp.sum(hits.astype(F32) * places, -1).astype(jnp.int32).reshape(tok, 2)


def spread(index, rows):
    return index[..., None] == lax.broadcasted_iota(jnp.int32, (1, 1, rows), 2)


def picker(index, rows):
    hits = lax.broadcasted_iota(jnp.int32, (rows, 1), 0)
    return (hits == index[:, 0][None]).astype(BF) + (hits == index[:, 1][None]).astype(BF)


def router_weights(normed, router, chosen):
    logits = jnp.dot(normed.astype(F32), router, precision=HIGHEST)
    picked = jnp.sum(jnp.where(chosen, logits[:, None, :], 0.0), -1)
    one = jax.nn.sigmoid(picked[:, 0:1] - picked[:, 1:2])
    return jnp.concatenate([one, 1.0 - one], 1)


def mix(index, weights, rows, cap):
    count = rows.shape[0]
    tables = []
    for shift in (0, cap):
        hot = spread(index + shift, count)
        tables.append(jnp.sum(jnp.where(hot, weights[..., None], 0.0), 1).astype(BF))
    tok = index.shape[0]
    sides = jnp.dot(jnp.concatenate(tables, 0), rows, preferred_element_type=F32)
    return jnp.concatenate([sides[:tok], sides[tok:]], 1)


def body(
    tokens,
    cotangent,
    norm_gain,
    router,
    dense_gate,
    dense_up,
    dense_down,
    expert_gate,
    expert_up,
    expert_down,
    routes,
):
    tok, width = tokens.shape
    experts = router.shape[1]
    cap = 5 * tok // (2 * experts)
    block = 2 * cap
    everything = experts * block

    values = tokens.astype(F32)
    inverse = lax.rsqrt(jnp.mean(values * values, -1, keepdims=True) + EPS)
    normed = (values * inverse * norm_gain).astype(BF)
    pair = jnp.concatenate([normed, cotangent], 0)

    routes_in = after(routes, pair)
    peer_routes = {k: receive_from(routes_in, k) for k in (1, 2, 3)}
    peer = {k: receive_from(pair, k) for k in (1, 2, 3)}

    def to_experts(rows, index):
        places = jnp.concatenate([index, index + cap], 0)
        return over(pick_rows(picker(places, everything), rows))

    known = after(routes, *peer_routes.values())
    own_index = known * block + slots_of(known, experts)
    far_index = peer_routes[2] * block + slots_of(peer_routes[2], experts)
    own = to_experts(pair, own_index)
    far = to_experts(peer[2], far_index)
    near1 = receive_from(own, 1)
    near3 = receive_from(own, 3)

    expert = weight_pieces(expert_gate[0], expert_up[0], expert_down[0])
    dense = weight_pieces(dense_gate, dense_up, dense_down)
    table = shuffle_table(cap, experts // 2)
    tables = (table, table.T)

    own_into, own_joint = hidden_grads([own], expert, tables)
    dense_part, unused = hidden_grads(
        [after(pair, own_into)] + [peer[k] for k in (1, 2, 3)], dense
    )
    far_into, far_joint = hidden_grads([after(far, dense_part)], expert, tables)
    far_back = over(far_into)
    near_into, near_joint = hidden_grads([after(near1, far_into), near3], expert, tables)
    home1 = send_to(after(dense_part[tok : 2 * tok], near1), 1)
    home3 = send_to(after(dense_part[3 * tok :], near3), 3)
    near_into = after(near_into, home1, home3)
    near1_back = send_to(near_into[:everything], 1)
    near3_back = send_to(near_into[everything:], 3)

    joints = jnp.stack(
        [
            own_joint.reshape(experts, cap),
            near_joint[: experts * cap].reshape(experts, cap),
            far_joint.reshape(experts, cap),
            near_joint[experts * cap :].reshape(experts, cap),
        ],
        1,
    )
    plane = lax.broadcasted_iota(jnp.int32, (1, PEERS, PEERS, 1), 1)
    offset = lax.broadcasted_iota(jnp.int32, (1, PEERS, PEERS, 1), 2)
    meant = plane == (lax.axis_index("y") + offset) % PEERS
    joints = jnp.sum(jnp.where(meant, joints[:, None], 0.0), 2).reshape(experts * PEERS, cap)
    joints = over(after(joints, far_back), ("ep", "y"))
    score = jnp.sum(joints.reshape(experts, PEERS, cap), 1)

    own_sum = own_into.astype(F32) + near1_back.astype(F32) + near3_back.astype(F32)
    own_back = over(after(own_sum.astype(BF), joints))

    ids = lax.broadcasted_iota(jnp.int32, (1, 1, experts), 2)
    chosen = routes[..., None] == ids
    weights = router_weights(normed, router, chosen)
    far_weights = router_weights(peer[2][:tok], router, peer_routes[2][..., None] == ids)
    mixed = dense_part[2 * tok : 3 * tok].astype(F32)
    mixed = mixed + mix(far_index, far_weights, far_back, cap)
    home2 = send_to(mixed.astype(BF), 2)

    scores = jnp.sum(
        jnp.where(
            spread(routes * cap + own_index - routes * block, experts * cap),
            score.reshape(1, 1, -1),
            0.0,
        ),
        -1,
    )
    delta = weights[:, 0] * weights[:, 1] * (scores[:, 0] - scores[:, 1])
    signed = chosen[:, 0].astype(F32) - chosen[:, 1].astype(F32)
    grad_logits = signed * delta[:, None]
    local_router = lax.dot_general(
        grad_logits, normed.astype(F32), (((0,), (0,)), ((), ())), precision=HIGHEST
    )
    early = dense_part[:tok].astype(F32)
    early = early + jnp.dot(grad_logits, router.T, precision=HIGHEST)
    for piece in (home1, home3):
        early = early + piece.astype(F32)

    total = early + home2.astype(F32) + mix(own_index, weights, own_back, cap)
    local_gain = jnp.sum(total * values * inverse, 0, keepdims=True)
    axes = ("ep", "y", "core")
    devices = lax.axis_size(axes)
    local = jnp.concatenate([local_router, local_gain], 0).reshape(devices, -1)
    mine = jnp.sum(over(local, axes), 0, keepdims=True)
    sums = over(jnp.broadcast_to(mine, local.shape), axes).reshape(experts + 1, width)
    scaled = total * norm_gain
    mean_term = jnp.mean(scaled * values, -1, keepdims=True)
    input_grad = cotangent.astype(F32) + inverse * (
        scaled - values * inverse * inverse * mean_term
    )
    return (input_grad.astype(BF), sums[experts], sums[:experts].T)


def solution(mesh):
    ep, sp = mesh.devices.shape
    grid = Mesh(mesh.devices.reshape(ep, sp // 2, 2), ("ep", "y", "core"))
    shared = ("y", "core")
    rows = ("ep", "y", "core")
    return jax.shard_map(
        body,
        mesh=grid,
        in_specs=(
            P(rows, None),
            P(rows, None),
            P(),
            P(),
            P(None, shared),
            P(None, shared),
            P(shared, None),
            P("ep", None, shared),
            P("ep", None, shared),
            P("ep", shared, None),
            P(rows, None),
        ),
        out_specs=(P(rows, None), P(), P()),
        check_vma=False,
    )
```

time: 457 us -> 403 us (0.88)
  waiting for transfers between devices: 221 us -> 149 us
  starting transfers between devices: 69 us -> 87 us
  matrix products: 20.7 us -> 9.43 us
  Pallas kernels: 96.8 us -> 106 us
    ppermute x8 -> x6, waiting for transfers between devices: 110 us -> 68.7 us  [receive_from(): lax.ppermute(value, 'y', [(i, (i - k) % PEERS) for i in range(PEERS)])]
    ppermute x5, waiting for transfers between devices: 70.9 us -> 34.3 us  [send_to(): lax.ppermute(value, 'y', [(i, (i + k) % PEERS) for i in range(PEERS)])]
    all_to_all x7, starting transfers between devices: 49.4 us -> 59.7 us  [over(): return lax.all_to_all(value, axes, split_axis=0, concat_axis=0, tiled=True)]
    pallas_call x6, Pallas kernels: 96.8 us -> 106 us  [the longest x4 95.8 us: hidden_grads(): pl.pallas_call(lambda *refs: hidden_kernel(count, mixed, *refs), grid=(to...]
    ppermute x6, starting transfers between devices: 2.98 us -> 10.6 us  [swap(): return lax.ppermute(value, 'core', [(0, 1), (1, 0)])]
    all_to_all x7, waiting for transfers between devices: 38.5 us -> 46.1 us  [over(): return lax.all_to_all(value, axes, split_axis=0, concat_axis=0, tiled=True)]
    dot_general x2, matrix products: 9.79 us -> 3.4 us  [mix(): jnp.dot(jnp.concatenate(tables, 0), rows, preferred_element_type=F32)]
    dot_general x4 -> x2, matrix products: 6.74 us -> 1.6 us  [router_weights(): logits = jnp.dot(normed.astype(F32), router, precision=HIGHEST)]
  transfers between devices with their start and end apart: 26 -> 24, of which waited for: 13 -> 10; matrix products, arithmetic and copies ran while one was open for 10% -> 8% of each run, Pallas kernels for 16% -> 25%
where the time goes in v5:
time: 403 us; the launch traced here: 397 us
  waiting for transfers between devices  149 us (37%)
  Pallas kernels  106 us (26%)
  starting transfers between devices  87 us (22%)
  local copies, waits for them, and re-layouts  25.6 us (6%)
  other arithmetic  18.8 us (5%)
  matrix products  9.43 us (2%)
    pallas_call x4, Pallas kernels, hidden_grads(): pl.pallas_call(lambda *refs: hidden_kernel(count, mixed, *refs), grid=(to...  95.8 us
    ppermute x6, waiting for transfers between devices, receive_from(): lax.ppermute(value, 'y', [(i, (i - k) % PEERS) for i in range(PEERS)])  68.7 us
    all_to_all x7, starting transfers between devices, over(): return lax.all_to_all(value, axes, split_axis=0, concat_axis=0, tiled=True)  59.7 us
    all_to_all x7, waiting for transfers between devices, over(): return lax.all_to_all(value, axes, split_axis=0, concat_axis=0, tiled=True)  46.1 us
    ppermute x5, waiting for transfers between devices, send_to(): lax.ppermute(value, 'y', [(i, (i + k) % PEERS) for i in range(PEERS)])  34.3 us
    ppermute x6, starting transfers between devices, receive_from(): lax.ppermute(value, 'y', [(i, (i - k) % PEERS) for i in range(PEERS)])  10.8 us
    ppermute x6, starting transfers between devices, swap(): return lax.ppermute(value, 'core', [(0, 1), (1, 0)])  10.6 us
    unnamed x40, local copies, waits for them, and re-layouts  10.1 us
  transfers between devices with their start and end apart: 24, of which 10 were waited for; matrix products, arithmetic and copies ran while one was open for 8% of the time, Pallas kernels for 25%

profile of v5, /device:TPU:1, one launch (start us, length us, event | category | flops | bytes accessed | tf_op | source)
XLA Modules:
  0.0 397.2 jit_solution(14394602585598101086)
XLA Ops:
  0.7 1.5 fusion.8
  2.2 1.5 fusion.2
  4.4 3.7 collective-permute-start
  10.0 5.0 %shard_map.130 = bf16[640,3584]{1,0:T(8,128)(2,1)} custom-call(bf16[640,256]{1,0:T(8,128)(2,1)S(1)} %fusion.46.table, bf16[256,3584]{1,0:T(8,128)(2,1)S(1)} %pad_maximum_fusion.rows.refs_0_), custom_call_target="tpu_custom_call" | custom-call | flops 1174405120 | bytes 6422528 | tf_op jit(solution)/shard_map/pallas_call | solution.py:191
  15.0 7.7 %all-to-all-start = ((bf16[16,40,3584]{2,1,0:T(8,128)(2,1)}), bf16[16,40,3584]{2,1,0:T(8,128)(2,1)}, u32[]{:S(2)}, u32[]{:S(2)}) async-start(bf16[16,40,3584]{2,1,0:T(8,128)(2,1)} %bitcast.46), calls=%async_computation | async-start | bytes 9175040 | tf_op jit(solution)/shard_map/all_to_all | solution.py:30
  22.7 3.0 collective-permute-start.5
  25.7 2.4 collective-permute-start.1
  30.1 33.7 %collective-permute-done.5.refs_2_.rows = bf16[256,3584]{1,0:T(8,128)(2,1)S(1)} collective-permute-done((bf16[256,3584]{1,0:T(8,128)(2,1)S(1)}, bf16[256,3584]{1,0:T(8,128)(2,1)S(1)}, u32[]{:S(2)}, u32[]{:S(2)}) %collective-permute-start.5) | collective-permute-done | bytes 1835040 | tf_op jit(solution)/shard_map/ppermute | solution.py:18
  63.8 1.3 copy-done.1
  65.1 5.5 %collective-permute-start.3 = (bf16[304,3584]{1,0:T(8,128)(2,1)}, bf16[304,3584]{1,0:T(8,128)(2,1)}, u32[]{:S(2)}, u32[]{:S(2)}) collective-permute-start(bf16[304,3584]{1,0:T(8,128)(2,1)} %bitcast.58), channel_id=1, source_target_pairs={{0,1},{1,0},{2,3},{3,2},{4,5},{5,4},{6,7},{7,6},{8,9},{9,8},{10,11... | collective-permute-start | bytes 6537224 | tf_op jit(solution)/shard_map/ppermute | solution.py:26
  71.5 1.5 copy-done.2
  73.0 5.0 %shard_map.133 = bf16[640,3584]{1,0:T(8,128)(2,1)} custom-call(bf16[640,256]{1,0:T(8,128)(2,1)S(1)} %fusion.45.table, bf16[256,3584]{1,0:T(8,128)(2,1)S(1)} %copy-done.2), custom_call_target="tpu_custom_call" | custom-call | flops 1174405120 | bytes 6422528 | tf_op jit(solution)/shard_map/pallas_call | solution.py:191
  78.0 26.9 %collective-permute-done.4.refs_1_ = bf16[256,3584]{1,0:T(8,128)(2,1)} collective-permute-done((bf16[256,3584]{1,0:T(8,128)(2,1)S(1)}, bf16[256,3584]{1,0:T(8,128)(2,1)}, u32[]{:S(2)}, u32[]{:S(2)}) %collective-permute-start.4) | collective-permute-done | bytes 1835040 | tf_op jit(solution)/shard_map/ppermute | solution.py:18
  104.9 1.6 collective-permute-start.7
  107.0 6.6 %all-to-all-start.1 = ((bf16[16,40,3584]{2,1,0:T(8,128)(2,1)}), bf16[16,40,3584]{2,1,0:T(8,128)(2,1)}, u32[]{:S(2)}, u32[]{:S(2)}) async-start(bf16[16,40,3584]{2,1,0:T(8,128)(2,1)} %bitcast.45), calls=%async_computation.1 | async-start | bytes 9175040 | tf_op jit(solution)/shard_map/all_to_all | solution.py:30
  113.7 2.4 collective-permute-start.10
  117.8 1.6 copy-done.4
  119.4 19.9 %shard_map.131 = (bf16[640,1792]{1,0:T(8,128)(2,1)}, f32[320,128]{1,0:T(8,128)S(1)}) custom-call(bf16[640,3584]{1,0:T(8,128)(2,1)} %bitcast.3.refs_0_, bf16[304,3584]{1,0:T(8,128)(2,1)S(1)} %bitcast.42, bf16[304,3584]{1,0:T(8,128)(2,1)} %collective-permute-done.1.refs_2_.refs_3_, bf16[304,3584]{1,0:T(8,128)(2,1)} %bitcast.55, ...), custom_call_target="tpu_custom_call" | custom-call | flops 7340032000 | bytes 20643840 | tf_op jit(solution)/shard_map/pallas_call | solution.py:153
  139.3 23.2 %shard_map.132 = (bf16[512,3584]{1,0:T(8,128)(2,1)}, f32[512,128]{1,0:T(8,128)}) custom-call(bf16[256,3584]{1,0:T(8,128)(2,1)S(1)} %pad_maximum_fusion.rows.refs_0_, bf16[256,3584]{1,0:T(8,128)(2,1)} %collective-permute-done.4.refs_1_, bf16[256,3584]{1,0:T(8,128)(2,1)} %copy-done.1, bf16[256,3584]{1,0:T(8,128)(2,1)} %collective-permute-done.6.refs_3_, ...), custom_call_target="tpu_custom_call" | custom-call | flops 11744051200 | bytes 24772608 | tf_op jit(solution)/shard_map/pallas_call | solution.py:153
  162.5 2.5 fusion.79
  165.0 9.2 %all-to-all-done.1 = bf16[16,40,3584]{2,1,0:T(8,128)(2,1)} async-done(((bf16[16,40,3584]{2,1,0:T(8,128)(2,1)}), bf16[16,40,3584]{2,1,0:T(8,128)(2,1)}, u32[]{:S(2)}, u32[]{:S(2)}) %all-to-all-start.1) | async-done | bytes 4587552 | tf_op jit(solution)/shard_map/all_to_all | solution.py:30
  174.2 1.6 copy-done.5
  175.8 20.3 %shard_map.134 = (bf16[640,1792]{1,0:T(8,128)(2,1)}, f32[320,128]{1,0:T(8,128)S(1)}) custom-call(bf16[640,3584]{1,0:T(8,128)(2,1)} %bitcast.17.refs_0_, bf16[304,3584]{1,0:T(8,128)(2,1)S(1)} %bitcast.43, bf16[304,3584]{1,0:T(8,128)(2,1)} %collective-permute-done.1.refs_2_.refs_3_, bf16[304,3584]{1,0:T(8,128)(2,1)} %bitcast.56, ...), custom_call_target="tpu_custom_call" | custom-call | flops 7340032000 | bytes 20643840 | tf_op jit(solution)/shard_map/pallas_call | solution.py:153
  196.1 14.5 %all-to-all-start.2 = ((bf16[16,40,1792]{2,1,0:T(8,128)(2,1)}), bf16[16,40,1792]{2,1,0:T(8,128)(2,1)}, u32[]{:S(2)}, u32[]{:S(2)}) async-start(bf16[16,40,1792]{2,1,0:T(8,128)(2,1)} %bitcast.48), calls=%async_computation.2 | async-start | bytes 4587520 | tf_op jit(solution)/shard_map/all_to_all | solution.py:30
  210.6 3.9 collective-permute-done.10.refs_0_
  214.5 3.2 collective-permute-done.11.refs_1_
  217.9 1.3 collective-permute-start.12
  219.2 1.6 copy-done.6
  220.8 32.4 %shard_map.135 = (bf16[1280,1792]{1,0:T(8,128)(2,1)}, f32[640,128]{1,0:T(8,128)S(1)}) custom-call(bf16[640,3584]{1,0:T(8,128)(2,1)} %collective-permute-done.10.refs_0_, bf16[640,3584]{1,0:T(8,128)(2,1)} %collective-permute-done.11.refs_1_, bf16[304,3584]{1,0:T(8,128)(2,1)S(1)} %bitcast.44, bf16[304,3584]{1,0:T(8,128)(2,1)} %collective-permute-done.1.refs_2_.refs_3_, ...), custom_call_target="tpu_custom_call" | custom-call | flops 14680064000 | bytes 27525120 | tf_op jit(solution)/shard_map/pallas_call | solution.py:153
  253.2 5.4 %fusion.78 = (bf16[640,1792]{1,0:T(8,128)(2,1)}, bf16[640,1792]{1,0:T(8,128)(2,1)}) fusion(bf16[1280,1792]{1,0:T(8,128)(2,1)} %get-tuple-element.34), kind=kLoop, calls=%fused_computation.156 | loop fusion | bytes 9175040 | tf_op jit(solution)/shard_map/slice | solution.py:301
  258.7 2.9 collective-permute-start.16
  263.2 2.5 fusion.47
  265.7 1.4 fusion.80
  268.2 7.2 %all-to-all-start.3 = ((f32[64,1,20]{2,1,0:T(1,128)}), f32[64,1,20]{2,1,0:T(1,128)S(1)}, u32[]{:S(2)}, u32[]{:S(2)}) async-start(f32[64,1,20]{2,1,0:T(1,128)} %bitcast.22), calls=%async_computation.3 | async-start | bytes 65536 | tf_op jit(solution)/shard_map/all_to_all | solution.py:30
  275.4 34.3 %collective-permute-done.15 = bf16[640,1792]{1,0:T(8,128)(2,1)} collective-permute-done((bf16[640,1792]{1,0:T(8,128)(2,1)}, bf16[640,1792]{1,0:T(8,128)(2,1)}, u32[]{:S(2)}, u32[]{:S(2)}) %collective-permute-start.15) | collective-permute-done | bytes 2293792 | tf_op jit(solution)/shard_map/ppermute | solution.py:22
  309.7 4.5 %add_convert_fusion = bf16[640,1792]{1,0:T(8,128)(2,1)} fusion(bf16[640,1792]{1,0:T(8,128)(2,1)} %collective-permute-done.16, bf16[640,1792]{1,0:T(8,128)(2,1)} %collective-permute-done.15, bf16[640,1792]{1,0:T(8,128)(2,1)S(1)} %copy-done.12), kind=kLoop, calls=%fused_computation | loop fusion | flops 6881280 | bytes 9175040 | tf_op jit(solution)/shard_map/convert_element_type | solution.py:321
  314.3 6.0 %all-to-all-start.4 = ((bf16[16,40,1792]{2,1,0:T(8,128)(2,1)}), bf16[16,40,1792]{2,1,0:T(8,128)(2,1)S(1)}, u32[]{:S(2)}, u32[]{:S(2)}) async-start(bf16[16,40,1792]{2,1,0:T(8,128)(2,1)} %bitcast.25), calls=%async_computation.4 | async-start | bytes 4587520 | tf_op jit(solution)/shard_map/all_to_all | solution.py:30
  320.3 2.9 fusion.12
  323.2 1.6 collective-permute-start.14
  325.1 1.2 fusion.58
  326.2 2.9 fusion.59
  329.3 18.0 %all-to-all-done.4 = bf16[16,40,1792]{2,1,0:T(8,128)(2,1)S(1)} async-done(((bf16[16,40,1792]{2,1,0:T(8,128)(2,1)}), bf16[16,40,1792]{2,1,0:T(8,128)(2,1)S(1)}, u32[]{:S(2)}, u32[]{:S(2)}) %all-to-all-start.4) | async-done | bytes 2293792 | tf_op jit(solution)/shard_map/all_to_all | solution.py:30
  350.3 2.8 fusion.11
  354.3 13.0 %all-to-all-start.5 = ((f32[128,1,476]{2,1,0:T(1,128)}), f32[128,1,476]{2,1,0:T(1,128)S(1)}, u32[]{:S(2)}, u32[]{:S(2)}) async-start(f32[128,1,476]{2,1,0:T(1,128)} %all_to_all.64), calls=%async_computation.5 | async-start | bytes 524288 | tf_op jit(solution)/shard_map/all_to_all | solution.py:30
  367.3 10.8 %all-to-all-done.5 = f32[128,1,476]{2,1,0:T(1,128)S(1)} async-done(((f32[128,1,476]{2,1,0:T(1,128)}), f32[128,1,476]{2,1,0:T(1,128)S(1)}, u32[]{:S(2)}, u32[]{:S(2)}) %all-to-all-start.5) | async-done | bytes 243744 | tf_op jit(solution)/shard_map/all_to_all | solution.py:30
  379.1 4.8 %all-to-all-start.6 = ((f32[128,1,476]{2,1,0:T(1,128)}), f32[128,1,476]{2,1,0:T(1,128)S(1)}, u32[]{:S(2)}, u32[]{:S(2)}) async-start(f32[128,1,476]{2,1,0:T(1,128)} %broadcast_in_dim.119), calls=%async_computation.6 | async-start | bytes 524288 | tf_op jit(solution)/shard_map/all_to_all | solution.py:30
  383.9 2.7 fusion.7
  386.6 8.0 %all-to-all-done.6 = f32[128,1,476]{2,1,0:T(1,128)S(1)} async-done(((f32[128,1,476]{2,1,0:T(1,128)}), f32[128,1,476]{2,1,0:T(1,128)S(1)}, u32[]{:S(2)}, u32[]{:S(2)}) %all-to-all-start.6) | async-done | bytes 243744 | tf_op jit(solution)/shard_map/all_to_all | solution.py:30
  (123 shorter events, 18.4 us)
Async XLA Ops:
  0.6 115.7 %copy-start = (f32[3584,16]{0,1:T(8,128)S(1)}, f32[3584,16]{0,1:T(8,128)}, u32[]{:S(2)}) copy-start(f32[3584,16]{0,1:T(8,128)} %param.14) | copy-start | bytes 688132
  0.6 3.0 copy-start.11
  3.7 112.6 %copy-start.7 = (bf16[128,3584]{1,0:T(8,128)(2,1)}, bf16[128,3584]{1,0:T(8,128)(2,1)S(1)}, u32[]{:S(2)}) copy-start(bf16[128,3584]{1,0:T(8,128)(2,1)S(1)} %fusion.2) | copy-start | bytes 2752516
  3.7 0.7 copy-start.19
  4.4 4.7 %collective-permute-start = (s32[128,2]{0,1:T(2,128)S(1)}, s32[128,2]{0,1:T(2,128)S(1)}, u32[]{:S(2)}, u32[]{:S(2)}) collective-permute-start(s32[128,2]{0,1:T(2,128)S(1)} %copy-done.19), channel_id=1, source_target_pairs={{0,4},{2,6},{4,0},{6,2},{1,5},{3,7},{5,1},{7,3},{8,12},{10,14},{12... | collective-permute-start | bytes 3080 | tf_op jit(solution)/shard_map/ppermute | solution.py:18
  15.0 92.1 %all-to-all-start = ((bf16[16,40,3584]{2,1,0:T(8,128)(2,1)}), bf16[16,40,3584]{2,1,0:T(8,128)(2,1)}, u32[]{:S(2)}, u32[]{:S(2)}) async-start(bf16[16,40,3584]{2,1,0:T(8,128)(2,1)} %bitcast.46), calls=%async_computation | async-start | bytes 9175040 | tf_op jit(solution)/shard_map/all_to_all | solution.py:30
  22.7 41.1 %collective-permute-start.5 = (bf16[256,3584]{1,0:T(8,128)(2,1)S(1)}, bf16[256,3584]{1,0:T(8,128)(2,1)S(1)}, u32[]{:S(2)}, u32[]{:S(2)}) collective-permute-start(bf16[256,3584]{1,0:T(8,128)(2,1)S(1)} %pad_maximum_fusion.rows.refs_0_), channel_id=1, source_target_pairs={{0,4},{2,6},{4,0},{6,2},{1,5},{3,7},{5,1},{7,3},{8,12},{10,14},{12... | collective-permute-start | bytes 5505032 | tf_op jit(solution)/shard_map/ppermute | solution.py:18
  25.7 80.8 %collective-permute-start.1 = (bf16[304,3584]{1,0:T(8,128)(2,1)}, bf16[304,3584]{1,0:T(8,128)(2,1)}, u32[]{:S(2)}, u32[]{:S(2)}) collective-permute-start(bf16[304,3584]{1,0:T(8,128)(2,1)} %bitcast.41), channel_id=1, source_target_pairs={{0,1},{1,0},{2,3},{3,2},{4,5},{5,4},{6,7},{7,6},{8,9},{9,8},{10,11... | collective-permute-start | bytes 6537224 | tf_op jit(solution)/shard_map/ppermute | solution.py:26
  28.1 76.8 %collective-permute-start.4 = (bf16[256,3584]{1,0:T(8,128)(2,1)S(1)}, bf16[256,3584]{1,0:T(8,128)(2,1)}, u32[]{:S(2)}, u32[]{:S(2)}) collective-permute-start(bf16[256,3584]{1,0:T(8,128)(2,1)S(1)} %pad_maximum_fusion.rows.refs_0_), channel_id=1, source_target_pairs={{0,6},{2,0},{4,2},{6,4},{1,7},{3,1},{5,3},{7,5},{8,14},{10,8},{12,... | collective-permute-start | bytes 5505032 | tf_op jit(solution)/shard_map/ppermute | solution.py:18
  28.8 77.7 %collective-permute-start.6 = (bf16[256,3584]{1,0:T(8,128)(2,1)S(1)}, bf16[256,3584]{1,0:T(8,128)(2,1)}, u32[]{:S(2)}, u32[]{:S(2)}) collective-permute-start(bf16[256,3584]{1,0:T(8,128)(2,1)S(1)} %pad_maximum_fusion.rows.refs_0_), channel_id=1, source_target_pairs={{0,2},{2,4},{4,6},{6,0},{1,3},{3,5},{5,7},{7,1},{8,10},{10,12},{12... | collective-permute-start | bytes 5505032 | tf_op jit(solution)/shard_map/ppermute | solution.py:18
  29.5 84.2 %collective-permute-start.2 = (bf16[304,3584]{1,0:T(8,128)(2,1)}, bf16[304,3584]{1,0:T(8,128)(2,1)}, u32[]{:S(2)}, u32[]{:S(2)}) collective-permute-start(bf16[304,3584]{1,0:T(8,128)(2,1)} %bitcast.54), channel_id=1, source_target_pairs={{0,1},{1,0},{2,3},{3,2},{4,5},{5,4},{6,7},{7,6},{8,9},{9,8},{10,11... | collective-permute-start | bytes 6537224 | tf_op jit(solution)/shard_map/ppermute | solution.py:26
  63.8 1.3 copy-start.1
  65.1 51.0 %collective-permute-start.3 = (bf16[304,3584]{1,0:T(8,128)(2,1)}, bf16[304,3584]{1,0:T(8,128)(2,1)}, u32[]{:S(2)}, u32[]{:S(2)}) collective-permute-start(bf16[304,3584]{1,0:T(8,128)(2,1)} %bitcast.58), channel_id=1, source_target_pairs={{0,1},{1,0},{2,3},{3,2},{4,5},{5,4},{6,7},{7,6},{8,9},{9,8},{10,11... | collective-permute-start | bytes 6537224 | tf_op jit(solution)/shard_map/ppermute | solution.py:26
  71.5 1.5 copy-start.2
  104.9 34.3 %collective-permute-start.7 = (bf16[304,3584]{1,0:T(8,128)(2,1)}, bf16[304,3584]{1,0:T(8,128)(2,1)}, u32[]{:S(2)}, u32[]{:S(2)}) collective-permute-start(bf16[304,3584]{1,0:T(8,128)(2,1)} %bitcast.11.refs_4_), channel_id=1, source_target_pairs={{0,1},{1,0},{2,3},{3,2},{4,5},{5,4},{6,7},{7,6},{8,9},{9,8},{10,11... | collective-permute-start | bytes 6537224 | tf_op jit(solution)/shard_map/ppermute | solution.py:26
  106.5 32.7 %collective-permute-start.8 = (bf16[304,3584]{1,0:T(8,128)(2,1)}, bf16[304,3584]{1,0:T(8,128)(2,1)}, u32[]{:S(2)}, u32[]{:S(2)}) collective-permute-start(bf16[304,3584]{1,0:T(8,128)(2,1)} %bitcast.12.refs_6_), channel_id=1, source_target_pairs={{0,1},{1,0},{2,3},{3,2},{4,5},{5,4},{6,7},{7,6},{8,9},{9,8},{10,11... | collective-permute-start | bytes 6537224 | tf_op jit(solution)/shard_map/ppermute | solution.py:26
  106.5 32.7 %collective-permute-start.9 = (bf16[304,3584]{1,0:T(8,128)(2,1)}, bf16[304,3584]{1,0:T(8,128)(2,1)}, u32[]{:S(2)}, u32[]{:S(2)}) collective-permute-start(bf16[304,3584]{1,0:T(8,128)(2,1)} %refs_8_.1), channel_id=1, source_target_pairs={{0,1},{1,0},{2,3},{3,2},{4,5},{5,4},{6,7},{7,6},{8,9},{9,8},{10,11... | collective-permute-start | bytes 6537224 | tf_op jit(solution)/shard_map/ppermute | solution.py:26
  107.0 67.2 %all-to-all-start.1 = ((bf16[16,40,3584]{2,1,0:T(8,128)(2,1)}), bf16[16,40,3584]{2,1,0:T(8,128)(2,1)}, u32[]{:S(2)}, u32[]{:S(2)}) async-start(bf16[16,40,3584]{2,1,0:T(8,128)(2,1)} %bitcast.45), calls=%async_computation.1 | async-start | bytes 9175040 | tf_op jit(solution)/shard_map/all_to_all | solution.py:30
  113.7 100.8 %collective-permute-start.10 = (bf16[640,3584]{1,0:T(8,128)(2,1)}, bf16[640,3584]{1,0:T(8,128)(2,1)}, u32[]{:S(2)}, u32[]{:S(2)}) collective-permute-start(bf16[640,3584]{1,0:T(8,128)(2,1)} %bitcast.3.refs_0_), channel_id=1, source_target_pairs={{0,6},{2,0},{4,2},{6,4},{1,7},{3,1},{5,3},{7,5},{8,14},{10,8},{12,... | collective-permute-start | bytes 13762568 | tf_op jit(solution)/shard_map/ppermute | solution.py:18
  116.1 101.6 %collective-permute-start.11 = (bf16[640,3584]{1,0:T(8,128)(2,1)}, bf16[640,3584]{1,0:T(8,128)(2,1)}, u32[]{:S(2)}, u32[]{:S(2)}) collective-permute-start(bf16[640,3584]{1,0:T(8,128)(2,1)} %bitcast.3.refs_0_), channel_id=1, source_target_pairs={{0,2},{2,4},{4,6},{6,0},{1,3},{3,5},{5,7},{7,1},{8,10},{10,12},{12... | collective-permute-start | bytes 13762568 | tf_op jit(solution)/shard_map/ppermute | solution.py:18
  117.7 1.6 copy-start.4
  174.2 1.6 copy-start.5
  196.1 67.1 %all-to-all-start.2 = ((bf16[16,40,1792]{2,1,0:T(8,128)(2,1)}), bf16[16,40,1792]{2,1,0:T(8,128)(2,1)}, u32[]{:S(2)}, u32[]{:S(2)}) async-start(bf16[16,40,1792]{2,1,0:T(8,128)(2,1)} %bitcast.48), calls=%async_computation.2 | async-start | bytes 4587520 | tf_op jit(solution)/shard_map/all_to_all | solution.py:30
  217.7 35.5 %collective-permute-start.13 = (bf16[128,3584]{1,0:T(8,128)(2,1)}, bf16[128,3584]{1,0:T(8,128)(2,1)S(1)}, u32[]{:S(2)}, u32[]{:S(2)}) collective-permute-start(bf16[128,3584]{1,0:T(8,128)(2,1)} %get-tuple-element.32), channel_id=1, source_target_pairs={{0,6},{2,0},{4,2},{6,4},{1,7},{3,1},{5,3},{7,5},{8,14},{10,8},{12,... | collective-permute-start | bytes 2752520 | tf_op jit(solution)/shard_map/ppermute | solution.py:22
  217.9 35.3 %collective-permute-start.12 = (bf16[128,3584]{1,0:T(8,128)(2,1)S(1)}, bf16[128,3584]{1,0:T(8,128)(2,1)S(1)}, u32[]{:S(2)}, u32[]{:S(2)}) collective-permute-start(bf16[128,3584]{1,0:T(8,128)(2,1)S(1)} %get-tuple-element.31), channel_id=1, source_target_pairs={{0,2},{2,4},{4,6},{6,0},{1,3},{3,5},{5,7},{7,1},{8,10},{10,12},{12... | collective-permute-start | bytes 2752520 | tf_op jit(solution)/shard_map/ppermute | solution.py:22
  219.2 1.6 copy-start.6
  253.2 5.5 %copy-start.14 = (bf16[128,3584]{1,0:T(8,128)(2,1)}, bf16[128,3584]{1,0:T(8,128)(2,1)S(1)}, u32[]{:S(2)}) copy-start(bf16[128,3584]{1,0:T(8,128)(2,1)S(1)} %collective-permute-done.13) | copy-start | bytes 2752516
  253.2 5.4 %copy-start.16 = (bf16[128,3584]{1,0:T(8,128)(2,1)}, bf16[128,3584]{1,0:T(8,128)(2,1)S(1)}, u32[]{:S(2)}) copy-start(bf16[128,3584]{1,0:T(8,128)(2,1)S(1)} %collective-permute-done.12) | copy-start | bytes 2752516
  253.2 8.3 %copy-start.3 = (bf16[256,3584]{1,0:T(8,128)(2,1)S(1)}, bf16[256,3584]{1,0:T(8,128)(2,1)}, u32[]{:S(2)}) copy-start(bf16[256,3584]{1,0:T(8,128)(2,1)} %copy-done.1) | copy-start | bytes 5505028
  258.7 51.1 %collective-permute-start.15 = (bf16[640,1792]{1,0:T(8,128)(2,1)}, bf16[640,1792]{1,0:T(8,128)(2,1)}, u32[]{:S(2)}, u32[]{:S(2)}) collective-permute-start(bf16[640,1792]{1,0:T(8,128)(2,1)} %get-tuple-element.52), channel_id=1, source_target_pairs={{0,2},{2,4},{4,6},{6,0},{1,3},{3,5},{5,7},{7,1},{8,10},{10,12},{12... | collective-permute-start | bytes 6881288 | tf_op jit(solution)/shard_map/ppermute | solution.py:22
  258.7 51.1 %collective-permute-start.16 = (bf16[640,1792]{1,0:T(8,128)(2,1)}, bf16[640,1792]{1,0:T(8,128)(2,1)}, u32[]{:S(2)}, u32[]{:S(2)}) collective-permute-start(bf16[640,1792]{1,0:T(8,128)(2,1)} %get-tuple-element.53), channel_id=1, source_target_pairs={{0,6},{2,0},{4,2},{6,4},{1,7},{3,1},{5,3},{7,5},{8,14},{10,8},{12,... | collective-permute-start | bytes 6881288 | tf_op jit(solution)/shard_map/ppermute | solution.py:22
  265.7 44.0 %copy-start.12 = (bf16[640,1792]{1,0:T(8,128)(2,1)S(1)}, bf16[640,1792]{1,0:T(8,128)(2,1)}, u32[]{:S(2)}) copy-start(bf16[640,1792]{1,0:T(8,128)(2,1)} %get-tuple-element.21) | copy-start | bytes 6881284
  268.2 46.1 %all-to-all-start.3 = ((f32[64,1,20]{2,1,0:T(1,128)}), f32[64,1,20]{2,1,0:T(1,128)S(1)}, u32[]{:S(2)}, u32[]{:S(2)}) async-start(f32[64,1,20]{2,1,0:T(1,128)} %bitcast.22), calls=%async_computation.3 | async-start | bytes 65536 | tf_op jit(solution)/shard_map/all_to_all | solution.py:30
  314.3 33.1 %all-to-all-start.4 = ((bf16[16,40,1792]{2,1,0:T(8,128)(2,1)}), bf16[16,40,1792]{2,1,0:T(8,128)(2,1)S(1)}, u32[]{:S(2)}, u32[]{:S(2)}) async-start(bf16[16,40,1792]{2,1,0:T(8,128)(2,1)} %bitcast.25), calls=%async_computation.4 | async-start | bytes 4587520 | tf_op jit(solution)/shard_map/all_to_all | solution.py:30
  320.3 4.8 %copy-start.8 = (bf16[128,3584]{1,0:T(8,128)(2,1)S(1)}, bf16[128,3584]{1,0:T(8,128)(2,1)}, u32[]{:S(2)}) copy-start(bf16[128,3584]{1,0:T(8,128)(2,1)} %copy-done.7) | copy-start | bytes 2752516
  323.2 25.2 %collective-permute-start.14 = (bf16[128,3584]{1,0:T(8,128)(2,1)}, bf16[128,3584]{1,0:T(8,128)(2,1)}, u32[]{:S(2)}, u32[]{:S(2)}) collective-permute-start(bf16[128,3584]{1,0:T(8,128)(2,1)} %fusion.12), channel_id=1, source_target_pairs={{0,4},{2,6},{4,0},{6,2},{1,5},{3,7},{5,1},{7,3},{8,12},{10,14},{12... | collective-permute-start | bytes 2752520 | tf_op jit(solution)/shard_map/ppermute | solution.py:22
  347.3 1.2 copy-start.17
  347.3 1.2 copy-start.18
  348.2 1.3 copy-start.9
  348.2 1.8 copy-start.10
  348.3 2.1 copy-start.15
  350.3 2.8 copy-start.13
  354.3 23.8 %all-to-all-start.5 = ((f32[128,1,476]{2,1,0:T(1,128)}), f32[128,1,476]{2,1,0:T(1,128)S(1)}, u32[]{:S(2)}, u32[]{:S(2)}) async-start(f32[128,1,476]{2,1,0:T(1,128)} %all_to_all.64), calls=%async_computation.5 | async-start | bytes 524288 | tf_op jit(solution)/shard_map/all_to_all | solution.py:30
  379.1 15.5 %all-to-all-start.6 = ((f32[128,1,476]{2,1,0:T(1,128)}), f32[128,1,476]{2,1,0:T(1,128)S(1)}, u32[]{:S(2)}, u32[]{:S(2)}) async-start(f32[128,1,476]{2,1,0:T(1,128)} %broadcast_in_dim.119), calls=%async_computation.6 | async-start | bytes 524288 | tf_op jit(solution)/shard_map/all_to_all | solution.py:30

commit v6 on v5

--- a/solution.py
+++ b/solution.py
@@ -67,7 +67,7 @@
 
     @pl.when(step == 0)
     def _():
-        for copy in copies:
+        for copy in copies[4:] + copies[:4]:
             copy.start()
         if half > 2 * part:
             for i in range(3):
@@ -81,6 +81,7 @@
 
         @pl.when(step == p // each)
         def _(p=p):
+            first = p % each * size
             if mixed:
                 chunk = table.shape[0]
                 for i in range(2 * size // chunk):
@@ -89,11 +90,11 @@
                         sources[p][i * chunk : (i + 1) * chunk, :],
                         preferred_element_type=F32,
                     ).astype(BF)
-                    at = slice(i * chunk // 2, (i + 1) * chunk // 2)
+                    at = slice(first + i * chunk // 2, first + (i + 1) * chunk // 2)
                     normed[at, :] = got[: chunk // 2]
                     other[at, :] = got[chunk // 2 :]
             else:
-                at = slice((p % each) * size, (p % each + 1) * size)
+                at = slice(first, first + size)
                 normed[at, :] = sources[p][:size, :]
                 other[at, :] = sources[p][size:, :]
 
@@ -103,13 +104,13 @@
             for copy in copies[i:j]:
                 copy.wait()
 
+    wait(4, 6)
+    back[...] = lax.dot_general(
+        other[...], weights[2 * half :, :], TRANS, preferred_element_type=F32
+    )
     wait(0, 4)
     both[...] = lax.dot_general(
         normed[...], weights[: 2 * half, :], TRANS, preferred_element_type=F32
-    )
-    wait(4, 6)
-    back[...] = lax.dot_general(
-        other[...], weights[2 * half :, :], TRANS, preferred_element_type=F32
     )
     gate, up, dy = both[:, :half], both[:, half:], back[...]
     sig = jax.nn.sigmoid(gate)
@@ -124,7 +125,7 @@
             grads[...], weights[: 2 * half, :], preferred_element_type=F32
         ).astype(BF)
         chunk = table.shape[0]
-        for i in range(2 * size // chunk):
+        for i in range(2 * normed.shape[0] // chunk):
             at = slice(i * chunk // 2, (i + 1) * chunk // 2)
             sides = jnp.concatenate([other[at, : width // 2], other[at, width // 2 :]], 0)
             into[i * chunk : (i + 1) * chunk, :] = jnp.dot(
@@ -142,8 +143,8 @@
     size = sources[0].shape[0] // 2
     part, width = pieces[0].shape
     half = -(-2 * part // 128) * 128
-    step_rows = size if mixed else 2 * size
     total = count * size
+    step_rows = min(total, 320) if mixed else 2 * size
     out = (2 * total, width // 2) if mixed else (total, width)
     block = (2 * step_rows, width // 2) if mixed else (step_rows, width)
 
@@ -269,7 +270,10 @@
 
     routes_in = after(routes, pair)
     peer_routes = {k: receive_from(routes_in, k) for k in (1, 2, 3)}
-    peer = {k: receive_from(pair, k) for k in (1, 2, 3)}
+    expert = weight_pieces(expert_gate[0], expert_up[0], expert_down[0])
+    dense = weight_pieces(dense_gate, dense_up, dense_down)
+    later = after(pair, *expert, *dense)
+    peer = {k: receive_from(later if k != 2 else pair, k) for k in (2, 1, 3)}
 
     def to_experts(rows, index):
         places = jnp.concatenate([index, index + cap], 0)
@@ -280,11 +284,9 @@
     far_index = peer_routes[2] * block + slots_of(peer_routes[2], experts)
     own = to_experts(pair, own_index)
     far = to_experts(peer[2], far_index)
-    near1 = receive_from(own, 1)
-    near3 = receive_from(own, 3)
-
-    expert = weight_pieces(expert_gate[0], expert_up[0], expert_down[0])
-    dense = weight_pieces(dense_gate, dense_up, dense_down)
+    chunk = everything // 2
+    parts = [own[:chunk], own[chunk:]]
+    near = [{k: receive_from(part, k) for k in (1, 3)} for part in parts]
     table = shuffle_table(cap, experts // 2)
     tables = (table, table.T)
 
@@ -292,21 +294,30 @@
     dense_part, unused = hidden_grads(
         [after(pair, own_into)] + [peer[k] for k in (1, 2, 3)], dense
     )
-    far_into, far_joint = hidden_grads([after(far, dense_part)], expert, tables)
+    near_into = [None, None]
+    near_joint = [None, None]
+    near_into[0], near_joint[0] = hidden_grads(
+        [after(near[0][1], dense_part), near[0][3]], expert, tables
+    )
+    far_into, far_joint = hidden_grads([after(far, near_into[0])], expert, tables)
     far_back = over(far_into)
-    near_into, near_joint = hidden_grads([after(near1, far_into), near3], expert, tables)
-    home1 = send_to(after(dense_part[tok : 2 * tok], near1), 1)
-    home3 = send_to(after(dense_part[3 * tok :], near3), 3)
-    near_into = after(near_into, home1, home3)
-    near1_back = send_to(near_into[:everything], 1)
-    near3_back = send_to(near_into[everything:], 3)
+    near_into[1], near_joint[1] = hidden_grads(
+        [after(near[1][1], far_into), near[1][3]], expert, tables
+    )
+    arrived = (near[1][1], near[1][3])
+    near_back = []
+    for i in (0, 1):
+        first = after(near_into[i], *arrived) if i == 0 else near_into[i]
+        near_back.append(send_to(first[:chunk], 1).astype(F32) + send_to(first[chunk:], 3).astype(F32))
+    home1 = send_to(after(dense_part[tok : 2 * tok], near_into[1]), 1)
+    home3 = send_to(after(dense_part[3 * tok :], near_into[1]), 3)
 
     joints = jnp.stack(
         [
             own_joint.reshape(experts, cap),
-            near_joint[: experts * cap].reshape(experts, cap),
+            jnp.concatenate([v[: chunk // 2] for v in near_joint]).reshape(experts, cap),
             far_joint.reshape(experts, cap),
-            near_joint[experts * cap :].reshape(experts, cap),
+            jnp.concatenate([v[chunk // 2 :] for v in near_joint]).reshape(experts, cap),
         ],
         1,
     )
@@ -317,7 +328,7 @@
     joints = over(after(joints, far_back), ("ep", "y"))
     score = jnp.sum(joints.reshape(experts, PEERS, cap), 1)
 
-    own_sum = own_into.astype(F32) + near1_back.astype(F32) + near3_back.astype(F32)
+    own_sum = own_into.astype(F32) + jnp.concatenate(near_back, 0)
     own_back = over(after(own_sum.astype(BF), joints))
 
     ids = lax.broadcasted_iota(jnp.int32, (1, 1, experts), 2)

time: 403 us -> 405 us (level)
  waiting for transfers between devices: 149 us -> 135 us
  other arithmetic: 18.8 us -> 24 us
  starting transfers between devices: 87 us -> 91.2 us
    ppermute x6 -> x8, starting transfers between devices: 10.8 us -> 28 us  [receive_from(): lax.ppermute(value, 'y', [(i, (i - k) % PEERS) for i in range(PEERS)])]
    all_to_all x7, starting transfers between devices: 59.7 us -> 48.1 us  [over(): return lax.all_to_all(value, axes, split_axis=0, concat_axis=0, tiled=True)]
    unnamed x40 -> x32, local copies, waits for them, and re-layouts: 10.1 us -> 2.77 us
    ppermute x6 -> x8, waiting for transfers between devices: 68.7 us -> 61.5 us  [receive_from(): lax.ppermute(value, 'y', [(i, (i - k) % PEERS) for i in range(PEERS)])]
    slice x3 -> x6, local copies, waits for them, and re-layouts: 8.1 us -> 12.4 us  [the longest x1 4.92 us: body(): parts = [own[:chunk], own[chunk:]]]
    all_to_all x7, waiting for transfers between devices: 46.1 us -> 41.9 us  [over(): return lax.all_to_all(value, axes, split_axis=0, concat_axis=0, tiled=True)]
    ppermute x5 -> x7, waiting for transfers between devices: 34.3 us -> 31.3 us  [send_to(): lax.ppermute(value, 'y', [(i, (i + k) % PEERS) for i in range(PEERS)])]
    pallas_call x4 -> x5, Pallas kernels: 95.8 us -> 98.6 us  [hidden_grads(): pl.pallas_call(lambda *refs: hidden_kernel(count, mixed, *refs), grid=(to...]
  transfers between devices with their start and end apart: 24 -> 28, of which waited for: 10 -> 11; matrix products, arithmetic and copies ran while one was open for 8% -> 11% of each run, Pallas kernels for 25% -> 28%
where the time goes in v6:
time: 405 us; the launch traced here: 398 us
  waiting for transfers between devices  135 us (33%)
  Pallas kernels  110 us (27%)
  starting transfers between devices  91.2 us (23%)
  local copies, waits for them, and re-layouts  24.5 us (6%)
  other arithmetic  24 us (6%)
  matrix products  11.4 us (3%)
    pallas_call x5, Pallas kernels, hidden_grads(): pl.pallas_call(lambda *refs: hidden_kernel(count, mixed, *refs), grid=(to...  98.6 us
    ppermute x8, waiting for transfers between devices, receive_from(): lax.ppermute(value, 'y', [(i, (i - k) % PEERS) for i in range(PEERS)])  61.5 us
    all_to_all x7, starting transfers between devices, over(): return lax.all_to_all(value, axes, split_axis=0, concat_axis=0, tiled=True)  48.1 us
    all_to_all x7, waiting for transfers between devices, over(): return lax.all_to_all(value, axes, split_axis=0, concat_axis=0, tiled=True)  41.9 us
    ppermute x7, waiting for transfers between devices, send_to(): lax.ppermute(value, 'y', [(i, (i + k) % PEERS) for i in range(PEERS)])  31.3 us
    ppermute x8, starting transfers between devices, receive_from(): lax.ppermute(value, 'y', [(i, (i - k) % PEERS) for i in range(PEERS)])  28 us
    pallas_call x2, Pallas kernels, pick_rows(): pl.pallas_call(pick_kernel, grid=(width // block,), in_specs=[pl.BlockSpe...  11.7 us
    ppermute x7, starting transfers between devices, send_to(): lax.ppermute(value, 'y', [(i, (i + k) % PEERS) for i in range(PEERS)])  8.17 us
  transfers between devices with their start and end apart: 28, of which 11 were waited for; matrix products, arithmetic and copies ran while one was open for 11% of the time, Pallas kernels for 28%

profile of v6, /device:TPU:1, one launch (start us, length us, event | category | flops | bytes accessed | tf_op | source)
XLA Modules:
  0.0 397.5 jit_solution(11603580982568292867)
XLA Ops:
  4.9 3.7 collective-permute-start
  11.1 5.0 %shard_map.130 = bf16[640,3584]{1,0:T(8,128)(2,1)} custom-call(bf16[640,256]{1,0:T(8,128)(2,1)S(1)} %fusion.47.table, bf16[256,3584]{1,0:T(8,128)(2,1)S(1)} %pad_maximum_fusion.rows.refs_0_), custom_call_target="tpu_custom_call" | custom-call | flops 1174405120 | bytes 6422528 | tf_op jit(solution)/shard_map/pallas_call | solution.py:192
  16.1 7.7 %all-to-all-start = ((bf16[16,40,3584]{2,1,0:T(8,128)(2,1)}), bf16[16,40,3584]{2,1,0:T(8,128)(2,1)}, u32[]{:S(2)}, u32[]{:S(2)}) async-start(bf16[16,40,3584]{2,1,0:T(8,128)(2,1)} %bitcast.43), calls=%async_computation | async-start | bytes 9175040 | tf_op jit(solution)/shard_map/all_to_all | solution.py:30
  23.8 3.0 collective-permute-start.8
  26.8 2.4 collective-permute-start.2
  31.2 33.7 %collective-permute-done.8.refs_2_.rows = bf16[256,3584]{1,0:T(8,128)(2,1)} collective-permute-done((bf16[256,3584]{1,0:T(8,128)(2,1)S(1)}, bf16[256,3584]{1,0:T(8,128)(2,1)}, u32[]{:S(2)}, u32[]{:S(2)}) %collective-permute-start.8) | collective-permute-done | bytes 1835040 | tf_op jit(solution)/shard_map/ppermute | solution.py:18
  64.9 3.0 collective-permute-start.5
  73.8 6.7 %shard_map.134 = bf16[640,3584]{1,0:T(8,128)(2,1)} custom-call(bf16[640,256]{1,0:T(8,128)(2,1)S(1)} %fusion.46.table, bf16[256,3584]{1,0:T(8,128)(2,1)} %collective-permute-done.8.refs_2_.rows), custom_call_target="tpu_custom_call" | custom-call | flops 1174405120 | bytes 6422528 | tf_op jit(solution)/shard_map/pallas_call | solution.py:192
  80.5 2.0 fusion.24
  83.5 2.8 collective-permute-start.7
  86.3 6.6 %all-to-all-start.1 = ((bf16[16,40,3584]{2,1,0:T(8,128)(2,1)}), bf16[16,40,3584]{2,1,0:T(8,128)(2,1)}, u32[]{:S(2)}, u32[]{:S(2)}) async-start(bf16[16,40,3584]{2,1,0:T(8,128)(2,1)} %bitcast.44), calls=%async_computation.1 | async-start | bytes 9175040 | tf_op jit(solution)/shard_map/all_to_all | solution.py:30
  92.9 4.9 %fusion.79 = (bf16[8,40,3584]{2,1,0:T(8,128)(2,1)}, bf16[8,40,3584]{2,1,0:T(8,128)(2,1)}) fusion(bf16[16,40,3584]{2,1,0:T(8,128)(2,1)} %all-to-all-done), kind=kLoop, calls=%fused_computation.161 | loop fusion | bytes 9175040 | tf_op jit(solution)/shard_map/slice | solution.py:288
  97.8 2.7 collective-permute-start.10
  100.7 19.0 %shard_map.131 = (bf16[640,1792]{1,0:T(8,128)(2,1)}, f32[320,128]{1,0:T(8,128)S(1)}) custom-call(bf16[640,3584]{1,0:T(8,128)(2,1)} %bitcast.3.refs_0_, bf16[304,3584]{1,0:T(8,128)(2,1)} %bitcast.5.refs_1_.refs_2_, bf16[304,3584]{1,0:T(8,128)(2,1)} %collective-permute-done.1.refs_2_.refs_3_, bf16[304,3584]{1,0:T(8,128)(2,1)} %bitcast.57, ...), custom_call_target="tpu_custom_call" | custom-call | flops 7340032000 | bytes 20643840 | tf_op jit(solution)/shard_map/pallas_call | solution.py:154
  119.7 2.7 collective-permute-start.12
  122.7 2.5 collective-permute-done.7.refs_1_
  125.2 12.8 %collective-permute-start.13 = (bf16[320,3584]{1,0:T(8,128)(2,1)}, bf16[320,3584]{1,0:T(8,128)(2,1)}, u32[]{:S(2)}, u32[]{:S(2)}) collective-permute-start(bf16[320,3584]{1,0:T(8,128)(2,1)} %bitcast.15), channel_id=1, source_target_pairs={{0,2},{2,4},{4,6},{6,0},{1,3},{3,5},{5,7},{7,1},{8,10},{10,12},{12... | collective-permute-start | bytes 6881288 | tf_op jit(solution)/shard_map/ppermute | solution.py:18
  138.0 22.0 %shard_map.132 = (bf16[512,3584]{1,0:T(8,128)(2,1)}, f32[512,128]{1,0:T(8,128)}) custom-call(bf16[256,3584]{1,0:T(8,128)(2,1)S(1)} %pad_maximum_fusion.rows.refs_0_, bf16[256,3584]{1,0:T(8,128)(2,1)} %collective-permute-done.7.refs_1_, bf16[256,3584]{1,0:T(8,128)(2,1)} %collective-permute-done.8.refs_2_.rows, ...), custom_call_target="tpu_custom_call" | custom-call | flops 11744051200 | bytes 24772608 | tf_op jit(solution)/shard_map/pallas_call | solution.py:154
  160.0 2.8 fusion.80
  162.8 11.6 %collective-permute-done.10.refs_0_ = bf16[320,3584]{1,0:T(8,128)(2,1)} collective-permute-done((bf16[320,3584]{1,0:T(8,128)(2,1)}, bf16[320,3584]{1,0:T(8,128)(2,1)}, u32[]{:S(2)}, u32[]{:S(2)}) %collective-permute-start.10) | collective-permute-done | bytes 2293792 | tf_op jit(solution)/shard_map/ppermute | solution.py:18
  174.4 3.1 collective-permute-done.11.refs_1_
  177.5 19.0 %shard_map.133 = (bf16[640,1792]{1,0:T(8,128)(2,1)}, f32[320,128]{1,0:T(8,128)S(1)}) custom-call(bf16[320,3584]{1,0:T(8,128)(2,1)} %collective-permute-done.10.refs_0_, bf16[320,3584]{1,0:T(8,128)(2,1)} %collective-permute-done.11.refs_1_, bf16[304,3584]{1,0:T(8,128)(2,1)} %bitcast.5.refs_1_.refs_2_, ...), custom_call_target="tpu_custom_call" | custom-call | flops 7340032000 | bytes 20643840 | tf_op jit(solution)/shard_map/pallas_call | solution.py:154
  196.6 19.5 %shard_map.135 = (bf16[640,1792]{1,0:T(8,128)(2,1)}, f32[320,128]{1,0:T(8,128)S(1)}) custom-call(bf16[640,3584]{1,0:T(8,128)(2,1)} %bitcast.19.refs_0_, bf16[304,3584]{1,0:T(8,128)(2,1)} %bitcast.5.refs_1_.refs_2_, bf16[304,3584]{1,0:T(8,128)(2,1)} %collective-permute-done.1.refs_2_.refs_3_, bf16[304,3584]{1,0:T(8,128)(2,1)} %bitcast.59, ...), custom_call_target="tpu_custom_call" | custom-call | flops 7340032000 | bytes 20643840 | tf_op jit(solution)/shard_map/pallas_call | solution.py:154
  216.1 7.5 %collective-permute-done.12.refs_0_ = bf16[320,3584]{1,0:T(8,128)(2,1)} collective-permute-done((bf16[320,3584]{1,0:T(8,128)(2,1)}, bf16[320,3584]{1,0:T(8,128)(2,1)}, u32[]{:S(2)}, u32[]{:S(2)}) %collective-permute-start.12) | collective-permute-done | bytes 2293792 | tf_op jit(solution)/shard_map/ppermute | solution.py:18
  223.6 3.1 collective-permute-done.13.refs_1_
  227.8 2.8 collective-permute-start.18
  230.7 19.1 %shard_map.136 = (bf16[640,1792]{1,0:T(8,128)(2,1)}, f32[320,128]{1,0:T(8,128)S(1)}) custom-call(bf16[320,3584]{1,0:T(8,128)(2,1)} %collective-permute-done.12.refs_0_, bf16[320,3584]{1,0:T(8,128)(2,1)} %collective-permute-done.13.refs_1_, bf16[304,3584]{1,0:T(8,128)(2,1)} %bitcast.5.refs_1_.refs_2_, ...), custom_call_target="tpu_custom_call" | custom-call | flops 7340032000 | bytes 20643840 | tf_op jit(solution)/shard_map/pallas_call | solution.py:154
  249.8 6.5 %all-to-all-start.2 = ((bf16[16,40,1792]{2,1,0:T(8,128)(2,1)}), bf16[16,40,1792]{2,1,0:T(8,128)(2,1)}, u32[]{:S(2)}, u32[]{:S(2)}) async-start(bf16[16,40,1792]{2,1,0:T(8,128)(2,1)} %bitcast.46), calls=%async_computation.2 | async-start | bytes 4587520 | tf_op jit(solution)/shard_map/all_to_all | solution.py:30
  256.4 3.2 fusion.82
  259.6 2.7 collective-permute-start.20
  263.9 1.6 collective-permute-start.15
  265.5 1.8 convert_add_fusion.1
  267.4 31.3 %collective-permute-done.19 = bf16[320,1792]{1,0:T(8,128)(2,1)} collective-permute-done((bf16[320,1792]{1,0:T(8,128)(2,1)}, bf16[320,1792]{1,0:T(8,128)(2,1)}, u32[]{:S(2)}, u32[]{:S(2)}) %collective-permute-start.19) | collective-permute-done | bytes 1146912 | tf_op jit(solution)/shard_map/ppermute | solution.py:22
  298.7 1.8 convert_add_fusion
  300.6 1.9 fusion
  302.5 7.4 %all-to-all-start.3 = ((f32[64,1,20]{2,1,0:T(1,128)}), f32[64,1,20]{2,1,0:T(1,128)S(1)}, u32[]{:S(2)}, u32[]{:S(2)}) async-start(f32[64,1,20]{2,1,0:T(1,128)} %bitcast.24), calls=%async_computation.3 | async-start | bytes 65536 | tf_op jit(solution)/shard_map/all_to_all | solution.py:30
  309.9 2.5 fusion.48
  313.8 4.5 %all-to-all-done.3 = f32[64,1,20]{2,1,0:T(1,128)S(1)} async-done(((f32[64,1,20]{2,1,0:T(1,128)}), f32[64,1,20]{2,1,0:T(1,128)S(1)}, u32[]{:S(2)}, u32[]{:S(2)}) %all-to-all-start.3) | async-done | bytes 5152 | tf_op jit(solution)/shard_map/all_to_all | solution.py:30
  318.3 3.7 all-to-all-start.4
  322.0 2.8 fusion.13
  327.3 2.9 fusion.60
  330.4 18.6 %all-to-all-done.4 = bf16[16,40,1792]{2,1,0:T(8,128)(2,1)S(1)} async-done(((bf16[16,40,1792]{2,1,0:T(8,128)(2,1)}), bf16[16,40,1792]{2,1,0:T(8,128)(2,1)S(1)}, u32[]{:S(2)}, u32[]{:S(2)}) %all-to-all-start.4) | async-done | bytes 2293792 | tf_op jit(solution)/shard_map/all_to_all | solution.py:30
  351.6 3.3 fusion.12
  356.1 11.5 %all-to-all-start.5 = ((f32[128,1,476]{2,1,0:T(1,128)}), f32[128,1,476]{2,1,0:T(1,128)S(1)}, u32[]{:S(2)}, u32[]{:S(2)}) async-start(f32[128,1,476]{2,1,0:T(1,128)} %all_to_all.64), calls=%async_computation.5 | async-start | bytes 524288 | tf_op jit(solution)/shard_map/all_to_all | solution.py:30
  367.6 10.8 %all-to-all-done.5 = f32[128,1,476]{2,1,0:T(1,128)S(1)} async-done(((f32[128,1,476]{2,1,0:T(1,128)}), f32[128,1,476]{2,1,0:T(1,128)S(1)}, u32[]{:S(2)}, u32[]{:S(2)}) %all-to-all-start.5) | async-done | bytes 243744 | tf_op jit(solution)/shard_map/all_to_all | solution.py:30
  379.5 4.8 %all-to-all-start.6 = ((f32[128,1,476]{2,1,0:T(1,128)}), f32[128,1,476]{2,1,0:T(1,128)S(1)}, u32[]{:S(2)}, u32[]{:S(2)}) async-start(f32[128,1,476]{2,1,0:T(1,128)} %broadcast_in_dim.119), calls=%async_computation.6 | async-start | bytes 524288 | tf_op jit(solution)/shard_map/all_to_all | solution.py:30
  384.2 2.7 fusion.8
  387.0 8.0 %all-to-all-done.6 = f32[128,1,476]{2,1,0:T(1,128)S(1)} async-done(((f32[128,1,476]{2,1,0:T(1,128)}), f32[128,1,476]{2,1,0:T(1,128)S(1)}, u32[]{:S(2)}, u32[]{:S(2)}) %all-to-all-start.6) | async-done | bytes 243744 | tf_op jit(solution)/shard_map/all_to_all | solution.py:30
  (131 shorter events, 29.9 us)
Async XLA Ops:
  0.6 29.1 %copy-start = (f32[3584,16]{0,1:T(8,128)S(1)}, f32[3584,16]{0,1:T(8,128)}, u32[]{:S(2)}) copy-start(f32[3584,16]{0,1:T(8,128)} %param.14) | copy-start | bytes 688132
  0.6 3.6 copy-start.3
  2.2 0.6 copy-start.11
  4.2 0.7 copy-start.10
  4.9 4.7 %collective-permute-start = (s32[128,2]{0,1:T(2,128)S(1)}, s32[128,2]{0,1:T(2,128)S(1)}, u32[]{:S(2)}, u32[]{:S(2)}) collective-permute-start(s32[128,2]{0,1:T(2,128)S(1)} %copy-done.10), channel_id=1, source_target_pairs={{0,4},{2,6},{4,0},{6,2},{1,5},{3,7},{5,1},{7,3},{8,12},{10,14},{12... | collective-permute-start | bytes 3080 | tf_op jit(solution)/shard_map/ppermute | solution.py:18
  8.7 59.3 %collective-permute-start.1 = (bf16[304,3584]{1,0:T(8,128)(2,1)}, bf16[304,3584]{1,0:T(8,128)(2,1)}, u32[]{:S(2)}, u32[]{:S(2)}) collective-permute-start(bf16[304,3584]{1,0:T(8,128)(2,1)} %bitcast.5.refs_1_.refs_2_), channel_id=1, source_target_pairs={{0,1},{1,0},{2,3},{3,2},{4,5},{5,4},{6,7},{7,6},{8,9},{9,8},{10,11... | collective-permute-start | bytes 6537224 | tf_op jit(solution)/shard_map/ppermute | solution.py:26
  16.1 70.2 %all-to-all-start = ((bf16[16,40,3584]{2,1,0:T(8,128)(2,1)}), bf16[16,40,3584]{2,1,0:T(8,128)(2,1)}, u32[]{:S(2)}, u32[]{:S(2)}) async-start(bf16[16,40,3584]{2,1,0:T(8,128)(2,1)} %bitcast.43), calls=%async_computation | async-start | bytes 9175040 | tf_op jit(solution)/shard_map/all_to_all | solution.py:30
  23.8 41.1 %collective-permute-start.8 = (bf16[256,3584]{1,0:T(8,128)(2,1)S(1)}, bf16[256,3584]{1,0:T(8,128)(2,1)}, u32[]{:S(2)}, u32[]{:S(2)}) collective-permute-start(bf16[256,3584]{1,0:T(8,128)(2,1)S(1)} %pad_maximum_fusion.rows.refs_0_), channel_id=1, source_target_pairs={{0,4},{2,6},{4,0},{6,2},{1,5},{3,7},{5,1},{7,3},{8,12},{10,14},{12... | collective-permute-start | bytes 5505032 | tf_op jit(solution)/shard_map/ppermute | solution.py:18
  26.8 56.6 %collective-permute-start.2 = (bf16[304,3584]{1,0:T(8,128)(2,1)}, bf16[304,3584]{1,0:T(8,128)(2,1)}, u32[]{:S(2)}, u32[]{:S(2)}) collective-permute-start(bf16[304,3584]{1,0:T(8,128)(2,1)} %bitcast.56), channel_id=1, source_target_pairs={{0,1},{1,0},{2,3},{3,2},{4,5},{5,4},{6,7},{7,6},{8,9},{9,8},{10,11... | collective-permute-start | bytes 6537224 | tf_op jit(solution)/shard_map/ppermute | solution.py:26
  29.2 54.3 %collective-permute-start.3 = (bf16[304,3584]{1,0:T(8,128)(2,1)}, bf16[304,3584]{1,0:T(8,128)(2,1)}, u32[]{:S(2)}, u32[]{:S(2)}) collective-permute-start(bf16[304,3584]{1,0:T(8,128)(2,1)} %bitcast.61), channel_id=1, source_target_pairs={{0,1},{1,0},{2,3},{3,2},{4,5},{5,4},{6,7},{7,6},{8,9},{9,8},{10,11... | collective-permute-start | bytes 6537224 | tf_op jit(solution)/shard_map/ppermute | solution.py:26
  29.2 54.3 %collective-permute-start.4 = (bf16[304,3584]{1,0:T(8,128)(2,1)}, bf16[304,3584]{1,0:T(8,128)(2,1)}, u32[]{:S(2)}, u32[]{:S(2)}) collective-permute-start(bf16[304,3584]{1,0:T(8,128)(2,1)} %bitcast.52), channel_id=1, source_target_pairs={{0,1},{1,0},{2,3},{3,2},{4,5},{5,4},{6,7},{7,6},{8,9},{9,8},{10,11... | collective-permute-start | bytes 6537224 | tf_op jit(solution)/shard_map/ppermute | solution.py:26
  64.9 18.5 %collective-permute-start.5 = (bf16[304,3584]{1,0:T(8,128)(2,1)}, bf16[304,3584]{1,0:T(8,128)(2,1)}, u32[]{:S(2)}, u32[]{:S(2)}) collective-permute-start(bf16[304,3584]{1,0:T(8,128)(2,1)} %bitcast.54), channel_id=1, source_target_pairs={{0,1},{1,0},{2,3},{3,2},{4,5},{5,4},{6,7},{7,6},{8,9},{9,8},{10,11... | collective-permute-start | bytes 6537224 | tf_op jit(solution)/shard_map/ppermute | solution.py:26
  67.9 15.5 %collective-permute-start.6 = (bf16[304,3584]{1,0:T(8,128)(2,1)}, bf16[304,3584]{1,0:T(8,128)(2,1)}, u32[]{:S(2)}, u32[]{:S(2)}) collective-permute-start(bf16[304,3584]{1,0:T(8,128)(2,1)} %refs_8_.1), channel_id=1, source_target_pairs={{0,1},{1,0},{2,3},{3,2},{4,5},{5,4},{6,7},{7,6},{8,9},{9,8},{10,11... | collective-permute-start | bytes 6537224 | tf_op jit(solution)/shard_map/ppermute | solution.py:26
  83.5 41.7 %collective-permute-start.7 = (bf16[256,3584]{1,0:T(8,128)(2,1)S(1)}, bf16[256,3584]{1,0:T(8,128)(2,1)}, u32[]{:S(2)}, u32[]{:S(2)}) collective-permute-start(bf16[256,3584]{1,0:T(8,128)(2,1)S(1)} %pad_maximum_fusion.rows.refs_0_), channel_id=1, source_target_pairs={{0,6},{2,0},{4,2},{6,4},{1,7},{3,1},{5,3},{7,5},{8,14},{10,8},{12,... | collective-permute-start | bytes 5505032 | tf_op jit(solution)/shard_map/ppermute | solution.py:18
  86.3 51.7 %collective-permute-start.9 = (bf16[256,3584]{1,0:T(8,128)(2,1)S(1)}, bf16[256,3584]{1,0:T(8,128)(2,1)}, u32[]{:S(2)}, u32[]{:S(2)}) collective-permute-start(bf16[256,3584]{1,0:T(8,128)(2,1)S(1)} %pad_maximum_fusion.rows.refs_0_), channel_id=1, source_target_pairs={{0,2},{2,4},{4,6},{6,0},{1,3},{3,5},{5,7},{7,1},{8,10},{10,12},{12... | collective-permute-start | bytes 5505032 | tf_op jit(solution)/shard_map/ppermute | solution.py:18
  86.3 110.3 %all-to-all-start.1 = ((bf16[16,40,3584]{2,1,0:T(8,128)(2,1)}), bf16[16,40,3584]{2,1,0:T(8,128)(2,1)}, u32[]{:S(2)}, u32[]{:S(2)}) async-start(bf16[16,40,3584]{2,1,0:T(8,128)(2,1)} %bitcast.44), calls=%async_computation.1 | async-start | bytes 9175040 | tf_op jit(solution)/shard_map/all_to_all | solution.py:30
  97.8 76.7 %collective-permute-start.10 = (bf16[320,3584]{1,0:T(8,128)(2,1)}, bf16[320,3584]{1,0:T(8,128)(2,1)}, u32[]{:S(2)}, u32[]{:S(2)}) collective-permute-start(bf16[320,3584]{1,0:T(8,128)(2,1)} %bitcast.14), channel_id=1, source_target_pairs={{0,6},{2,0},{4,2},{6,4},{1,7},{3,1},{5,3},{7,5},{8,14},{10,8},{12,... | collective-permute-start | bytes 6881288 | tf_op jit(solution)/shard_map/ppermute | solution.py:18
  100.4 77.1 %collective-permute-start.11 = (bf16[320,3584]{1,0:T(8,128)(2,1)}, bf16[320,3584]{1,0:T(8,128)(2,1)}, u32[]{:S(2)}, u32[]{:S(2)}) collective-permute-start(bf16[320,3584]{1,0:T(8,128)(2,1)} %bitcast.14), channel_id=1, source_target_pairs={{0,2},{2,4},{4,6},{6,0},{1,3},{3,5},{5,7},{7,1},{8,10},{10,12},{12... | collective-permute-start | bytes 6881288 | tf_op jit(solution)/shard_map/ppermute | solution.py:18
  119.7 103.9 %collective-permute-start.12 = (bf16[320,3584]{1,0:T(8,128)(2,1)}, bf16[320,3584]{1,0:T(8,128)(2,1)}, u32[]{:S(2)}, u32[]{:S(2)}) collective-permute-start(bf16[320,3584]{1,0:T(8,128)(2,1)} %bitcast.15), channel_id=1, source_target_pairs={{0,6},{2,0},{4,2},{6,4},{1,7},{3,1},{5,3},{7,5},{8,14},{10,8},{12,... | collective-permute-start | bytes 6881288 | tf_op jit(solution)/shard_map/ppermute | solution.py:18
  125.2 101.5 %collective-permute-start.13 = (bf16[320,3584]{1,0:T(8,128)(2,1)}, bf16[320,3584]{1,0:T(8,128)(2,1)}, u32[]{:S(2)}, u32[]{:S(2)}) collective-permute-start(bf16[320,3584]{1,0:T(8,128)(2,1)} %bitcast.15), channel_id=1, source_target_pairs={{0,2},{2,4},{4,6},{6,0},{1,3},{3,5},{5,7},{7,1},{8,10},{10,12},{12... | collective-permute-start | bytes 6881288 | tf_op jit(solution)/shard_map/ppermute | solution.py:18
  196.6 30.1 %copy-start.5 = (bf16[640,1792]{1,0:T(8,128)(2,1)S(1)}, bf16[640,1792]{1,0:T(8,128)(2,1)}, u32[]{:S(2)}) copy-start(bf16[640,1792]{1,0:T(8,128)(2,1)} %get-tuple-element.42) | copy-start | bytes 6881284
  227.8 36.0 %collective-permute-start.17 = (bf16[320,1792]{1,0:T(8,128)(2,1)}, bf16[320,1792]{1,0:T(8,128)(2,1)}, u32[]{:S(2)}, u32[]{:S(2)}) collective-permute-start(bf16[320,1792]{1,0:T(8,128)(2,1)} %get-tuple-element.66), channel_id=1, source_target_pairs={{0,2},{2,4},{4,6},{6,0},{1,3},{3,5},{5,7},{7,1},{8,10},{10,12},{12... | collective-permute-start | bytes 3440648 | tf_op jit(solution)/shard_map/ppermute | solution.py:22
  227.8 37.7 %collective-permute-start.18 = (bf16[320,1792]{1,0:T(8,128)(2,1)S(1)}, bf16[320,1792]{1,0:T(8,128)(2,1)}, u32[]{:S(2)}, u32[]{:S(2)}) collective-permute-start(bf16[320,1792]{1,0:T(8,128)(2,1)S(1)} %get-tuple-element.67), channel_id=1, source_target_pairs={{0,6},{2,0},{4,2},{6,4},{1,7},{3,1},{5,3},{7,5},{8,14},{10,8},{12,... | collective-permute-start | bytes 3440648 | tf_op jit(solution)/shard_map/ppermute | solution.py:22
  249.8 100.3 %collective-permute-start.14 = (bf16[128,3584]{1,0:T(8,128)(2,1)}, bf16[128,3584]{1,0:T(8,128)(2,1)}, u32[]{:S(2)}, u32[]{:S(2)}) collective-permute-start(bf16[128,3584]{1,0:T(8,128)(2,1)} %get-tuple-element.40), channel_id=1, source_target_pairs={{0,2},{2,4},{4,6},{6,0},{1,3},{3,5},{5,7},{7,1},{8,10},{10,12},{12... | collective-permute-start | bytes 2752520 | tf_op jit(solution)/shard_map/ppermute | solution.py:22
  249.8 52.7 %all-to-all-start.2 = ((bf16[16,40,1792]{2,1,0:T(8,128)(2,1)}), bf16[16,40,1792]{2,1,0:T(8,128)(2,1)}, u32[]{:S(2)}, u32[]{:S(2)}) async-start(bf16[16,40,1792]{2,1,0:T(8,128)(2,1)} %bitcast.46), calls=%async_computation.2 | async-start | bytes 4587520 | tf_op jit(solution)/shard_map/all_to_all | solution.py:30
  256.4 6.8 %copy-start.15 = (pred[4,4]{1,0:T(4,128)(4,1)S(1)}, pred[4,4]{1,0:T(4,128)(4,1)}, u32[]{:S(2)}) copy-start(pred[4,4]{1,0:T(4,128)(4,1)} %select_compare_fusion) | copy-start | bytes 52
  259.6 39.1 %collective-permute-start.19 = (bf16[320,1792]{1,0:T(8,128)(2,1)}, bf16[320,1792]{1,0:T(8,128)(2,1)}, u32[]{:S(2)}, u32[]{:S(2)}) collective-permute-start(bf16[320,1792]{1,0:T(8,128)(2,1)} %get-tuple-element.68), channel_id=1, source_target_pairs={{0,2},{2,4},{4,6},{6,0},{1,3},{3,5},{5,7},{7,1},{8,10},{10,12},{12... | collective-permute-start | bytes 3440648 | tf_op jit(solution)/shard_map/ppermute | solution.py:22
  259.6 39.1 %collective-permute-start.20 = (bf16[320,1792]{1,0:T(8,128)(2,1)}, bf16[320,1792]{1,0:T(8,128)(2,1)}, u32[]{:S(2)}, u32[]{:S(2)}) collective-permute-start(bf16[320,1792]{1,0:T(8,128)(2,1)} %get-tuple-element.69), channel_id=1, source_target_pairs={{0,6},{2,0},{4,2},{6,4},{1,7},{3,1},{5,3},{7,5},{8,14},{10,8},{12,... | collective-permute-start | bytes 3440648 | tf_op jit(solution)/shard_map/ppermute | solution.py:22
  263.9 86.2 %collective-permute-start.15 = (bf16[128,3584]{1,0:T(8,128)(2,1)}, bf16[128,3584]{1,0:T(8,128)(2,1)}, u32[]{:S(2)}, u32[]{:S(2)}) collective-permute-start(bf16[128,3584]{1,0:T(8,128)(2,1)} %get-tuple-element.41), channel_id=1, source_target_pairs={{0,6},{2,0},{4,2},{6,4},{1,7},{3,1},{5,3},{7,5},{8,14},{10,8},{12,... | collective-permute-start | bytes 2752520 | tf_op jit(solution)/shard_map/ppermute | solution.py:22
  267.3 33.2 %copy-start.4 = (bf16[640,1792]{1,0:T(8,128)(2,1)S(1)}, bf16[640,1792]{1,0:T(8,128)(2,1)}, u32[]{:S(2)}) copy-start(bf16[640,1792]{1,0:T(8,128)(2,1)} %get-tuple-element.25) | copy-start | bytes 6881284
  300.5 9.4 %copy-start.7 = (bf16[128,640]{1,0:T(8,128)(2,1)S(1)}, bf16[128,640]{1,0:T(8,128)(2,1)}, u32[]{:S(2)}) copy-start(bf16[128,640]{1,0:T(8,128)(2,1)} %get-tuple-element.49) | copy-start | bytes 491524
  300.5 9.3 %copy-start.8 = (bf16[128,640]{1,0:T(8,128)(2,1)S(1)}, bf16[128,640]{1,0:T(8,128)(2,1)}, u32[]{:S(2)}) copy-start(bf16[128,640]{1,0:T(8,128)(2,1)} %get-tuple-element.50) | copy-start | bytes 491524
  302.5 15.8 %all-to-all-start.3 = ((f32[64,1,20]{2,1,0:T(1,128)}), f32[64,1,20]{2,1,0:T(1,128)S(1)}, u32[]{:S(2)}, u32[]{:S(2)}) async-start(f32[64,1,20]{2,1,0:T(1,128)} %bitcast.24), calls=%async_computation.3 | async-start | bytes 65536 | tf_op jit(solution)/shard_map/all_to_all | solution.py:30
  318.3 30.7 %all-to-all-start.4 = ((bf16[16,40,1792]{2,1,0:T(8,128)(2,1)}), bf16[16,40,1792]{2,1,0:T(8,128)(2,1)S(1)}, u32[]{:S(2)}, u32[]{:S(2)}) async-start(bf16[16,40,1792]{2,1,0:T(8,128)(2,1)} %bitcast.27), calls=%async_computation.4 | async-start | bytes 4587520 | tf_op jit(solution)/shard_map/all_to_all | solution.py:30
  322.0 3.9 copy-start.14
  322.0 4.0 %copy-start.13 = (f32[128,2]{0,1:T(2,128)S(1)}, f32[128,2]{0,1:T(2,128)}, u32[]{:S(2)}) copy-start(f32[128,2]{0,1:T(2,128)} %select_reduce_fusion.7) | copy-start | bytes 3076
  324.9 25.2 %collective-permute-start.16 = (bf16[128,3584]{1,0:T(8,128)(2,1)}, bf16[128,3584]{1,0:T(8,128)(2,1)}, u32[]{:S(2)}, u32[]{:S(2)}) collective-permute-start(bf16[128,3584]{1,0:T(8,128)(2,1)} %fusion.13), channel_id=1, source_target_pairs={{0,4},{2,6},{4,0},{6,2},{1,5},{3,7},{5,1},{7,3},{8,12},{10,14},{12... | collective-permute-start | bytes 2752520 | tf_op jit(solution)/shard_map/ppermute | solution.py:22
  349.8 1.2 copy-start.1
  349.8 1.8 copy-start.2
  349.9 1.8 copy-start.9
  349.9 1.8 copy-start.12
  351.6 3.3 copy-start.6
  356.1 22.2 %all-to-all-start.5 = ((f32[128,1,476]{2,1,0:T(1,128)}), f32[128,1,476]{2,1,0:T(1,128)S(1)}, u32[]{:S(2)}, u32[]{:S(2)}) async-start(f32[128,1,476]{2,1,0:T(1,128)} %all_to_all.64), calls=%async_computation.5 | async-start | bytes 524288 | tf_op jit(solution)/shard_map/all_to_all | solution.py:30
  379.5 15.5 %all-to-all-start.6 = ((f32[128,1,476]{2,1,0:T(1,128)}), f32[128,1,476]{2,1,0:T(1,128)S(1)}, u32[]{:S(2)}, u32[]{:S(2)}) async-start(f32[128,1,476]{2,1,0:T(1,128)} %broadcast_in_dim.119), calls=%async_computation.6 | async-start | bytes 524288 | tf_op jit(solution)/shard_map/all_to_all | solution.py:30

commit v7 on v6

--- a/solution.py
+++ b/solution.py
@@ -35,8 +35,7 @@
 
 
 def weight_pieces(gate, up, down):
-    both = [gate.T, up.T, down]
-    return [piece for value in both for piece in (value, swap(value))]
+    return [lax.all_gather(v, "core", axis=0, tiled=True) for v in (gate.T, up.T, down)]
 
 
 def shuffle_table(cap, group):
@@ -49,8 +48,8 @@
 
 def hidden_kernel(count, mixed, *refs):
     sources = refs[:count]
-    pieces = refs[count : count + 6]
-    refs = refs[count + 6 :]
+    pieces = refs[count : count + 3]
+    refs = refs[count + 3 :]
     if mixed:
         table, table_back = refs[:2]
         refs = refs[2:]
@@ -58,22 +57,18 @@
     step = pl.program_id(0)
     part, width = pieces[0].shape
     half = weights.shape[0] // 3
-    copies = []
-    for i in range(6):
-        start = i // 2 * half + i % 2 * part
-        copies.append(
-            pltpu.make_async_copy(pieces[i], weights.at[pl.ds(start, part), :], sems.at[i])
-        )
+    copies = [
+        pltpu.make_async_copy(pieces[i], weights.at[pl.ds(i * half, part), :], sems.at[i])
+        for i in range(3)
+    ]
 
     @pl.when(step == 0)
     def _():
-        for copy in copies[4:] + copies[:4]:
+        for copy in copies[2:] + copies[:2]:
             copy.start()
-        if half > 2 * part:
+        if half > part:
             for i in range(3):
-                weights[i * half + 2 * part : (i + 1) * half, :] = jnp.zeros(
-                    (half - 2 * part, width), BF
-                )
+                weights[i * half + part : (i + 1) * half, :] = jnp.zeros((half - part, width), BF)
 
     size = sources[0].shape[0] // 2
     each = normed.shape[0] // size
@@ -104,11 +99,11 @@
             for copy in copies[i:j]:
                 copy.wait()
 
-    wait(4, 6)
+    wait(2, 3)
     back[...] = lax.dot_general(
         other[...], weights[2 * half :, :], TRANS, preferred_element_type=F32
     )
-    wait(0, 4)
+    wait(0, 2)
     both[...] = lax.dot_general(
         normed[...], weights[: 2 * half, :], TRANS, preferred_element_type=F32
     )
@@ -142,7 +137,7 @@
     mixed = len(tables) > 0
     size = sources[0].shape[0] // 2
     part, width = pieces[0].shape
-    half = -(-2 * part // 128) * 128
+    half = -(-part // 128) * 128
     total = count * size
     step_rows = min(total, 320) if mixed else 2 * size
     out = (2 * total, width // 2) if mixed else (total, width)
@@ -155,7 +150,7 @@
         lambda *refs: hidden_kernel(count, mixed, *refs),
         grid=(total // step_rows,),
         in_specs=[whole(v) for v in sources]
-        + [pl.BlockSpec(memory_space=pl.ANY)] * 6
+        + [pl.BlockSpec(memory_space=pl.ANY)] * 3
         + [whole(v) for v in tables],
         out_specs=[
             pl.BlockSpec(block, lambda i: (i, 0)),
@@ -169,7 +164,7 @@
             pltpu.VMEM((step_rows, 2 * half), F32),
             pltpu.VMEM((step_rows, half), F32),
             pltpu.VMEM((step_rows, 2 * half), BF),
-            pltpu.SemaphoreType.DMA((6,)),
+            pltpu.SemaphoreType.DMA((3,)),
         ],
         compiler_params=pltpu.CompilerParams(vmem_limit_bytes=VMEM_LIMIT),
         cost_estimate=pl.CostEstimate(
@@ -272,8 +267,7 @@
     peer_routes = {k: receive_from(routes_in, k) for k in (1, 2, 3)}
     expert = weight_pieces(expert_gate[0], expert_up[0], expert_down[0])
     dense = weight_pieces(dense_gate, dense_up, dense_down)
-    later = after(pair, *expert, *dense)
-    peer = {k: receive_from(later if k != 2 else pair, k) for k in (2, 1, 3)}
+    peer = {k: receive_from(pair, k) for k in (2, 1, 3)}
 
     def to_experts(rows, index):
         places = jnp.concatenate([index, index + cap], 0)
@@ -294,16 +288,17 @@
     dense_part, unused = hidden_grads(
         [after(pair, own_into)] + [peer[k] for k in (1, 2, 3)], dense
     )
+    far_into, far_joint = hidden_grads([after(far, dense_part)], expert, tables)
+    far_back = over(far_into)
     near_into = [None, None]
     near_joint = [None, None]
     near_into[0], near_joint[0] = hidden_grads(
-        [after(near[0][1], dense_part), near[0][3]], expert, tables
-    )
-    far_into, far_joint = hidden_grads([after(far, near_into[0])], expert, tables)
-    far_back = over(far_into)
+        [after(near[0][1], far_into), near[0][3]], expert, tables
+    )
     near_into[1], near_joint[1] = hidden_grads(
-        [after(near[1][1], far_into), near[1][3]], expert, tables
-    )
+        [after(near[1][1], near_into[0]), near[1][3]], expert, tables
+    )
+    near_into[1] = after(near_into[1], far_back)
     arrived = (near[1][1], near[1][3])
     near_back = []
     for i in (0, 1):

time: 405 us -> 383 us (0.946)
  starting transfers between devices: 91.2 us -> 75 us
  between operations: 1.47 us -> 15.2 us
  waiting for transfers between devices: 135 us -> 128 us
  Pallas kernels: 110 us -> 105 us
  other arithmetic: 24 us -> 19.8 us
    ppermute x7, waiting for transfers between devices: 31.3 us -> 8.95 us  [send_to(): lax.ppermute(value, 'y', [(i, (i + k) % PEERS) for i in range(PEERS)])]
    all_to_all x7, waiting for transfers between devices: 41.9 us -> 63 us  [over(): return lax.all_to_all(value, axes, split_axis=0, concat_axis=0, tiled=True)]
    ppermute x8, starting transfers between devices: 28 us -> 14.2 us  [receive_from(): lax.ppermute(value, 'y', [(i, (i - k) % PEERS) for i in range(PEERS)])]
    ppermute x8, waiting for transfers between devices: 61.5 us -> 50 us  [receive_from(): lax.ppermute(value, 'y', [(i, (i - k) % PEERS) for i in range(PEERS)])]
    ppermute x6 -> x0, starting transfers between devices: 6.89 us -> none  [swap(): return lax.ppermute(value, 'core', [(0, 1), (1, 0)])]
    pallas_call x5, Pallas kernels: 98.6 us -> 93.7 us  [hidden_grads(): pl.pallas_call(lambda *refs: hidden_kernel(count, mixed, *refs), grid=(to...]
  transfers between devices with their start and end apart: 28 -> 28, of which waited for: 11 -> 13; matrix products, arithmetic and copies ran while one was open for 11% -> 11% of each run, Pallas kernels for 28% -> 28%
where the time goes in v7:
time: 383 us; the launch traced here: 376 us
  waiting for transfers between devices  128 us (33%)
  Pallas kernels  105 us (27%)
  starting transfers between devices  75 us (20%)
  local copies, waits for them, and re-layouts  22.8 us (6%)
  other arithmetic  19.8 us (5%)
  between operations  15.2 us (4%)
  matrix products  10.6 us (3%)
    pallas_call x5, Pallas kernels, hidden_grads(): pl.pallas_call(lambda *refs: hidden_kernel(count, mixed, *refs), grid=(to...  93.7 us
    all_to_all x7, waiting for transfers between devices, over(): return lax.all_to_all(value, axes, split_axis=0, concat_axis=0, tiled=True)  63 us
    all_to_all x7, starting transfers between devices, over(): return lax.all_to_all(value, axes, split_axis=0, concat_axis=0, tiled=True)  50.9 us
    ppermute x8, waiting for transfers between devices, receive_from(): lax.ppermute(value, 'y', [(i, (i - k) % PEERS) for i in range(PEERS)])  50 us
    ppermute x8, starting transfers between devices, receive_from(): lax.ppermute(value, 'y', [(i, (i - k) % PEERS) for i in range(PEERS)])  14.2 us
    pallas_call x2, Pallas kernels, pick_rows(): pl.pallas_call(pick_kernel, grid=(width // block,), in_specs=[pl.BlockSpe...  11.7 us
    ppermute x7, starting transfers between devices, send_to(): lax.ppermute(value, 'y', [(i, (i + k) % PEERS) for i in range(PEERS)])  9.63 us
    ppermute x7, waiting for transfers between devices, send_to(): lax.ppermute(value, 'y', [(i, (i + k) % PEERS) for i in range(PEERS)])  8.95 us
  transfers between devices with their start and end apart: 28, of which 13 were waited for; matrix products, arithmetic and copies ran while one was open for 11% of the time, Pallas kernels for 28%

profile of v7, /device:TPU:1, one launch (start us, length us, event | category | flops | bytes accessed | tf_op | source)
XLA Modules:
  0.0 376.3 jit_solution(230893504920895764)
XLA Ops:
  12.5 3.7 collective-permute-start
  18.7 5.0 %shard_map.130 = bf16[640,3584]{1,0:T(8,128)(2,1)} custom-call(bf16[640,256]{1,0:T(8,128)(2,1)S(1)} %fusion.47.table, bf16[256,3584]{1,0:T(8,128)(2,1)S(1)} %pad_maximum_fusion.rows.refs_0_), custom_call_target="tpu_custom_call" | custom-call | flops 1174405120 | bytes 6422528 | tf_op jit(solution)/shard_map/pallas_call | solution.py:187
  23.6 7.7 %all-to-all-start = ((bf16[16,40,3584]{2,1,0:T(8,128)(2,1)}), bf16[16,40,3584]{2,1,0:T(8,128)(2,1)}, u32[]{:S(2)}, u32[]{:S(2)}) async-start(bf16[16,40,3584]{2,1,0:T(8,128)(2,1)} %bitcast.43), calls=%async_computation | async-start | bytes 9175040 | tf_op jit(solution)/shard_map/all_to_all | solution.py:30
  31.4 3.0 collective-permute-start.2
  39.5 33.0 %collective-permute-done.2.refs_2_.rows = bf16[256,3584]{1,0:T(8,128)(2,1)} collective-permute-done((bf16[256,3584]{1,0:T(8,128)(2,1)S(1)}, bf16[256,3584]{1,0:T(8,128)(2,1)}, u32[]{:S(2)}, u32[]{:S(2)}) %collective-permute-start.2) | collective-permute-done | bytes 1835040 | tf_op jit(solution)/shard_map/ppermute | solution.py:18
  72.5 6.7 %shard_map.133 = bf16[640,3584]{1,0:T(8,128)(2,1)} custom-call(bf16[640,256]{1,0:T(8,128)(2,1)S(1)} %fusion.46.table, bf16[256,3584]{1,0:T(8,128)(2,1)} %collective-permute-done.2.refs_2_.rows), custom_call_target="tpu_custom_call" | custom-call | flops 1174405120 | bytes 6422528 | tf_op jit(solution)/shard_map/pallas_call | solution.py:187
  79.2 2.0 fusion.24
  81.3 6.2 %all-to-all-done = bf16[16,40,3584]{2,1,0:T(8,128)(2,1)} async-done(((bf16[16,40,3584]{2,1,0:T(8,128)(2,1)}), bf16[16,40,3584]{2,1,0:T(8,128)(2,1)}, u32[]{:S(2)}, u32[]{:S(2)}) %all-to-all-start) | async-done | bytes 4587552 | tf_op jit(solution)/shard_map/all_to_all | solution.py:30
  87.4 7.8 %all-to-all-start.1 = ((bf16[16,40,3584]{2,1,0:T(8,128)(2,1)}), bf16[16,40,3584]{2,1,0:T(8,128)(2,1)}, u32[]{:S(2)}, u32[]{:S(2)}) async-start(bf16[16,40,3584]{2,1,0:T(8,128)(2,1)} %bitcast.44), calls=%async_computation.1 | async-start | bytes 9175040 | tf_op jit(solution)/shard_map/all_to_all | solution.py:30
  95.4 4.8 %fusion.79 = (bf16[8,40,3584]{2,1,0:T(8,128)(2,1)}, bf16[8,40,3584]{2,1,0:T(8,128)(2,1)}) fusion(bf16[16,40,3584]{2,1,0:T(8,128)(2,1)} %all-to-all-done), kind=kLoop, calls=%fused_computation.161 | loop fusion | bytes 9175040 | tf_op jit(solution)/shard_map/slice | solution.py:282
  100.2 2.6 collective-permute-start.4
  102.9 2.9 collective-permute-start.6
  105.7 17.5 %shard_map.131 = (bf16[640,1792]{1,0:T(8,128)(2,1)S(1)}, f32[320,128]{1,0:T(8,128)S(1)}) custom-call(bf16[640,3584]{1,0:T(8,128)(2,1)} %bitcast.3.refs_0_, bf16[608,3584]{1,0:T(8,128)(2,1)} %all-gather.8.cloned.1.call-done.refs_1_.refs_2_, bf16[608,3584]{1,0:T(8,128)(2,1)} %all-gather.10.cloned.1.call-done.refs_2_.refs_3_, bf16[608,3584]{1,0:T(8,128)(2,1)} %bitcast.55, ...), custom_call_target="tpu_custom_call" | custom-call | flops 7340032000 | bytes 20643840 | tf_op jit(solution)/shard_map/pallas_call | solution.py:149
  123.3 1.4 copy-done.1
  125.3 2.4 all-gather.16.cloned.1.call-done.refs_6_
  127.7 22.0 %shard_map.132 = (bf16[512,3584]{1,0:T(8,128)(2,1)}, f32[512,128]{1,0:T(8,128)}) custom-call(bf16[256,3584]{1,0:T(8,128)(2,1)S(1)} %pad_maximum_fusion.rows.refs_0_, bf16[256,3584]{1,0:T(8,128)(2,1)} %collective-permute-done.1.refs_1_, bf16[256,3584]{1,0:T(8,128)(2,1)} %collective-permute-done.2.refs_2_.rows, ...), custom_call_target="tpu_custom_call" | custom-call | flops 11744051200 | bytes 24772608 | tf_op jit(solution)/shard_map/pallas_call | solution.py:149
  149.9 2.8 fusion.80
  152.7 19.0 %shard_map.134 = (bf16[640,1792]{1,0:T(8,128)(2,1)}, f32[320,128]{1,0:T(8,128)S(1)}) custom-call(bf16[640,3584]{1,0:T(8,128)(2,1)} %bitcast.16.refs_0_, bf16[608,3584]{1,0:T(8,128)(2,1)} %all-gather.8.cloned.1.call-done.refs_1_.refs_2_, bf16[608,3584]{1,0:T(8,128)(2,1)} %all-gather.10.cloned.1.call-done.refs_2_.refs_3_, bf16[608,3584]{1,0:T(8,128)(2,1)} %bitcast.56, ...), custom_call_target="tpu_custom_call" | custom-call | flops 7340032000 | bytes 20643840 | tf_op jit(solution)/shard_map/pallas_call | solution.py:149
  171.7 7.0 %all-to-all-start.2 = ((bf16[16,40,1792]{2,1,0:T(8,128)(2,1)}), bf16[16,40,1792]{2,1,0:T(8,128)(2,1)}, u32[]{:S(2)}, u32[]{:S(2)}) async-start(bf16[16,40,1792]{2,1,0:T(8,128)(2,1)} %bitcast.19), calls=%async_computation.2 | async-start | bytes 4587520 | tf_op jit(solution)/shard_map/all_to_all | solution.py:30
  179.0 17.6 %shard_map.135 = (bf16[640,1792]{1,0:T(8,128)(2,1)S(1)}, f32[320,128]{1,0:T(8,128)S(1)}) custom-call(bf16[320,3584]{1,0:T(8,128)(2,1)} %collective-permute-done.4.refs_0_, bf16[320,3584]{1,0:T(8,128)(2,1)} %collective-permute-done.5.refs_1_, bf16[608,3584]{1,0:T(8,128)(2,1)} %all-gather.8.cloned.1.call-done.refs_1_.refs_2_, ...), custom_call_target="tpu_custom_call" | custom-call | flops 7340032000 | bytes 20643840 | tf_op jit(solution)/shard_map/pallas_call | solution.py:149
  196.6 15.4 %collective-permute-done.6.refs_0_ = bf16[320,3584]{1,0:T(8,128)(2,1)} collective-permute-done((bf16[320,3584]{1,0:T(8,128)(2,1)}, bf16[320,3584]{1,0:T(8,128)(2,1)}, u32[]{:S(2)}, u32[]{:S(2)}) %collective-permute-start.6) | collective-permute-done | bytes 2293792 | tf_op jit(solution)/shard_map/ppermute | solution.py:18
  212.6 1.5 fusion.81
  214.2 1.3 collective-permute-start.11
  215.5 1.6 collective-permute-start.12
  217.1 17.6 %shard_map.136 = (bf16[640,1792]{1,0:T(8,128)(2,1)S(1)}, f32[320,128]{1,0:T(8,128)S(1)}) custom-call(bf16[320,3584]{1,0:T(8,128)(2,1)} %collective-permute-done.6.refs_0_, bf16[320,3584]{1,0:T(8,128)(2,1)} %collective-permute-done.7.refs_1_, bf16[608,3584]{1,0:T(8,128)(2,1)} %all-gather.8.cloned.1.call-done.refs_1_.refs_2_, ...), custom_call_target="tpu_custom_call" | custom-call | flops 7340032000 | bytes 20643840 | tf_op jit(solution)/shard_map/pallas_call | solution.py:149
  236.1 1.6 fusion.82
  237.7 2.7 collective-permute-start.14
  240.3 1.4 collective-permute-done.11
  241.8 1.8 convert_add_fusion.1
  243.7 1.5 collective-permute-start.8
  246.4 9.1 %all-to-all-start.3 = ((f32[64,1,20]{2,1,0:T(1,128)}), f32[64,1,20]{2,1,0:T(1,128)S(1)}, u32[]{:S(2)}, u32[]{:S(2)}) async-start(f32[64,1,20]{2,1,0:T(1,128)} %bitcast.22), calls=%async_computation.3 | async-start | bytes 65536 | tf_op jit(solution)/shard_map/all_to_all | solution.py:30
  255.5 2.5 fusion.48
  258.0 1.4 fusion.83
  259.4 7.4 %collective-permute-done.13 = bf16[320,1792]{1,0:T(8,128)(2,1)} collective-permute-done((bf16[320,1792]{1,0:T(8,128)(2,1)}, bf16[320,1792]{1,0:T(8,128)(2,1)}, u32[]{:S(2)}, u32[]{:S(2)}) %collective-permute-start.13) | collective-permute-done | bytes 1146912 | tf_op jit(solution)/shard_map/ppermute | solution.py:22
  266.8 1.8 convert_add_fusion
  268.6 2.0 fusion
  270.6 19.3 %all-to-all-done.3 = f32[64,1,20]{2,1,0:T(1,128)S(1)} async-done(((f32[64,1,20]{2,1,0:T(1,128)}), f32[64,1,20]{2,1,0:T(1,128)S(1)}, u32[]{:S(2)}, u32[]{:S(2)}) %all-to-all-start.3) | async-done | bytes 5152 | tf_op jit(solution)/shard_map/all_to_all | solution.py:30
  290.0 4.7 %all-to-all-start.4 = ((bf16[16,40,1792]{2,1,0:T(8,128)(2,1)}), bf16[16,40,1792]{2,1,0:T(8,128)(2,1)S(1)}, u32[]{:S(2)}, u32[]{:S(2)}) async-start(bf16[16,40,1792]{2,1,0:T(8,128)(2,1)} %bitcast.25), calls=%async_computation.4 | async-start | bytes 4587520 | tf_op jit(solution)/shard_map/all_to_all | solution.py:30
  294.7 2.9 fusion.13
  297.6 1.3 collective-permute-start.10
  300.4 2.9 fusion.60
  303.5 18.6 %all-to-all-done.4 = bf16[16,40,1792]{2,1,0:T(8,128)(2,1)S(1)} async-done(((bf16[16,40,1792]{2,1,0:T(8,128)(2,1)}), bf16[16,40,1792]{2,1,0:T(8,128)(2,1)S(1)}, u32[]{:S(2)}, u32[]{:S(2)}) %all-to-all-start.4) | async-done | bytes 2293792 | tf_op jit(solution)/shard_map/all_to_all | solution.py:30
  324.8 3.3 fusion.12
  329.3 10.0 %all-to-all-start.5 = ((f32[128,1,476]{2,1,0:T(1,128)}), f32[128,1,476]{2,1,0:T(1,128)S(1)}, u32[]{:S(2)}, u32[]{:S(2)}) async-start(f32[128,1,476]{2,1,0:T(1,128)} %all_to_all.64), calls=%async_computation.5 | async-start | bytes 524288 | tf_op jit(solution)/shard_map/all_to_all | solution.py:30
  339.3 10.8 %all-to-all-done.5 = f32[128,1,476]{2,1,0:T(1,128)S(1)} async-done(((f32[128,1,476]{2,1,0:T(1,128)}), f32[128,1,476]{2,1,0:T(1,128)S(1)}, u32[]{:S(2)}, u32[]{:S(2)}) %all-to-all-start.5) | async-done | bytes 243744 | tf_op jit(solution)/shard_map/all_to_all | solution.py:30
  351.2 4.8 %all-to-all-start.6 = ((f32[128,1,476]{2,1,0:T(1,128)}), f32[128,1,476]{2,1,0:T(1,128)S(1)}, u32[]{:S(2)}, u32[]{:S(2)}) async-start(f32[128,1,476]{2,1,0:T(1,128)} %broadcast_in_dim.119), calls=%async_computation.6 | async-start | bytes 524288 | tf_op jit(solution)/shard_map/all_to_all | solution.py:30
  355.9 2.7 fusion.8
  358.7 8.0 %all-to-all-done.6 = f32[128,1,476]{2,1,0:T(1,128)S(1)} async-done(((f32[128,1,476]{2,1,0:T(1,128)}), f32[128,1,476]{2,1,0:T(1,128)S(1)}, u32[]{:S(2)}, u32[]{:S(2)}) %all-to-all-start.6) | async-done | bytes 243744 | tf_op jit(solution)/shard_map/all_to_all | solution.py:30
  (147 shorter events, 26.1 us)
Async XLA Ops:
  7.2 28.7 %copy-start = (f32[3584,16]{0,1:T(8,128)S(1)}, f32[3584,16]{0,1:T(8,128)}, u32[]{:S(2)}) copy-start(f32[3584,16]{0,1:T(8,128)} %param.14) | copy-start | bytes 688132
  7.2 98.5 %all-gather.10.cloned.1.call-start = ((), (), s32[]{:S(2)}) async-start(), calls=%async_computation.8 | async-start | bytes 6537216 | tf_op jit(solution)/shard_map/all_gather | solution.py:38
  7.9 97.8 %all-gather.8.cloned.1.call-start = ((), (), s32[]{:S(2)}) async-start(), calls=%async_computation.7 | async-start | bytes 6537216 | tf_op jit(solution)/shard_map/all_gather | solution.py:38
  8.7 97.1 %all-gather.18.cloned.1.call-start = ((), (), s32[]{:S(2)}) async-start(), calls=%async_computation.12 | async-start | bytes 6537216 | tf_op jit(solution)/shard_map/all_gather | solution.py:38
  9.4 115.8 %all-gather.12.cloned.1.call-start = ((), (), s32[]{:S(2)}) async-start(), calls=%async_computation.9 | async-start | bytes 6537216 | tf_op jit(solution)/shard_map/all_gather | solution.py:38
  9.4 1.2 copy-start.5
  10.0 0.9 copy-start.10
  10.0 115.3 %all-gather.14.cloned.1.call-start = ((), (), s32[]{:S(2)}) async-start(), calls=%async_computation.10 | async-start | bytes 6537216 | tf_op jit(solution)/shard_map/all_gather | solution.py:38
  10.6 1.2 copy-start.8
  10.9 1.0 copy-start.17
  11.8 24.1 %copy-start.3 = (bf16[128,3584]{1,0:T(8,128)(2,1)}, bf16[128,3584]{1,0:T(8,128)(2,1)S(1)}, u32[]{:S(2)}) copy-start(bf16[128,3584]{1,0:T(8,128)(2,1)S(1)} %fusion.3) | copy-start | bytes 2752516
  12.5 4.7 %collective-permute-start = (s32[128,2]{0,1:T(2,128)S(1)}, s32[128,2]{0,1:T(2,128)S(1)}, u32[]{:S(2)}, u32[]{:S(2)}) collective-permute-start(s32[128,2]{0,1:T(2,128)S(1)} %copy-done.11), channel_id=1, source_target_pairs={{0,4},{2,6},{4,0},{6,2},{1,5},{3,7},{5,1},{7,3},{8,12},{10,14},{12... | collective-permute-start | bytes 3080 | tf_op jit(solution)/shard_map/ppermute | solution.py:18
  18.5 5.2 %copy-start.12 = (s32[128,2]{0,1:T(2,128)}, s32[128,2]{0,1:T(2,128)S(1)}, u32[]{:S(2)}) copy-start(s32[128,2]{0,1:T(2,128)S(1)} %get-tuple-element.57) | copy-start | bytes 3076
  18.5 5.1 %copy-start.15 = (s32[128,2]{0,1:T(2,128)}, s32[128,2]{0,1:T(2,128)S(1)}, u32[]{:S(2)}) copy-start(s32[128,2]{0,1:T(2,128)S(1)} %broadcast_add_fusion.2) | copy-start | bytes 3076
  23.6 63.8 %all-to-all-start = ((bf16[16,40,3584]{2,1,0:T(8,128)(2,1)}), bf16[16,40,3584]{2,1,0:T(8,128)(2,1)}, u32[]{:S(2)}, u32[]{:S(2)}) async-start(bf16[16,40,3584]{2,1,0:T(8,128)(2,1)} %bitcast.43), calls=%async_computation | async-start | bytes 9175040 | tf_op jit(solution)/shard_map/all_to_all | solution.py:30
  31.3 96.4 %all-gather.16.cloned.1.call-start = ((), (), s32[]{:S(2)}) async-start(), calls=%async_computation.11 | async-start | bytes 6537216 | tf_op jit(solution)/shard_map/all_gather | solution.py:38
  31.4 41.1 %collective-permute-start.2 = (bf16[256,3584]{1,0:T(8,128)(2,1)S(1)}, bf16[256,3584]{1,0:T(8,128)(2,1)}, u32[]{:S(2)}, u32[]{:S(2)}) collective-permute-start(bf16[256,3584]{1,0:T(8,128)(2,1)S(1)} %pad_maximum_fusion.rows.refs_0_), channel_id=1, source_target_pairs={{0,4},{2,6},{4,0},{6,2},{1,5},{3,7},{5,1},{7,3},{8,12},{10,14},{12... | collective-permute-start | bytes 5505032 | tf_op jit(solution)/shard_map/ppermute | solution.py:18
  34.4 90.4 %collective-permute-start.1 = (bf16[256,3584]{1,0:T(8,128)(2,1)S(1)}, bf16[256,3584]{1,0:T(8,128)(2,1)}, u32[]{:S(2)}, u32[]{:S(2)}) collective-permute-start(bf16[256,3584]{1,0:T(8,128)(2,1)S(1)} %pad_maximum_fusion.rows.refs_0_), channel_id=1, source_target_pairs={{0,6},{2,0},{4,2},{6,4},{1,7},{3,1},{5,3},{7,5},{8,14},{10,8},{12,... | collective-permute-start | bytes 5505032 | tf_op jit(solution)/shard_map/ppermute | solution.py:18
  35.2 90.0 %collective-permute-start.3 = (bf16[256,3584]{1,0:T(8,128)(2,1)S(1)}, bf16[256,3584]{1,0:T(8,128)(2,1)}, u32[]{:S(2)}, u32[]{:S(2)}) collective-permute-start(bf16[256,3584]{1,0:T(8,128)(2,1)S(1)} %pad_maximum_fusion.rows.refs_0_), channel_id=1, source_target_pairs={{0,2},{2,4},{4,6},{6,0},{1,3},{3,5},{5,7},{7,1},{8,10},{10,12},{12... | collective-permute-start | bytes 5505032 | tf_op jit(solution)/shard_map/ppermute | solution.py:18
  87.4 65.3 %all-to-all-start.1 = ((bf16[16,40,3584]{2,1,0:T(8,128)(2,1)}), bf16[16,40,3584]{2,1,0:T(8,128)(2,1)}, u32[]{:S(2)}, u32[]{:S(2)}) async-start(bf16[16,40,3584]{2,1,0:T(8,128)(2,1)} %bitcast.44), calls=%async_computation.1 | async-start | bytes 9175040 | tf_op jit(solution)/shard_map/all_to_all | solution.py:30
  100.2 78.8 %collective-permute-start.4 = (bf16[320,3584]{1,0:T(8,128)(2,1)}, bf16[320,3584]{1,0:T(8,128)(2,1)}, u32[]{:S(2)}, u32[]{:S(2)}) collective-permute-start(bf16[320,3584]{1,0:T(8,128)(2,1)} %bitcast.12), channel_id=1, source_target_pairs={{0,6},{2,0},{4,2},{6,4},{1,7},{3,1},{5,3},{7,5},{8,14},{10,8},{12,... | collective-permute-start | bytes 6881288 | tf_op jit(solution)/shard_map/ppermute | solution.py:18
  102.8 76.1 %collective-permute-start.5 = (bf16[320,3584]{1,0:T(8,128)(2,1)}, bf16[320,3584]{1,0:T(8,128)(2,1)}, u32[]{:S(2)}, u32[]{:S(2)}) collective-permute-start(bf16[320,3584]{1,0:T(8,128)(2,1)} %bitcast.12), channel_id=1, source_target_pairs={{0,2},{2,4},{4,6},{6,0},{1,3},{3,5},{5,7},{7,1},{8,10},{10,12},{12... | collective-permute-start | bytes 6881288 | tf_op jit(solution)/shard_map/ppermute | solution.py:18
  102.9 109.1 %collective-permute-start.6 = (bf16[320,3584]{1,0:T(8,128)(2,1)}, bf16[320,3584]{1,0:T(8,128)(2,1)}, u32[]{:S(2)}, u32[]{:S(2)}) collective-permute-start(bf16[320,3584]{1,0:T(8,128)(2,1)} %bitcast.17), channel_id=1, source_target_pairs={{0,6},{2,0},{4,2},{6,4},{1,7},{3,1},{5,3},{7,5},{8,14},{10,8},{12,... | collective-permute-start | bytes 6881288 | tf_op jit(solution)/shard_map/ppermute | solution.py:18
  123.3 1.4 copy-start.1
  124.7 87.9 %collective-permute-start.7 = (bf16[320,3584]{1,0:T(8,128)(2,1)}, bf16[320,3584]{1,0:T(8,128)(2,1)}, u32[]{:S(2)}, u32[]{:S(2)}) collective-permute-start(bf16[320,3584]{1,0:T(8,128)(2,1)} %bitcast.17), channel_id=1, source_target_pairs={{0,2},{2,4},{4,6},{6,0},{1,3},{3,5},{5,7},{7,1},{8,10},{10,12},{12... | collective-permute-start | bytes 6881288 | tf_op jit(solution)/shard_map/ppermute | solution.py:18
  171.7 64.4 %all-to-all-start.2 = ((bf16[16,40,1792]{2,1,0:T(8,128)(2,1)}), bf16[16,40,1792]{2,1,0:T(8,128)(2,1)}, u32[]{:S(2)}, u32[]{:S(2)}) async-start(bf16[16,40,1792]{2,1,0:T(8,128)(2,1)} %bitcast.19), calls=%async_computation.2 | async-start | bytes 4587520 | tf_op jit(solution)/shard_map/all_to_all | solution.py:30
  214.2 27.6 %collective-permute-start.11 = (bf16[320,1792]{1,0:T(8,128)(2,1)}, bf16[320,1792]{1,0:T(8,128)(2,1)}, u32[]{:S(2)}, u32[]{:S(2)}) collective-permute-start(bf16[320,1792]{1,0:T(8,128)(2,1)} %get-tuple-element.66), channel_id=1, source_target_pairs={{0,2},{2,4},{4,6},{6,0},{1,3},{3,5},{5,7},{7,1},{8,10},{10,12},{12... | collective-permute-start | bytes 3440648 | tf_op jit(solution)/shard_map/ppermute | solution.py:22
  215.5 26.4 %collective-permute-start.12 = (bf16[320,1792]{1,0:T(8,128)(2,1)}, bf16[320,1792]{1,0:T(8,128)(2,1)}, u32[]{:S(2)}, u32[]{:S(2)}) collective-permute-start(bf16[320,1792]{1,0:T(8,128)(2,1)} %get-tuple-element.67), channel_id=1, source_target_pairs={{0,6},{2,0},{4,2},{6,4},{1,7},{3,1},{5,3},{7,5},{8,14},{10,8},{12,... | collective-permute-start | bytes 3440648 | tf_op jit(solution)/shard_map/ppermute | solution.py:22
  237.7 29.1 %collective-permute-start.13 = (bf16[320,1792]{1,0:T(8,128)(2,1)}, bf16[320,1792]{1,0:T(8,128)(2,1)}, u32[]{:S(2)}, u32[]{:S(2)}) collective-permute-start(bf16[320,1792]{1,0:T(8,128)(2,1)} %get-tuple-element.68), channel_id=1, source_target_pairs={{0,2},{2,4},{4,6},{6,0},{1,3},{3,5},{5,7},{7,1},{8,10},{10,12},{12... | collective-permute-start | bytes 3440648 | tf_op jit(solution)/shard_map/ppermute | solution.py:22
  237.7 29.1 %collective-permute-start.14 = (bf16[320,1792]{1,0:T(8,128)(2,1)}, bf16[320,1792]{1,0:T(8,128)(2,1)}, u32[]{:S(2)}, u32[]{:S(2)}) collective-permute-start(bf16[320,1792]{1,0:T(8,128)(2,1)} %get-tuple-element.69), channel_id=1, source_target_pairs={{0,6},{2,0},{4,2},{6,4},{1,7},{3,1},{5,3},{7,5},{8,14},{10,8},{12,... | collective-permute-start | bytes 3440648 | tf_op jit(solution)/shard_map/ppermute | solution.py:22
  243.7 79.5 %collective-permute-start.8 = (bf16[128,3584]{1,0:T(8,128)(2,1)}, bf16[128,3584]{1,0:T(8,128)(2,1)}, u32[]{:S(2)}, u32[]{:S(2)}) collective-permute-start(bf16[128,3584]{1,0:T(8,128)(2,1)} %get-tuple-element.40), channel_id=1, source_target_pairs={{0,2},{2,4},{4,6},{6,0},{1,3},{3,5},{5,7},{7,1},{8,10},{10,12},{12... | collective-permute-start | bytes 2752520 | tf_op jit(solution)/shard_map/ppermute | solution.py:22
  245.2 78.0 %collective-permute-start.9 = (bf16[128,3584]{1,0:T(8,128)(2,1)}, bf16[128,3584]{1,0:T(8,128)(2,1)}, u32[]{:S(2)}, u32[]{:S(2)}) collective-permute-start(bf16[128,3584]{1,0:T(8,128)(2,1)} %get-tuple-element.41), channel_id=1, source_target_pairs={{0,6},{2,0},{4,2},{6,4},{1,7},{3,1},{5,3},{7,5},{8,14},{10,8},{12,... | collective-permute-start | bytes 2752520 | tf_op jit(solution)/shard_map/ppermute | solution.py:22
  246.4 43.5 %all-to-all-start.3 = ((f32[64,1,20]{2,1,0:T(1,128)}), f32[64,1,20]{2,1,0:T(1,128)S(1)}, u32[]{:S(2)}, u32[]{:S(2)}) async-start(f32[64,1,20]{2,1,0:T(1,128)} %bitcast.22), calls=%async_computation.3 | async-start | bytes 65536 | tf_op jit(solution)/shard_map/all_to_all | solution.py:30
  259.4 9.3 %copy-start.2 = (bf16[640,1792]{1,0:T(8,128)(2,1)S(1)}, bf16[640,1792]{1,0:T(8,128)(2,1)}, u32[]{:S(2)}) copy-start(bf16[640,1792]{1,0:T(8,128)(2,1)} %copy-done.1) | copy-start | bytes 6881284
  290.0 32.2 %all-to-all-start.4 = ((bf16[16,40,1792]{2,1,0:T(8,128)(2,1)}), bf16[16,40,1792]{2,1,0:T(8,128)(2,1)S(1)}, u32[]{:S(2)}, u32[]{:S(2)}) async-start(bf16[16,40,1792]{2,1,0:T(8,128)(2,1)} %bitcast.25), calls=%async_computation.4 | async-start | bytes 4587520 | tf_op jit(solution)/shard_map/all_to_all | solution.py:30
  294.7 4.4 %copy-start.20 = (s32[128,2]{0,1:T(2,128)S(1)}, s32[128,2]{0,1:T(2,128)}, u32[]{:S(2)}) copy-start(s32[128,2]{0,1:T(2,128)} %get-tuple-element.56) | copy-start | bytes 3076
  294.7 4.5 %copy-start.19 = (f32[128,2]{0,1:T(2,128)S(1)}, f32[128,2]{0,1:T(2,128)}, u32[]{:S(2)}) copy-start(f32[128,2]{0,1:T(2,128)} %select_reduce_fusion.7) | copy-start | bytes 3076
  294.7 4.5 %copy-start.4 = (bf16[128,3584]{1,0:T(8,128)(2,1)S(1)}, bf16[128,3584]{1,0:T(8,128)(2,1)}, u32[]{:S(2)}) copy-start(bf16[128,3584]{1,0:T(8,128)(2,1)} %copy-done.3) | copy-start | bytes 2752516
  294.7 4.5 %copy-start.14 = (pred[128,2,16]{0,2,1:T(8,128)(4,1)S(1)}, pred[128,2,16]{0,2,1:T(8,128)(4,1)}, u32[]{:S(2)}) copy-start(pred[128,2,16]{0,2,1:T(8,128)(4,1)} %iota_compare_fusion.15) | copy-start | bytes 12292
  297.6 5.6 %copy-start.13 = (s32[128,2]{0,1:T(2,128)S(1)}, s32[128,2]{0,1:T(2,128)}, u32[]{:S(2)}) copy-start(s32[128,2]{0,1:T(2,128)} %copy-done.12) | copy-start | bytes 3076
  297.6 5.6 %copy-start.16 = (s32[128,2]{0,1:T(2,128)S(1)}, s32[128,2]{0,1:T(2,128)}, u32[]{:S(2)}) copy-start(s32[128,2]{0,1:T(2,128)} %copy-done.15) | copy-start | bytes 3076
  297.6 25.6 %collective-permute-start.10 = (bf16[128,3584]{1,0:T(8,128)(2,1)}, bf16[128,3584]{1,0:T(8,128)(2,1)}, u32[]{:S(2)}, u32[]{:S(2)}) collective-permute-start(bf16[128,3584]{1,0:T(8,128)(2,1)} %fusion.13), channel_id=1, source_target_pairs={{0,4},{2,6},{4,0},{6,2},{1,5},{3,7},{5,1},{7,3},{8,12},{10,14},{12... | collective-permute-start | bytes 2752520 | tf_op jit(solution)/shard_map/ppermute | solution.py:22
  323.0 1.2 copy-start.6
  323.0 1.8 copy-start.7
  323.0 1.8 copy-start.18
  324.8 3.3 copy-start.9
  329.3 20.8 %all-to-all-start.5 = ((f32[128,1,476]{2,1,0:T(1,128)}), f32[128,1,476]{2,1,0:T(1,128)S(1)}, u32[]{:S(2)}, u32[]{:S(2)}) async-start(f32[128,1,476]{2,1,0:T(1,128)} %all_to_all.64), calls=%async_computation.5 | async-start | bytes 524288 | tf_op jit(solution)/shard_map/all_to_all | solution.py:30
  351.2 15.5 %all-to-all-start.6 = ((f32[128,1,476]{2,1,0:T(1,128)}), f32[128,1,476]{2,1,0:T(1,128)S(1)}, u32[]{:S(2)}, u32[]{:S(2)}) async-start(f32[128,1,476]{2,1,0:T(1,128)} %broadcast_in_dim.119), calls=%async_computation.6 | async-start | bytes 524288 | tf_op jit(solution)/shard_map/all_to_all | solution.py:30
  (1 other events, 0.7 us)
Sparse Core Ops, SparseCore 0:
  9.7 20.2 all-gather.9
  31.6 17.9 all-gather.7
  51.2 17.9 all-gather.17
  70.7 17.9 all-gather.11
  90.2 17.9 all-gather.13
  109.7 17.9 all-gather.15
